TPU v7x, 32 devices: a whole 2x2x4 slice. The times are simulated.
32 devices in a mesh: cuts: 2 (over y), row: 4 (over z), vec: 4 (over x, core).
Axes of the slice: x: 2, y: 2, z: 4, core: 2. Of those that a mesh axis runs over, the one named last changes fastest.
Arguments:
- vectors: float32 [16384, 512], P(('cuts', 'row'), 'vec'), parts along dimension 0, may hold values from -6 to 6
- intersection: float32 [8192, 1536], P('row'), may hold values from -0.15625 to 0.15625
- factor: float32 [16384, 2048], P(('cuts', 'row')), parts along dimension 0, may hold values from -0.1875 to 0.1875
- pivot_rows: int32 [16384], P(('cuts', 'row')), parts along dimension 0, may hold values from 0 to 2047, as said below
- pivot_sizes: int32 [2048], P('cuts'), parts along dimension 0, may hold values from 1 to 2
- pivot_diag: float32 [4096], P('cuts'), parts along dimension 0, may hold values from 0.5 to 2
- pivot_off: float32 [2048], P('cuts'), parts along dimension 0, may hold values from 2.5 to 4
Outputs:
- partial_solve: float32 [16384, 512], P(('cuts', 'row'), 'vec'), parts along dimension 0
There are 2 independent parts, one for each index of `cuts`. A program takes and returns all parts, laid end to end along the dimension named above; an argument that names none is the same for every part. Nothing has to cross between parts.
Inputs may be any that keep to these rules, and one draw needn't show every extreme that they name: `pivot_rows`: each aligned run of 2048 entries is a permutation of 0 to 2047. `pivot_sizes`: 2 marks a 2x2 pivot block on the pair of rows, 1 two 1x1 blocks.
All inputs are finite; a program needn't handle non-finite values.
Results may differ from a plain program's by a relative error of at most 0.00011.
Values sent between devices are 32-bit elements; how exact they have to be, the bound alone decides.
No kernel may reach another device: no remote copies, remote signals or barrier semaphores. Data moves between devices by JAX's collectives and lax.ppermute only.
A program may use at most 128 MiB of HBM per device.

v0:
```python
import functools

import jax
import jax.numpy as jnp
from jax import lax
from jax.experimental import pallas as pl
from jax.experimental.pallas import tpu as pltpu
from jax.sharding import PartitionSpec as P

BS = 512
PANEL = 1024
PANELS = 2
CYC = 16
DIAG = 256
HALF = 128
MIB = 1024 * 1024
HEAVY = 2**37
LIGHT = 2**30
F32 = jnp.float32
BF16 = jnp.bfloat16


def params(mib):
    return pltpu.CompilerParams(vmem_limit_bytes=mib * MIB)


IN_VMEM = pl.BlockSpec(memory_space=pltpu.VMEM)
IN_SMEM = pl.BlockSpec(memory_space=pltpu.SMEM)
IN_HBM = pl.BlockSpec(memory_space=pltpu.HBM)


def shaped(*shape, dtype=F32):
    return jax.ShapeDtypeStruct(shape, dtype)


def cost(flops, moved):
    return pl.CostEstimate(flops=int(flops), bytes_accessed=int(moved), transcendentals=0)


def split(value):
    high = value.astype(BF16)
    low = (value - high.astype(F32)).astype(BF16)
    return high, low


def side_by_side(value):
    return jnp.concatenate(split(value), axis=1)


def dot(left, right):
    return jnp.dot(left, right, preferred_element_type=F32)


def fold(wide):
    width = wide.shape[1] // 2
    return wide[:, :width] + wide[:, width:]


def times(left, right_wide):
    high, low = split(left)
    return parts_times(high, low, right_wide)


def parts_times(high, low, right_wide):
    return fold(dot(high, right_wide)) + dot(low, right_wide[:, : right_wide.shape[1] // 2])


def small_times(left_wide, right):
    wide = side_by_side(right)
    return fold(dot(left_wide, jnp.concatenate([wide, wide], axis=0)))


def start_kernel(slots, shares, place_ref, factor_ref, vec_ref, *refs):
    share_ref, first_ref, last_ref, sems = refs
    groups = PANEL // DIAG
    part = place_ref[1]
    rows = vec_ref.shape[0]
    copies = [(vec_ref.at[pl.ds(rows - BS, BS)], last_ref), (vec_ref.at[pl.ds(0, BS)], first_ref)]
    for panel in range(PANELS):
        at = 0
        for k in range(groups):
            row = pl.multiple_of((panel * slots + k * shares + part) * CYC, CYC)
            for j in range(k + 1):
                source = factor_ref.at[pl.ds(row, CYC), pl.ds(panel * PANEL + j * DIAG, DIAG)]
                copies.append((source, share_ref.at[panel, at]))
                at += 1
    started = [pltpu.make_async_copy(a, b, sems.at[i]) for i, (a, b) in enumerate(copies)]
    for copy in started:
        copy.start()
    for copy in started:
        copy.wait()


def first_sends(place, factor, vectors, slots, shares):
    groups = PANEL // DIAG
    blocks = groups * (groups + 1) // 2
    edge = shaped(BS, vectors.shape[1])
    return pl.pallas_call(
        functools.partial(start_kernel, slots, shares),
        out_shape=[shaped(PANELS, blocks, CYC, DIAG), edge, edge],
        in_specs=[IN_SMEM, IN_HBM, IN_HBM],
        out_specs=[IN_VMEM] * 3,
        scratch_shapes=[pltpu.SemaphoreType.DMA((PANELS * blocks + 2,))],
        compiler_params=params(4),
        cost_estimate=cost(0, 4 * MIB),
        name="first_sends",
    )(place, factor, vectors)


def band_kernel(inter_ref, vec_ref, before_ref, after_ref, out_ref, wide_ref):
    tile = pl.program_id(0)
    rows = vec_ref.shape[0]
    tile_rows = inter_ref.shape[0]
    owners = out_ref.shape[0]

    @pl.when(tile == 0)
    def _():
        wide_ref[:BS] = side_by_side(before_ref[...])
        wide_ref[BS : BS + rows] = side_by_side(vec_ref[...])
        wide_ref[BS + rows :] = side_by_side(after_ref[...])

    window = wide_ref[pl.ds(pl.multiple_of(tile * BS, BS), 3 * BS)]
    product = times(inter_ref[...], window)
    groups = tile_rows // (owners * CYC)
    for g in range(groups):
        for owner in range(owners):
            first = (g * owners + owner) * CYC
            out_ref[owner, g * CYC : (g + 1) * CYC] = product[first : first + CYC]


def band_product_split(intersection, vectors, halo, owners):
    rows, columns = vectors.shape
    width = intersection.shape[1]
    tile_rows = BS
    slot_rows = tile_rows // owners
    whole = lambda t: (0, 0)
    return pl.pallas_call(
        band_kernel,
        out_shape=shaped(owners, rows // owners, columns),
        grid=(rows // tile_rows,),
        in_specs=[
            pl.BlockSpec((tile_rows, width), lambda t: (t, 0)),
            pl.BlockSpec((rows, columns), whole),
            pl.BlockSpec((BS, columns), whole),
            pl.BlockSpec((BS, columns), whole),
        ],
        out_specs=pl.BlockSpec((owners, slot_rows, columns), lambda t: (0, t, 0)),
        scratch_shapes=[pltpu.VMEM((rows + 2 * BS, 2 * columns), BF16)],
        compiler_params=params(16),
        cost_estimate=cost(8 * rows * width * columns, 4 * rows * width),
        name="band_product_split",
    )(intersection, vectors, *halo)


def stack_kernel(panel, count, *refs):
    for k in range(count):
        refs[-1][k] = refs[k][panel]


def stack(panel, pieces, after):
    count = len(pieces)
    return pl.pallas_call(
        functools.partial(stack_kernel, panel, count),
        out_shape=shaped(count, *pieces[0].shape[1:]),
        in_specs=[IN_VMEM] * count + [pl.BlockSpec(memory_space=pl.ANY)],
        out_specs=IN_VMEM,
        compiler_params=params(4),
        name="stack",
    )(*pieces, after)


def pair_kernel(first_ref, second_ref, *refs):
    out_ref = refs[-1]
    out_ref[0] = first_ref[...]
    out_ref[1] = second_ref[...]


def pair(first, second, after):
    return pl.pallas_call(
        pair_kernel,
        out_shape=shaped(2, *first.shape),
        in_specs=[IN_VMEM] * 2 + [pl.BlockSpec(memory_space=pl.ANY)] * len(after),
        out_specs=IN_VMEM,
        compiler_params=params(4),
        name="pair",
    )(first, second, *after)


def invert_kernel(panel, owners, shares, place_ref, after_ref, factor_ref, *refs):
    mine_ref, theirs_ref, high_ref, low_ref, inv_high_ref, inv_low_ref, own_ref, tri_ref, sem = refs
    groups = PANEL // DIAG
    me, part = place_ref[0], place_ref[1]
    rows = own_ref.shape[0]
    copy = pltpu.make_async_copy(
        factor_ref.at[pl.ds(panel * rows, rows), pl.ds(panel * PANEL, PANEL)], own_ref, sem
    )
    copy.start()
    for other in range(1, owners):
        owner = me ^ other
        for turn in range(shares):
            at = 0
            for k in range(groups):
                for j in range(k + 1):
                    source = theirs_ref if turn % 2 else mine_ref
                    piece = source[turn // 2, other - 1, at]
                    to = (k * shares + (part ^ turn)) * owners + owner
                    tri_ref[to, :, j * DIAG : (j + 1) * DIAG] = piece
                    at += 1
    copy.wait()
    for k in range(groups):
        reach = (k + 1) * DIAG
        for s in range(shares):
            row = (k * shares + s) * CYC
            tri_ref[(k * shares + s) * owners + me, :, :reach] = own_ref[row : row + CYC, :reach]

    def block(row, column, size):
        part_rows = tri_ref[row // CYC : (row + size) // CYC, :, column : column + size]
        return part_rows.reshape(size, size)

    for k in range(1, groups):
        rows = slice(k * DIAG, (k + 1) * DIAG)
        left = tri_ref[rows.start // CYC : rows.stop // CYC, :, : k * DIAG].reshape(DIAG, k * DIAG)
        high_ref[rows, : k * DIAG], low_ref[rows, : k * DIAG] = split(left)

    down = lax.broadcasted_iota(jnp.int32, (HALF, HALF), 0)
    along = lax.broadcasted_iota(jnp.int32, (HALF, HALF), 1)
    eye = jnp.where(down == along, 1.0, 0.0).astype(F32)

    def below(size):
        return (down // size == along // size + 1) & ((down // size) % 2 == 1)

    count = PANEL // HALF
    diagonal = [block(i * HALF, i * HALF, HALF) for i in range(count)]
    wides = [side_by_side(d) for d in diagonal]
    inverse = [eye - jnp.where(below(1), d, 0.0) for d in diagonal]
    size = 2
    while size < HALF:
        keep = jnp.where(below(size), 1.0, 0.0).astype(BF16)
        keep = jnp.concatenate([keep, keep], axis=1)
        right = [small_times(wides[i] * keep, inverse[i]) for i in range(count)]
        inverse = [inverse[i] - small_times(side_by_side(inverse[i]), right[i]) for i in range(count)]
        size *= 2
    for k in range(groups):
        first, second = inverse[2 * k], inverse[2 * k + 1]
        corner = block(k * DIAG + HALF, k * DIAG, HALF)
        right = small_times(side_by_side(corner), first)
        corner = -small_times(side_by_side(second), right)
        empty = jnp.zeros((HALF, HALF), F32)
        whole = jnp.concatenate(
            [jnp.concatenate([first, empty], axis=1), jnp.concatenate([corner, second], axis=1)], axis=0
        )
        inv_high_ref[k], inv_low_ref[k] = split(whole)


def invert_panel(panel, place, factor, pieces, owners, shares, panel_rows, after, flops):
    groups = PANEL // DIAG
    return pl.pallas_call(
        functools.partial(invert_kernel, panel, owners, shares),
        out_shape=[shaped(PANEL, PANEL, dtype=BF16)] * 2 + [shaped(groups, DIAG, DIAG, dtype=BF16)] * 2,
        in_specs=[IN_SMEM, pl.BlockSpec(memory_space=pl.ANY), IN_HBM] + [IN_VMEM] * len(pieces),
        out_specs=[IN_VMEM] * 4,
        scratch_shapes=[
            pltpu.VMEM((panel_rows, PANEL), F32),
            pltpu.VMEM((PANEL // CYC, CYC, PANEL), F32),
            pltpu.SemaphoreType.DMA,
        ],
        compiler_params=params(16),
        cost_estimate=cost(flops, 12 * MIB),
        name="invert_panel",
    )(place, after, factor, *pieces)


def order_kernel(first, pivot_ref, grouped_ref, after_ref, *out_refs):
    for out_ref in out_refs:
        pick_rows(pivot_ref, first, grouped_ref, out_ref)
        first += out_ref.shape[0]


def pick_rows(pivot_ref, first, source_ref, target_ref):
    step = 8

    def body(i, _):
        base = i * step
        rows = [source_ref[pl.ds(pivot_ref[first + base + j], 1)] for j in range(step)]
        target_ref[pl.ds(pl.multiple_of(base, step), step)] = jnp.concatenate(rows, axis=0)
        return 0

    lax.fori_loop(0, target_ref.shape[0] // step, body, 0, unroll=4)


def order_rows(first, counts, pivot_rows, grouped, after):
    return pl.pallas_call(
        functools.partial(order_kernel, first),
        out_shape=[shaped(count, grouped.shape[1]) for count in counts],
        in_specs=[IN_SMEM, IN_VMEM, pl.BlockSpec(memory_space=pl.ANY)],
        out_specs=[IN_VMEM] * len(counts),
        compiler_params=params(4),
        cost_estimate=cost(0, 2 * MIB),
        name="order_rows",
    )(pivot_rows, grouped, after)


def solve_into(me, owners, pieces, high_ref, low_ref, inv_high_ref, inv_low_ref, rhs_ref, wide_ref, y_ref):
    slots = pieces[0].shape[0] // CYC
    columns = pieces[0].shape[1]
    for k in range(owners):
        for s in range(slots):
            rhs_ref[s * owners + (me ^ k)] = pieces[k][s * CYC : (s + 1) * CYC]
    for k in range(PANEL // DIAG):
        rows = slice(k * DIAG, (k + 1) * DIAG)
        rhs = rhs_ref[rows.start // CYC : rows.stop // CYC].reshape(DIAG, columns)
        if k:
            done = wide_ref[: k * DIAG]
            rhs = rhs - parts_times(high_ref[rows, : k * DIAG], low_ref[rows, : k * DIAG], done)
        wide = side_by_side(rhs)
        block = parts_times(inv_high_ref[k], inv_low_ref[k], wide)
        wide_ref[rows] = side_by_side(block)
        y_ref[rows.start // CYC : rows.stop // CYC] = block.reshape(DIAG // CYC, CYC, columns)


def first_kernel(owners, place_ref, factor_ref, *refs):
    pieces = refs[:owners]
    high, low, inv_high, inv_low, current_ref = refs[owners : owners + 5]
    y_ref, next_ref, rhs_ref, wide_ref, left_ref, sem = refs[owners + 5 :]
    rows = left_ref.shape[0]
    copy = pltpu.make_async_copy(factor_ref.at[pl.ds(rows, rows), pl.ds(0, PANEL)], left_ref, sem)
    copy.start()
    solve_into(place_ref[0], owners, pieces, high, low, inv_high, inv_low, rhs_ref, wide_ref, y_ref)
    copy.wait()
    next_ref[...] = current_ref[...] - times(left_ref[...], wide_ref[...])


def first_solve(place, pieces, prepared, factor, current, panel_rows):
    owners = len(pieces)
    columns = current.shape[1]
    return pl.pallas_call(
        functools.partial(first_kernel, owners),
        out_shape=[shaped(PANEL // CYC, CYC, columns), shaped(panel_rows, columns)],
        in_specs=[IN_SMEM, IN_HBM] + [IN_VMEM] * (owners + 5),
        out_specs=[IN_VMEM] * 2,
        scratch_shapes=[
            pltpu.VMEM((PANEL // CYC, CYC, columns), F32),
            pltpu.VMEM((PANEL, 2 * columns), BF16),
            pltpu.VMEM((panel_rows, PANEL), F32),
            pltpu.SemaphoreType.DMA,
        ],
        compiler_params=params(8),
        cost_estimate=cost(HEAVY, 6 * MIB),
        name="first_solve",
    )(place, factor, *pieces, *prepared, current)


def pivot_weights(me, sizes, diag, off):
    pairs, lanes = off.shape[1], diag.shape[1]
    spread = lax.broadcasted_iota(jnp.int32, (pairs, lanes), 1) // 2 == lax.broadcasted_iota(
        jnp.int32, (pairs, lanes), 0
    )
    spread = jnp.where(spread, 1.0, 0.0).astype(F32)
    off = jnp.dot(off, spread, precision=lax.Precision.HIGHEST, preferred_element_type=F32)
    sizes = jnp.dot(sizes.astype(F32), spread, precision=lax.Precision.HIGHEST, preferred_element_type=F32)
    odd = lax.broadcasted_iota(jnp.int32, diag.shape, 1) % 2 == 1
    other = jnp.where(odd, pltpu.roll(diag, 1, 1), pltpu.roll(diag, lanes - 1, 1))
    determ = diag * other - off * off
    is_pair = sizes > 1.5
    keep = jnp.where(is_pair, other / determ, 1.0 / diag)
    swap = jnp.where(is_pair, -off / determ, 0.0)
    turned = []
    for weight in (keep, swap):
        weight = pltpu.roll(weight, lax.rem(lanes - CYC * me, lanes), 1)
        tall = jnp.concatenate([weight] * (HALF // weight.shape[0]), axis=0)
        turned.append(tall.T)
    return turned


def ready_kernel(
    tile_rows, place_ref, after_ref, factor_ref, sizes_ref, diag_ref, off_ref, keep_ref, swap_ref, high_ref, low_ref,
    left_ref, sems,
):
    tiles = left_ref.shape[0]
    loads = []
    for t in range(tiles):
        source = factor_ref.at[pl.ds((t + 1) * tile_rows, tile_rows), pl.ds((PANELS - 1) * PANEL, PANEL)]
        loads.append(pltpu.make_async_copy(source, left_ref.at[t], sems.at[t]))
        loads[t].start()
    keep_ref[...], swap_ref[...] = pivot_weights(place_ref[0], sizes_ref[...], diag_ref[...], off_ref[...])
    for t in range(tiles):
        loads[t].wait()
        rows = slice(t * tile_rows, (t + 1) * tile_rows)
        high_ref[rows], low_ref[rows] = split(left_ref[t])


def make_ready(place, factor, pivots, tile_rows, after):
    weight = shaped(pivots[1].shape[1], HALF)
    tiles = factor.shape[0] // tile_rows - 1
    return pl.pallas_call(
        functools.partial(ready_kernel, tile_rows),
        out_shape=[weight, weight] + [shaped(tiles * tile_rows, PANEL, dtype=BF16)] * 2,
        in_specs=[IN_SMEM, pl.BlockSpec(memory_space=pl.ANY), IN_HBM] + [IN_VMEM] * len(pivots),
        out_specs=[IN_VMEM] * 4,
        scratch_shapes=[pltpu.VMEM((tiles, tile_rows, PANEL), F32), pltpu.SemaphoreType.DMA((tiles,))],
        compiler_params=params(12),
        cost_estimate=cost(HEAVY, 0),
        name="make_ready",
    )(place, after, factor, *pivots)


def middle_kernel(tile_rows, factor_ref, rest_ref, y_ref, out_ref, wide_ref, left_ref, sems):
    tiles = left_ref.shape[0]
    loads = []
    for t in range(tiles):
        source = factor_ref.at[pl.ds((t + 1) * tile_rows, tile_rows), pl.ds(0, PANEL)]
        loads.append(pltpu.make_async_copy(source, left_ref.at[t], sems.at[t]))
        loads[t].start()
    wide_ref[...] = side_by_side(y_ref[...].reshape(PANEL, y_ref.shape[2]))
    for t in range(tiles):
        loads[t].wait()
        rows = slice(t * tile_rows, (t + 1) * tile_rows)
        out_ref[rows] = rest_ref[rows] - times(left_ref[t], wide_ref[...])


def middle_update(rest, y, factor, tile_rows):
    rows, columns = rest.shape
    tiles = rows // tile_rows
    return pl.pallas_call(
        functools.partial(middle_kernel, tile_rows),
        out_shape=shaped(rows, columns),
        in_specs=[IN_HBM] + [IN_VMEM] * 2,
        out_specs=IN_VMEM,
        scratch_shapes=[
            pltpu.VMEM((PANEL, 2 * columns), BF16),
            pltpu.VMEM((tiles, tile_rows, PANEL), F32),
            pltpu.SemaphoreType.DMA((tiles,)),
        ],
        compiler_params=params(12),
        cost_estimate=cost(8 * rows * PANEL * columns, 8 * MIB),
        name="middle_update",
    )(factor, rest, y)


def last_kernel(owners, tile_rows, place_ref, *refs):
    pieces = refs[:owners]
    high, low, inv_high, inv_low, y_ref, keep_ref, swap_ref = refs[owners : owners + 7]
    left_high, left_low, rest_ref, out_ref, rhs_ref, wide_ref, second_ref, stage_ref, sems = refs[owners + 7 :]
    me = place_ref[0]
    solve_into(me, owners, pieces, high, low, inv_high, inv_low, rhs_ref, wide_ref, second_ref)
    stores = []
    for t in range(stage_ref.shape[0]):
        if t:
            rows = slice((t - 1) * tile_rows, t * tile_rows)
            stage_ref[t] = rest_ref[rows] - parts_times(left_high[rows], left_low[rows], wide_ref[...])
        else:
            scale_own_rows(me, owners, y_ref, second_ref, keep_ref, swap_ref, stage_ref)
        target = out_ref.at[pl.ds(t * tile_rows, tile_rows)]
        stores.append(pltpu.make_async_copy(stage_ref.at[t], target, sems.at[t]))
        stores[t].start()
    for store in stores:
        store.wait()


def scale_own_rows(me, owners, first_ref, second_ref, keep_ref, swap_ref, stage_ref):
    slots = first_ref.shape[0] // owners
    runs = keep_ref.shape[0] // (owners * CYC)
    for panel, source in enumerate((first_ref, second_ref)):
        for s in range(slots):
            at = panel * slots + s
            rows = source[s * owners + me]
            odd = lax.broadcasted_iota(jnp.int32, rows.shape, 0) % 2 == 1
            other = jnp.where(odd, pltpu.roll(rows, 1, 0), pltpu.roll(rows, CYC - 1, 0))
            first = (at % runs) * owners * CYC
            keep = keep_ref[first : first + CYC, at // runs : at // runs + 1]
            swap = swap_ref[first : first + CYC, at // runs : at // runs + 1]
            mixed = keep * rows + jnp.where(swap != 0, swap * other, 0.0)
            stage_ref[0, at * CYC : (at + 1) * CYC] = mixed


def last_solve(place, pieces, prepared, y, weights, left, rest, tile_rows):
    owners = len(pieces)
    columns = rest.shape[1]
    rows = rest.shape[0] + tile_rows
    return pl.pallas_call(
        functools.partial(last_kernel, owners, tile_rows),
        out_shape=shaped(rows, columns),
        in_specs=[IN_SMEM] + [IN_VMEM] * (owners + 10),
        out_specs=IN_HBM,
        scratch_shapes=[
            pltpu.VMEM((PANEL // CYC, CYC, columns), F32),
            pltpu.VMEM((PANEL, 2 * columns), BF16),
            pltpu.VMEM((PANEL // CYC, CYC, columns), F32),
            pltpu.VMEM((rows // tile_rows, tile_rows, columns), F32),
            pltpu.SemaphoreType.DMA((rows // tile_rows,)),
        ],
        compiler_params=params(12),
        cost_estimate=cost(8 * rows * PANEL * columns, 12 * MIB),
        name="last_solve",
    )(place, *pieces, *prepared, y, *weights, *left, rest)


def swap_with(value, axis, distance):
    size = lax.axis_size(axis)
    return lax.ppermute(value, axis, [(i, i ^ distance) for i in range(size)])


def from_all(value, axis):
    return [value] + [swap_with(value, axis, k) for k in range(1, lax.axis_size(axis))]


def local(vectors, intersection, factor, pivot_rows, pivot_sizes, pivot_diag, pivot_off):
    owners, shares = lax.axis_size("row"), lax.axis_size("vec")
    slots = PANEL // owners // CYC
    panel_rows = slots * CYC
    place = jnp.stack([lax.axis_index("row"), lax.axis_index("vec")]).astype(jnp.int32)
    intersection, factor = (pltpu.with_memory_space_constraint(a, pltpu.HBM) for a in (intersection, factor))

    share, first, last = first_sends(
        place, factor, pltpu.with_memory_space_constraint(vectors, pltpu.HBM), slots, shares
    )
    up = [(i, i + 1) for i in range(owners - 1)]
    down = [(j, i) for i, j in up]
    halo = lax.ppermute(last, "row", up), lax.ppermute(first, "row", down)
    direct = from_all(share, "row")[1:]
    product = band_product_split(intersection, vectors, halo, owners)
    grouped = lax.all_to_all(product, "row", 0, 0, tiled=True).reshape(vectors.shape)

    def share_out(panel, after, after_crossing):
        stacked = stack(panel, direct, after)
        mine = pair(stacked, swap_with(stacked, "vec", 2), after_crossing)
        return mine, swap_with(mine, "vec", 1)

    tile_rows = PANELS * panel_rows
    pivots = [a.reshape(pivot_diag.shape[0] // DIAG, -1) for a in (pivot_sizes, pivot_diag, pivot_off)]
    keep, swap, *left = make_ready(place, factor, pivots, tile_rows, product)
    shared = share_out(0, keep, ())
    (first,) = order_rows(0, [panel_rows], pivot_rows, grouped, place)
    prepared = invert_panel(0, place, factor, shared, owners, shares, panel_rows, first, HEAVY)
    rest_rows = factor.shape[0] - tile_rows
    second, rest = order_rows(panel_rows, [tile_rows - panel_rows, rest_rows], pivot_rows, grouped, first)
    later = share_out(1, first, (prepared[2], second))
    pieces = from_all(first, "row")
    y, second = first_solve(place, pieces, prepared, factor, second, panel_rows)
    pieces = from_all(second, "row")
    rest = middle_update(rest, y, factor, tile_rows)
    prepared = invert_panel(1, place, factor, later, owners, shares, panel_rows, y, LIGHT)
    return last_solve(place, pieces, prepared, y, (keep, swap), left, rest, tile_rows)


def padded_2(shard, sides, width):
    for axis, dim in sides:
        devices, length = (lax.axis_size(axis), shard.shape[dim])
        up = [(i, (i + 1) % devices) for i in range(devices - 1)]
        down = [(j, i) for i, j in up]
        last = lax.slice_in_dim(shard, length - width, length, axis=dim)
        leading = lax.slice_in_dim(shard, 0, width, axis=dim)
        before = lax.ppermute(last, axis, up)
        after = lax.ppermute(leading, axis, down)
        shard = jnp.concatenate([before, shard, after], axis=dim)
    return shard


def band_product(intersection, padded, blocks_here):
    band_width = intersection.shape[1] // 3
    band_rows = intersection.reshape(blocks_here, band_width, 3 * band_width)
    result = jnp.zeros((blocks_here, band_width, padded.shape[1]), jnp.float32)
    for offset in range(3):
        window = padded[offset * band_width : offset * band_width + blocks_here * band_width]
        window = window.reshape(blocks_here, band_width, padded.shape[1])
        result = result + jnp.einsum(
            "kij,kjv->kiv",
            band_rows[:, :, offset * band_width : (offset + 1) * band_width],
            window,
            precision=lax.Precision.HIGHEST,
        )
    return result.reshape(blocks_here * band_width, padded.shape[1])


def scale_pivots(values, sizes_here, diag_here, off_here):
    paired = values.reshape(-1, 2, values.shape[1])
    leading = paired[:, 0]
    trailing = paired[:, 1]
    diag_lead = diag_here[0::2][:, None]
    diag_next = diag_here[1::2][:, None]
    coupling = off_here[:, None]
    determ = diag_lead * diag_next - coupling * coupling
    is_pair = (sizes_here == 2)[:, None]
    new_lead = jnp.where(
        is_pair, (diag_next * leading - coupling * trailing) / determ, leading / diag_lead
    )
    new_next = jnp.where(
        is_pair, (diag_lead * trailing - coupling * leading) / determ, trailing / diag_next
    )
    return jnp.stack([new_lead, new_next], axis=1).reshape(values.shape)


def local_many(vectors, intersection, factor, pivot_rows, pivot_sizes, pivot_diag, pivot_off):
    owners = lax.axis_size("row")
    device = lax.axis_index("row")
    rows_here = vectors.shape[0]
    columns = vectors.shape[1]
    slot_count = PANEL // owners // CYC
    panel_rows = slot_count * CYC
    triangles = []
    quarter = PANEL // lax.axis_size("vec")
    column_idx = lax.axis_index("vec")
    for panel_num in range(PANELS):
        local_rows = factor[panel_num * panel_rows : (panel_num + 1) * panel_rows]
        column_part = lax.dynamic_slice_in_dim(
            local_rows, panel_num * PANEL + column_idx * quarter, quarter, 1
        )
        column_part = column_part.reshape(slot_count, 1, CYC, quarter)
        gathered = lax.all_gather(column_part, "row", axis=1, tiled=True)
        triangles.append(lax.all_gather(gathered, "vec", axis=3, tiled=True).reshape(PANEL, PANEL))
    padded = padded_2(vectors, (("row", 0),), BS)
    product = band_product(intersection, padded, rows_here // BS)
    grouped = product.reshape(rows_here // (CYC * owners), owners, CYC, columns)
    regrouped = lax.all_to_all(grouped, "row", split_axis=1, concat_axis=0, tiled=True).reshape(
        rows_here, columns
    )
    current = jnp.take(regrouped, pivot_rows, axis=0)
    outputs = []
    for panel_num in range(PANELS):
        row_first = panel_num * panel_rows
        row_end = row_first + panel_rows
        col_first = panel_num * PANEL
        col_end = col_first + PANEL
        rhs_local = current[row_first:row_end].reshape(slot_count, 1, CYC, columns)
        rhs_all = lax.all_gather(rhs_local, "row", axis=1, tiled=True)
        triangle = triangles[panel_num]
        block_sol = jax.scipy.linalg.solve_triangular(
            triangle, rhs_all.reshape(PANEL, columns), lower=True, unit_diagonal=True
        )
        update = jnp.dot(
            factor[row_end:, col_first:col_end], block_sol, precision=lax.Precision.HIGHEST
        )
        current = jnp.concatenate([current[:row_end], current[row_end:] - update], axis=0)
        scaled = scale_pivots(
            block_sol,
            pivot_sizes[col_first // 2 : col_end // 2],
            pivot_diag[col_first:col_end],
            pivot_off[col_first // 2 : col_end // 2],
        )
        own_rows = lax.dynamic_slice_in_dim(
            scaled.reshape(slot_count, owners, CYC, columns), device, 1, 1
        )
        outputs.append(own_rows.reshape(panel_rows, columns))
    outputs.append(current[PANELS * panel_rows :])
    return jnp.concatenate(outputs, axis=0)


def solution(mesh):
    in_specs = (
        P(("cuts", "row"), "vec"),
        P("row", None),
        P(("cuts", "row"), None),
        P(("cuts", "row")),
        P("cuts"),
        P("cuts"),
        P("cuts"),
    )
    out_specs = P(("cuts", "row"), "vec")
    owners, shares = mesh.shape["row"], mesh.shape["vec"]
    few = owners == 4 and shares == 4 and DIAG == owners * shares * CYC
    body = local if few else local_many
    return jax.shard_map(body, mesh=mesh, in_specs=in_specs, out_specs=out_specs, check_vma=False)
```

profile of v0, /device:TPU:0, one launch (start us, length us, event | category | flops | bytes accessed | tf_op | source)
XLA Modules:
  0.0 107.0 jit_solution(12448993854041734896)
XLA Ops:
  0.0 0.1 pad_add_fusion.place_ref.after_ref
  0.1 1.8 %first_sends.1 = (f32[2,10,16,256]{3,2,1,0:T(8,128)S(1)}, f32[512,128]{1,0:T(8,128)S(1)}, f32[512,128]{1,0:T(8,128)S(1)}) custom-call(s32[2]{0:T(128)S(1)} %pad_add_fusion.place_ref.after_ref, f32[2048,2048]{1,0:T(8,128)} %factor_ref.11, f32[2048,128]{1,0:T(8,128)} %vec_ref.3), custom_call_target="tpu_custom_call" | custom-call | bytes 4194304 | tf_op jit(solution)/shard_map/first_sends/pallas_call | solution.py:98
  1.9 4.9 %collective-permute-start = (f32[512,128]{1,0:T(8,128)S(1)}, f32[512,128]{1,0:T(8,128)S(1)}, u32[]{:S(2)}, u32[]{:S(2)}) collective-permute-start(f32[512,128]{1,0:T(8,128)S(1)} %get-tuple-element.24), channel_id=1, source_target_pairs={{0,4},{4,8},{8,12},{1,5},{5,9},{9,13},{2,6},{6,10},{10,14},{3,7},{... | collective-permute-start | bytes 786440 | tf_op jit(solution)/shard_map/ppermute | solution.py:519
  6.8 1.3 %collective-permute-start.1 = (f32[512,128]{1,0:T(8,128)S(1)}, f32[512,128]{1,0:T(8,128)S(1)}, u32[]{:S(2)}, u32[]{:S(2)}) collective-permute-start(f32[512,128]{1,0:T(8,128)S(1)} %get-tuple-element.25), channel_id=1, source_target_pairs={{4,0},{8,4},{12,8},{5,1},{9,5},{13,9},{6,2},{10,6},{14,10},{7,3},{... | collective-permute-start | bytes 786440 | tf_op jit(solution)/shard_map/ppermute | solution.py:519
  8.1 2.7 %collective-permute-start.5 = (f32[2,10,16,256]{3,2,1,0:T(8,128)S(1)}, f32[2,10,16,256]{3,2,1,0:T(8,128)S(1)}, u32[]{:S(2)}, u32[]{:S(2)}) collective-permute-start(f32[2,10,16,256]{3,2,1,0:T(8,128)S(1)} %get-tuple-element.26), channel_id=1, source_target_pairs={{0,4},{4,0},{8,12},{12,8},{1,5},{5,1},{9,13},{13,9},{2,6},{6,2},{1... | collective-permute-start | bytes 983048 | tf_op jit(solution)/shard_map/ppermute | solution.py:500
  10.8 2.6 %collective-permute-start.6 = (f32[2,10,16,256]{3,2,1,0:T(8,128)S(1)}, f32[2,10,16,256]{3,2,1,0:T(8,128)S(1)}, u32[]{:S(2)}, u32[]{:S(2)}) collective-permute-start(f32[2,10,16,256]{3,2,1,0:T(8,128)S(1)} %get-tuple-element.26), channel_id=1, source_target_pairs={{0,8},{4,12},{8,0},{12,4},{1,9},{5,13},{9,1},{13,5},{2,10},{6,14},... | collective-permute-start | bytes 983048 | tf_op jit(solution)/shard_map/ppermute | solution.py:500
  13.4 0.0 collective-permute-start.7
  13.4 0.0 copy-start.8
  13.5 0.0 copy-start.9
  13.5 0.0 collective-permute-done.before_ref
  13.5 10.4 %collective-permute-done.1.after_ref = f32[512,128]{1,0:T(8,128)S(1)} collective-permute-done((f32[512,128]{1,0:T(8,128)S(1)}, f32[512,128]{1,0:T(8,128)S(1)}, u32[]{:S(2)}, u32[]{:S(2)}) %collective-permute-start.1) | collective-permute-done | bytes 262176 | tf_op jit(solution)/shard_map/ppermute | solution.py:519
  23.9 8.0 %band_product_split.1.after_ref = f32[4,512,128]{2,1,0:T(8,128)} custom-call(f32[2048,1536]{1,0:T(8,128)} %inter_ref.1, f32[2048,128]{1,0:T(8,128)S(1)} %copy-done, f32[512,128]{1,0:T(8,128)S(1)} %collective-permute-done.before_ref, f32[512,128]{1,0:T(8,128)S(1)} %collective-permute-done.1.after_ref), custom_call_target="tpu_custom_call" | custom-call | flops 3221225472 | bytes 12582912 | tf_op jit(solution)/shard_map/band_product_split/pallas_call | solution.py:137
  32.0 3.5 %all-to-all-start = ((f32[4,512,128]{2,1,0:T(8,128)}), f32[4,512,128]{2,1,0:T(8,128)S(1)}, u32[]{:S(2)}, u32[]{:S(2)}) async-start(f32[4,512,128]{2,1,0:T(8,128)} %band_product_split.1.after_ref), calls=%async_computation | async-start | bytes 2097152 | tf_op jit(solution)/shard_map/all_to_all | solution.py:522
  35.5 3.7 %make_ready.1 = (f32[256,128]{1,0:T(8,128)S(1)}, f32[256,128]{1,0:T(8,128)S(1)}, bf16[1536,1024]{1,0:T(8,128)(2,1)S(1)}, bf16[1536,1024]{1,0:T(8,128)(2,1)S(1)}) custom-call(s32[2]{0:T(128)S(1)} %pad_add_fusion.place_ref.after_ref, f32[4,512,128]{2,1,0:T(8,128)} %band_product_split.1.after_ref, f32[2048,2048]{1,0:T(8,128)} %factor_ref.11, ...), custom_call_target="tpu_custom_call" | custom-call | flops 137438953472 | tf_op jit(solution)/shard_map/make_ready/pallas_call | solution.py:395
  39.3 1.6 %copy-done.3 = bf16[1536,1024]{1,0:T(8,128)(2,1)} copy-done((bf16[1536,1024]{1,0:T(8,128)(2,1)}, bf16[1536,1024]{1,0:T(8,128)(2,1)S(1)}, u32[]{:S(2)}) %copy-start.3) | copy-done | bytes 3145752
  40.9 0.0 collective-permute-done.5.refs_0_
  40.9 3.8 %collective-permute-done.6.refs_1_ = f32[2,10,16,256]{3,2,1,0:T(8,128)S(1)} collective-permute-done((f32[2,10,16,256]{3,2,1,0:T(8,128)S(1)}, f32[2,10,16,256]{3,2,1,0:T(8,128)S(1)}, u32[]{:S(2)}, u32[]{:S(2)}) %collective-permute-start.6) | collective-permute-done | bytes 327712 | tf_op jit(solution)/shard_map/ppermute | solution.py:500
  44.7 0.0 collective-permute-done.7.refs_2_
  44.7 1.6 %collective-permute-start.8 = (f32[3,10,16,256]{3,2,1,0:T(8,128)S(1)}, f32[3,10,16,256]{3,2,1,0:T(8,128)S(1)}, u32[]{:S(2)}, u32[]{:S(2)}) collective-permute-start(f32[3,10,16,256]{3,2,1,0:T(8,128)S(1)} %stack.14.first_ref), channel_id=1, source_target_pairs={{0,2},{1,3},{2,0},{3,1},{4,6},{5,7},{6,4},{7,5},{8,10},{9,11},{10,... | collective-permute-start | bytes 1474568 | tf_op jit(solution)/shard_map/ppermute | solution.py:500
  46.3 7.3 %collective-permute-done.8.second_ref = f32[3,10,16,256]{3,2,1,0:T(8,128)S(1)} collective-permute-done((f32[3,10,16,256]{3,2,1,0:T(8,128)S(1)}, f32[3,10,16,256]{3,2,1,0:T(8,128)S(1)}, u32[]{:S(2)}, u32[]{:S(2)}) %collective-permute-start.8) | collective-permute-done | bytes 491552 | tf_op jit(solution)/shard_map/ppermute | solution.py:500
  53.6 0.1 pair.2.refs_0_
  53.7 0.1 collective-permute-start.9
  53.8 14.3 %all-to-all-done = f32[4,512,128]{2,1,0:T(8,128)S(1)} async-done(((f32[4,512,128]{2,1,0:T(8,128)}), f32[4,512,128]{2,1,0:T(8,128)S(1)}, u32[]{:S(2)}, u32[]{:S(2)}) %all-to-all-start) | async-done | bytes 1048608 | tf_op jit(solution)/shard_map/all_to_all | solution.py:522
  68.1 0.9 order_rows.2.after_ref.refs_0_.refs_3_
  69.1 0.1 collective-permute-start.2
  69.1 0.1 collective-permute-start.3
  69.2 4.3 %collective-permute-start.4 = (f32[256,128]{1,0:T(8,128)S(1)}, f32[256,128]{1,0:T(8,128)S(1)}, u32[]{:S(2)}, u32[]{:S(2)}) collective-permute-start(f32[256,128]{1,0:T(8,128)S(1)} %order_rows.2.after_ref.refs_0_.refs_3_), channel_id=1, source_target_pairs={{0,12},{4,8},{8,4},{12,0},{1,13},{5,9},{9,5},{13,1},{2,14},{6,10},... | collective-permute-start | bytes 393224 | tf_op jit(solution)/shard_map/ppermute | solution.py:500
  73.6 1.6 %collective-permute-start.13 = (f32[3,10,16,256]{3,2,1,0:T(8,128)S(1)}, f32[3,10,16,256]{3,2,1,0:T(8,128)S(1)}, u32[]{:S(2)}, u32[]{:S(2)}) collective-permute-start(f32[3,10,16,256]{3,2,1,0:T(8,128)S(1)} %stack.15.first_ref), channel_id=1, source_target_pairs={{0,2},{1,3},{2,0},{3,1},{4,6},{5,7},{6,4},{7,5},{8,10},{9,11},{10,... | collective-permute-start | bytes 1474568 | tf_op jit(solution)/shard_map/ppermute | solution.py:500
  75.1 0.0 collective-permute-done.9.refs_1_
  75.1 5.8 %invert_panel.2 = (bf16[1024,1024]{1,0:T(8,128)(2,1)S(1)}, bf16[1024,1024]{1,0:T(8,128)(2,1)S(1)}, bf16[4,256,256]{2,1,0:T(8,128)(2,1)S(1)}, bf16[4,256,256]{2,1,0:T(8,128)(2,1)S(1)}) custom-call(s32[2]{0:T(128)S(1)} %pad_add_fusion.place_ref.after_ref, f32[256,128]{1,0:T(8,128)S(1)} %order_rows.2.after_ref.refs_0_.refs_3_, f32[2048,2048]{1,0:T(8,128)} %factor_ref.11, ...), custom_call_target="tpu_custom_call" | custom-call | flops 137438953472 | bytes 12582912 | tf_op jit(solution)/shard_map/invert_panel/pallas_call | solution.py:257
  81.0 2.6 %order_rows.3 = (f32[256,128]{1,0:T(8,128)S(1)}, f32[1536,128]{1,0:T(8,128)S(1)}) custom-call(s32[2048]{0:T(1024)S(1)} %copy-done.7, f32[2048,128]{1,0:T(8,128)S(1)} %bitcast.6, f32[256,128]{1,0:T(8,128)S(1)} %order_rows.2.after_ref.refs_0_.refs_3_), custom_call_target="tpu_custom_call" | custom-call | bytes 2097152 | tf_op jit(solution)/shard_map/order_rows/pallas_call | solution.py:292
  83.6 1.0 collective-permute-done.13.second_ref
  84.6 0.1 pair.3.refs_0_
  84.7 0.1 collective-permute-start.14
  84.8 0.0 collective-permute-done.2.refs_1_
  84.8 0.0 collective-permute-done.3.refs_2_
  84.8 0.0 collective-permute-done.4.refs_3_
  84.8 3.5 %first_solve.1 = (f32[64,16,128]{2,1,0:T(8,128)S(1)}, f32[256,128]{1,0:T(8,128)S(1)}) custom-call(s32[2]{0:T(128)S(1)} %pad_add_fusion.place_ref.after_ref, f32[2048,2048]{1,0:T(8,128)} %factor_ref.11, f32[256,128]{1,0:T(8,128)S(1)} %order_rows.2.after_ref.refs_0_.refs_3_, f32[256,128]{1,0:T(8,128)S(1)} %collective-permute-done.2.refs_1_, ...), custom_call_target="tpu_custom_call" | custom-call | flops 137438953472 | bytes 6291456 | tf_op jit(solution)/shard_map/first_solve/pallas_call | solution.py:336
  88.4 0.8 collective-permute-start.10
  89.2 1.2 %collective-permute-start.11 = (f32[256,128]{1,0:T(8,128)S(1)}, f32[256,128]{1,0:T(8,128)S(1)}, u32[]{:S(2)}, u32[]{:S(2)}) collective-permute-start(f32[256,128]{1,0:T(8,128)S(1)} %get-tuple-element.33.refs_0_), channel_id=1, source_target_pairs={{0,8},{4,12},{8,0},{12,4},{1,9},{5,13},{9,1},{13,5},{2,10},{6,14},... | collective-permute-start | bytes 393224 | tf_op jit(solution)/shard_map/ppermute | solution.py:500
  90.4 2.4 %collective-permute-start.12 = (f32[256,128]{1,0:T(8,128)S(1)}, f32[256,128]{1,0:T(8,128)S(1)}, u32[]{:S(2)}, u32[]{:S(2)}) collective-permute-start(f32[256,128]{1,0:T(8,128)S(1)} %get-tuple-element.33.refs_0_), channel_id=1, source_target_pairs={{0,12},{4,8},{8,4},{12,0},{1,13},{5,9},{9,5},{13,1},{2,14},{6,10},... | collective-permute-start | bytes 393224 | tf_op jit(solution)/shard_map/ppermute | solution.py:500
  92.8 3.8 %middle_update.1.refs_13_ = f32[1536,128]{1,0:T(8,128)S(1)} custom-call(f32[2048,2048]{1,0:T(8,128)} %factor_ref.11, f32[1536,128]{1,0:T(8,128)S(1)} %get-tuple-element.42.rest_ref, f32[64,16,128]{2,1,0:T(8,128)S(1)} %get-tuple-element.34.after_ref.y_ref.refs_8_), custom_call_target="tpu_custom_call" | custom-call | flops 1610612736 | bytes 8388608 | tf_op jit(solution)/shard_map/middle_update/pallas_call | solution.py:424
  96.6 0.0 collective-permute-done.14.refs_1_
  96.7 5.6 %invert_panel.3 = (bf16[1024,1024]{1,0:T(8,128)(2,1)S(1)}, bf16[1024,1024]{1,0:T(8,128)(2,1)S(1)}, bf16[4,256,256]{2,1,0:T(8,128)(2,1)S(1)}, bf16[4,256,256]{2,1,0:T(8,128)(2,1)S(1)}) custom-call(s32[2]{0:T(128)S(1)} %pad_add_fusion.place_ref.after_ref, f32[64,16,128]{2,1,0:T(8,128)S(1)} %get-tuple-element.34.after_ref.y_ref.refs_8_, ...), custom_call_target="tpu_custom_call" | custom-call | flops 1073741824 | bytes 12582912 | tf_op jit(solution)/shard_map/invert_panel/pallas_call | solution.py:257
  102.3 0.0 collective-permute-done.10.refs_1_
  102.3 0.0 collective-permute-done.11.refs_2_
  102.3 0.0 collective-permute-done.12.refs_3_
  102.3 4.5 %last_solve.1 = f32[2048,128]{1,0:T(8,128)} custom-call(s32[2]{0:T(128)S(1)} %pad_add_fusion.place_ref.after_ref, f32[256,128]{1,0:T(8,128)S(1)} %get-tuple-element.33.refs_0_, f32[256,128]{1,0:T(8,128)S(1)} %collective-permute-done.10.refs_1_, f32[256,128]{1,0:T(8,128)S(1)} %collective-permute-done.11.refs_2_, ...), custom_call_target="tpu_custom_call" | custom-call | flops 2147483648 | bytes 12582912 | tf_op jit(solution)/shard_map/last_solve/pallas_call | solution.py:480
  (22 shorter events, 0.1 us)
Async XLA Ops:
  0.1 13.4 %copy-start.10 = (f32[2048]{0:T(1024)S(1)}, f32[2048]{0:T(1024)}, u32[]{:S(2)}) copy-start(f32[2048]{0:T(1024)} %param.12) | copy-start | bytes 24580
  0.1 23.9 %copy-start = (f32[2048,128]{1,0:T(8,128)S(1)}, f32[2048,128]{1,0:T(8,128)}, u32[]{:S(2)}) copy-start(f32[2048,128]{1,0:T(8,128)} %vec_ref.3) | copy-start | bytes 3145732
  1.9 11.6 %collective-permute-start = (f32[512,128]{1,0:T(8,128)S(1)}, f32[512,128]{1,0:T(8,128)S(1)}, u32[]{:S(2)}, u32[]{:S(2)}) collective-permute-start(f32[512,128]{1,0:T(8,128)S(1)} %get-tuple-element.24), channel_id=1, source_target_pairs={{0,4},{4,8},{8,12},{1,5},{5,9},{9,13},{2,6},{6,10},{10,14},{3,7},{... | collective-permute-start | bytes 786440 | tf_op jit(solution)/shard_map/ppermute | solution.py:519
  6.8 17.1 %collective-permute-start.1 = (f32[512,128]{1,0:T(8,128)S(1)}, f32[512,128]{1,0:T(8,128)S(1)}, u32[]{:S(2)}, u32[]{:S(2)}) collective-permute-start(f32[512,128]{1,0:T(8,128)S(1)} %get-tuple-element.25), channel_id=1, source_target_pairs={{4,0},{8,4},{12,8},{5,1},{9,5},{13,9},{6,2},{10,6},{14,10},{7,3},{... | collective-permute-start | bytes 786440 | tf_op jit(solution)/shard_map/ppermute | solution.py:519
  8.1 32.8 %collective-permute-start.5 = (f32[2,10,16,256]{3,2,1,0:T(8,128)S(1)}, f32[2,10,16,256]{3,2,1,0:T(8,128)S(1)}, u32[]{:S(2)}, u32[]{:S(2)}) collective-permute-start(f32[2,10,16,256]{3,2,1,0:T(8,128)S(1)} %get-tuple-element.26), channel_id=1, source_target_pairs={{0,4},{4,0},{8,12},{12,8},{1,5},{5,1},{9,13},{13,9},{2,6},{6,2},{1... | collective-permute-start | bytes 983048 | tf_op jit(solution)/shard_map/ppermute | solution.py:500
  10.8 33.9 %collective-permute-start.6 = (f32[2,10,16,256]{3,2,1,0:T(8,128)S(1)}, f32[2,10,16,256]{3,2,1,0:T(8,128)S(1)}, u32[]{:S(2)}, u32[]{:S(2)}) collective-permute-start(f32[2,10,16,256]{3,2,1,0:T(8,128)S(1)} %get-tuple-element.26), channel_id=1, source_target_pairs={{0,8},{4,12},{8,0},{12,4},{1,9},{5,13},{9,1},{13,5},{2,10},{6,14},... | collective-permute-start | bytes 983048 | tf_op jit(solution)/shard_map/ppermute | solution.py:500
  13.4 31.3 %collective-permute-start.7 = (f32[2,10,16,256]{3,2,1,0:T(8,128)S(1)}, f32[2,10,16,256]{3,2,1,0:T(8,128)S(1)}, u32[]{:S(2)}, u32[]{:S(2)}) collective-permute-start(f32[2,10,16,256]{3,2,1,0:T(8,128)S(1)} %get-tuple-element.26), channel_id=1, source_target_pairs={{0,12},{4,8},{8,4},{12,0},{1,13},{5,9},{9,5},{13,1},{2,14},{6,10},... | collective-permute-start | bytes 983048 | tf_op jit(solution)/shard_map/ppermute | solution.py:500
  13.4 22.1 %copy-start.8 = (s32[1024]{0:T(1024)S(1)}, s32[1024]{0:T(1024)}, u32[]{:S(2)}) copy-start(s32[1024]{0:T(1024)} %param.11) | copy-start | bytes 12292
  13.5 22.1 %copy-start.9 = (f32[1024]{0:T(1024)S(1)}, f32[1024]{0:T(1024)}, u32[]{:S(2)}) copy-start(f32[1024]{0:T(1024)} %param.13) | copy-start | bytes 12292
  32.0 36.2 %all-to-all-start = ((f32[4,512,128]{2,1,0:T(8,128)}), f32[4,512,128]{2,1,0:T(8,128)S(1)}, u32[]{:S(2)}, u32[]{:S(2)}) async-start(f32[4,512,128]{2,1,0:T(8,128)} %band_product_split.1.after_ref), calls=%async_computation | async-start | bytes 2097152 | tf_op jit(solution)/shard_map/all_to_all | solution.py:522
  39.3 1.6 %copy-start.3 = (bf16[1536,1024]{1,0:T(8,128)(2,1)}, bf16[1536,1024]{1,0:T(8,128)(2,1)S(1)}, u32[]{:S(2)}) copy-start(bf16[1536,1024]{1,0:T(8,128)(2,1)S(1)} %get-tuple-element.41.refs_12_) | copy-start | bytes 9437188
  40.9 12.8 %copy-start.1 = (bf16[1536,1024]{1,0:T(8,128)(2,1)}, bf16[1536,1024]{1,0:T(8,128)(2,1)S(1)}, u32[]{:S(2)}) copy-start(bf16[1536,1024]{1,0:T(8,128)(2,1)S(1)} %get-tuple-element.40.refs_11_) | copy-start | bytes 9437188
  40.9 12.8 %copy-start.5 = (f32[256,128]{1,0:T(8,128)}, f32[256,128]{1,0:T(8,128)S(1)}, u32[]{:S(2)}) copy-start(f32[256,128]{1,0:T(8,128)S(1)} %get-tuple-element.27.refs_3_.refs_9_) | copy-start | bytes 393220
  40.9 27.2 %copy-start.7 = (s32[2048]{0:T(1024)S(1)}, s32[2048]{0:T(1024)}, u32[]{:S(2)}) copy-start(s32[2048]{0:T(1024)} %pivot_ref.3) | copy-start | bytes 24580
  44.7 8.9 %collective-permute-start.8 = (f32[3,10,16,256]{3,2,1,0:T(8,128)S(1)}, f32[3,10,16,256]{3,2,1,0:T(8,128)S(1)}, u32[]{:S(2)}, u32[]{:S(2)}) collective-permute-start(f32[3,10,16,256]{3,2,1,0:T(8,128)S(1)} %stack.14.first_ref), channel_id=1, source_target_pairs={{0,2},{1,3},{2,0},{3,1},{4,6},{5,7},{6,4},{7,5},{8,10},{9,11},{10,... | collective-permute-start | bytes 1474568 | tf_op jit(solution)/shard_map/ppermute | solution.py:500
  53.7 21.4 %collective-permute-start.9 = (f32[2,3,10,16,256]{4,3,2,1,0:T(8,128)S(1)}, f32[2,3,10,16,256]{4,3,2,1,0:T(8,128)}, u32[]{:S(2)}, u32[]{:S(2)}) collective-permute-start(f32[2,3,10,16,256]{4,3,2,1,0:T(8,128)S(1)} %pair.2.refs_0_), channel_id=1, source_target_pairs={{0,1},{1,0},{2,3},{3,2},{4,5},{5,4},{6,7},{7,6},{8,9},{9,8},{10,11... | collective-permute-start | bytes 2949128 | tf_op jit(solution)/shard_map/ppermute | solution.py:500
  69.1 15.7 %collective-permute-start.2 = (f32[256,128]{1,0:T(8,128)S(1)}, f32[256,128]{1,0:T(8,128)S(1)}, u32[]{:S(2)}, u32[]{:S(2)}) collective-permute-start(f32[256,128]{1,0:T(8,128)S(1)} %order_rows.2.after_ref.refs_0_.refs_3_), channel_id=1, source_target_pairs={{0,4},{4,0},{8,12},{12,8},{1,5},{5,1},{9,13},{13,9},{2,6},{6,2},{1... | collective-permute-start | bytes 393224 | tf_op jit(solution)/shard_map/ppermute | solution.py:500
  69.1 15.6 %collective-permute-start.3 = (f32[256,128]{1,0:T(8,128)S(1)}, f32[256,128]{1,0:T(8,128)S(1)}, u32[]{:S(2)}, u32[]{:S(2)}) collective-permute-start(f32[256,128]{1,0:T(8,128)S(1)} %order_rows.2.after_ref.refs_0_.refs_3_), channel_id=1, source_target_pairs={{0,8},{4,12},{8,0},{12,4},{1,9},{5,13},{9,1},{13,5},{2,10},{6,14},... | collective-permute-start | bytes 393224 | tf_op jit(solution)/shard_map/ppermute | solution.py:500
  69.2 15.6 %collective-permute-start.4 = (f32[256,128]{1,0:T(8,128)S(1)}, f32[256,128]{1,0:T(8,128)S(1)}, u32[]{:S(2)}, u32[]{:S(2)}) collective-permute-start(f32[256,128]{1,0:T(8,128)S(1)} %order_rows.2.after_ref.refs_0_.refs_3_), channel_id=1, source_target_pairs={{0,12},{4,8},{8,4},{12,0},{1,13},{5,9},{9,5},{13,1},{2,14},{6,10},... | collective-permute-start | bytes 393224 | tf_op jit(solution)/shard_map/ppermute | solution.py:500
  73.6 11.1 %collective-permute-start.13 = (f32[3,10,16,256]{3,2,1,0:T(8,128)S(1)}, f32[3,10,16,256]{3,2,1,0:T(8,128)S(1)}, u32[]{:S(2)}, u32[]{:S(2)}) collective-permute-start(f32[3,10,16,256]{3,2,1,0:T(8,128)S(1)} %stack.15.first_ref), channel_id=1, source_target_pairs={{0,2},{1,3},{2,0},{3,1},{4,6},{5,7},{6,4},{7,5},{8,10},{9,11},{10,... | collective-permute-start | bytes 1474568 | tf_op jit(solution)/shard_map/ppermute | solution.py:500
  84.7 11.9 %collective-permute-start.14 = (f32[2,3,10,16,256]{4,3,2,1,0:T(8,128)S(1)}, f32[2,3,10,16,256]{4,3,2,1,0:T(8,128)S(1)}, u32[]{:S(2)}, u32[]{:S(2)}) collective-permute-start(f32[2,3,10,16,256]{4,3,2,1,0:T(8,128)S(1)} %pair.3.refs_0_), channel_id=1, source_target_pairs={{0,1},{1,0},{2,3},{3,2},{4,5},{5,4},{6,7},{7,6},{8,9},{9,8},{10,11... | collective-permute-start | bytes 2949128 | tf_op jit(solution)/shard_map/ppermute | solution.py:500
  88.4 13.9 %collective-permute-start.10 = (f32[256,128]{1,0:T(8,128)S(1)}, f32[256,128]{1,0:T(8,128)S(1)}, u32[]{:S(2)}, u32[]{:S(2)}) collective-permute-start(f32[256,128]{1,0:T(8,128)S(1)} %get-tuple-element.33.refs_0_), channel_id=1, source_target_pairs={{0,4},{4,0},{8,12},{12,8},{1,5},{5,1},{9,13},{13,9},{2,6},{6,2},{1... | collective-permute-start | bytes 393224 | tf_op jit(solution)/shard_map/ppermute | solution.py:500
  89.2 13.1 %collective-permute-start.11 = (f32[256,128]{1,0:T(8,128)S(1)}, f32[256,128]{1,0:T(8,128)S(1)}, u32[]{:S(2)}, u32[]{:S(2)}) collective-permute-start(f32[256,128]{1,0:T(8,128)S(1)} %get-tuple-element.33.refs_0_), channel_id=1, source_target_pairs={{0,8},{4,12},{8,0},{12,4},{1,9},{5,13},{9,1},{13,5},{2,10},{6,14},... | collective-permute-start | bytes 393224 | tf_op jit(solution)/shard_map/ppermute | solution.py:500
  90.4 11.9 %collective-permute-start.12 = (f32[256,128]{1,0:T(8,128)S(1)}, f32[256,128]{1,0:T(8,128)S(1)}, u32[]{:S(2)}, u32[]{:S(2)}) collective-permute-start(f32[256,128]{1,0:T(8,128)S(1)} %get-tuple-element.33.refs_0_), channel_id=1, source_target_pairs={{0,12},{4,8},{8,4},{12,0},{1,13},{5,9},{9,5},{13,1},{2,14},{6,10},... | collective-permute-start | bytes 393224 | tf_op jit(solution)/shard_map/ppermute | solution.py:500
  96.6 5.7 %copy-start.2 = (bf16[1536,1024]{1,0:T(8,128)(2,1)S(1)}, bf16[1536,1024]{1,0:T(8,128)(2,1)}, u32[]{:S(2)}) copy-start(bf16[1536,1024]{1,0:T(8,128)(2,1)} %copy-done.1) | copy-start | bytes 9437188
  96.6 5.7 %copy-start.4 = (bf16[1536,1024]{1,0:T(8,128)(2,1)S(1)}, bf16[1536,1024]{1,0:T(8,128)(2,1)}, u32[]{:S(2)}) copy-start(bf16[1536,1024]{1,0:T(8,128)(2,1)} %copy-done.3) | copy-start | bytes 9437188
  96.6 5.7 %copy-start.6 = (f32[256,128]{1,0:T(8,128)S(1)}, f32[256,128]{1,0:T(8,128)}, u32[]{:S(2)}) copy-start(f32[256,128]{1,0:T(8,128)} %copy-done.5) | copy-start | bytes 393220
where the time goes:
time: 107 us
  Pallas kernels  40.6 us (38%)
  waiting for transfers between devices  37 us (35%)
  starting transfers between devices  27.2 us (25%)
  local copies, waits for them, and re-layouts  1.67 us (2%)
    ppermute x13, starting transfers between devices, swap_with(): return lax.ppermute(value, axis, [(i, i ^ distance) for i in range(size)])  17.4 us
    all_to_all x1, waiting for transfers between devices, local(): lax.all_to_all(product, 'row', 0, 0, tiled=True).reshape(vectors.shape)  14.3 us
    ppermute x13, waiting for transfers between devices, swap_with(): return lax.ppermute(value, axis, [(i, i ^ distance) for i in range(size)])  12.2 us
    pallas_call x2, Pallas kernels, invert_panel(): pl.pallas_call(functools.partial(invert_kernel, panel, owners, shares), o...  11.4 us
    ppermute x2, waiting for transfers between devices, local(): halo = (lax.ppermute(last, 'row', up), lax.ppermute(first, 'row', down))  10.5 us
    pallas_call x1, Pallas kernels, band_product_split(): pl.pallas_call(band_kernel, out_shape=shaped(owners, rows // owners, colu...  8.04 us
    ppermute x2, starting transfers between devices, local(): halo = (lax.ppermute(last, 'row', up), lax.ppermute(first, 'row', down))  6.24 us
    pallas_call x1, Pallas kernels, last_solve(): pl.pallas_call(functools.partial(last_kernel, owners, tile_rows), out_sha...  4.51 us
  transfers between devices with their start and end apart: 16, of which 5 were waited for; matrix products, arithmetic and copies ran while one was open for 0% of the time, Pallas kernels for 32%

commit v1 on v0

--- a/solution.py
+++ b/solution.py
@@ -152,42 +152,64 @@
     )(intersection, vectors, *halo)
 
 
-def stack_kernel(panel, count, *refs):
-    for k in range(count):
-        refs[-1][k] = refs[k][panel]
-
-
-def stack(panel, pieces, after):
-    count = len(pieces)
-    return pl.pallas_call(
-        functools.partial(stack_kernel, panel, count),
-        out_shape=shaped(count, *pieces[0].shape[1:]),
-        in_specs=[IN_VMEM] * count + [pl.BlockSpec(memory_space=pl.ANY)],
-        out_specs=IN_VMEM,
+def pass_kernel(value_ref, after_ref, out_ref):
+    pass
+
+
+def pass_on(value, after):
+    anywhere = pl.BlockSpec(memory_space=pl.ANY)
+    return pl.pallas_call(
+        pass_kernel,
+        out_shape=shaped(*value.shape),
+        in_specs=[anywhere, anywhere],
+        out_specs=anywhere,
+        input_output_aliases={0: 0},
+        compiler_params=params(1),
+        name="pass_on",
+    )(value, after)
+
+
+def from_others(value, after):
+    end = lax.axis_size("row") - 1
+    middle = [(i, end - i) for i in range(1, end)]
+    across = pass_on(swap_with(value, "row", 2), after)
+    near, inner = swap_with(value, "row", 1), lax.ppermute(value, "row", middle)
+    outer = lax.ppermute(across, "row", [(i, i ^ 1) for i, _ in middle])
+    return near, across, inner, outer
+
+
+def stack_kernel(place_ref, near_ref, across_ref, inner_ref, outer_ref, after_ref, *out_refs):
+    me = place_ref[0]
+    end = out_refs[0].shape[0]
+    for panel, out_ref in enumerate(out_refs):
+        out_ref[0] = near_ref[panel]
+        out_ref[1] = across_ref[panel]
+
+    @pl.when((me > 0) & (me < end))
+    def _():
+        for panel, out_ref in enumerate(out_refs):
+            out_ref[2] = inner_ref[panel]
+
+    @pl.when((me == 0) | (me == end))
+    def _():
+        for panel, out_ref in enumerate(out_refs):
+            out_ref[2] = outer_ref[panel]
+
+
+def stack(place, pieces, after):
+    return pl.pallas_call(
+        stack_kernel,
+        out_shape=[shaped(3, *pieces[0].shape[1:])] * PANELS,
+        in_specs=[IN_SMEM] + [IN_VMEM] * 4 + [pl.BlockSpec(memory_space=pl.ANY)],
+        out_specs=[IN_VMEM] * PANELS,
         compiler_params=params(4),
         name="stack",
-    )(*pieces, after)
-
-
-def pair_kernel(first_ref, second_ref, *refs):
-    out_ref = refs[-1]
-    out_ref[0] = first_ref[...]
-    out_ref[1] = second_ref[...]
-
-
-def pair(first, second, after):
-    return pl.pallas_call(
-        pair_kernel,
-        out_shape=shaped(2, *first.shape),
-        in_specs=[IN_VMEM] * 2 + [pl.BlockSpec(memory_space=pl.ANY)] * len(after),
-        out_specs=IN_VMEM,
-        compiler_params=params(4),
-        name="pair",
-    )(first, second, *after)
+    )(place, *pieces, after)
 
 
 def invert_kernel(panel, owners, shares, place_ref, after_ref, factor_ref, *refs):
-    mine_ref, theirs_ref, high_ref, low_ref, inv_high_ref, inv_low_ref, own_ref, tri_ref, sem = refs
+    pieces = refs[:shares]
+    high_ref, low_ref, inv_high_ref, inv_low_ref, own_ref, tri_ref, sem = refs[-7:]
     groups = PANEL // DIAG
     me, part = place_ref[0], place_ref[1]
     rows = own_ref.shape[0]
@@ -201,8 +223,7 @@
             at = 0
             for k in range(groups):
                 for j in range(k + 1):
-                    source = theirs_ref if turn % 2 else mine_ref
-                    piece = source[turn // 2, other - 1, at]
+                    piece = pieces[turn][other - 1, at]
                     to = (k * shares + (part ^ turn)) * owners + owner
                     tri_ref[to, :, j * DIAG : (j + 1) * DIAG] = piece
                     at += 1
@@ -372,36 +393,57 @@
     return turned
 
 
-def ready_kernel(
-    tile_rows, place_ref, after_ref, factor_ref, sizes_ref, diag_ref, off_ref, keep_ref, swap_ref, high_ref, low_ref,
-    left_ref, sems,
-):
+def weights_kernel(place_ref, after_ref, sizes_ref, diag_ref, off_ref, keep_ref, swap_ref):
+    keep_ref[...], swap_ref[...] = pivot_weights(place_ref[0], sizes_ref[...], diag_ref[...], off_ref[...])
+
+
+def own_weights(place, pivots, after):
+    weight = shaped(pivots[1].shape[1], HALF)
+    return pl.pallas_call(
+        weights_kernel,
+        out_shape=[weight, weight],
+        in_specs=[IN_SMEM, pl.BlockSpec(memory_space=pl.ANY)] + [IN_VMEM] * len(pivots),
+        out_specs=[IN_VMEM] * 2,
+        compiler_params=params(4),
+        cost_estimate=cost(HEAVY, 0),
+        name="own_weights",
+    )(place, after, *pivots)
+
+
+def halve_kernel(tile_rows, factor_ref, after_ref, out_ref, token_ref, left_ref, parts_ref, in_sems, out_sems):
+    token_ref[...] = jnp.zeros_like(token_ref)
     tiles = left_ref.shape[0]
-    loads = []
+    loads, stores = [], []
     for t in range(tiles):
         source = factor_ref.at[pl.ds((t + 1) * tile_rows, tile_rows), pl.ds((PANELS - 1) * PANEL, PANEL)]
-        loads.append(pltpu.make_async_copy(source, left_ref.at[t], sems.at[t]))
+        loads.append(pltpu.make_async_copy(source, left_ref.at[t], in_sems.at[t]))
         loads[t].start()
-    keep_ref[...], swap_ref[...] = pivot_weights(place_ref[0], sizes_ref[...], diag_ref[...], off_ref[...])
     for t in range(tiles):
         loads[t].wait()
-        rows = slice(t * tile_rows, (t + 1) * tile_rows)
-        high_ref[rows], low_ref[rows] = split(left_ref[t])
-
-
-def make_ready(place, factor, pivots, tile_rows, after):
-    weight = shaped(pivots[1].shape[1], HALF)
+        parts_ref[t, 0], parts_ref[t, 1] = split(left_ref[t])
+        stores.append(pltpu.make_async_copy(parts_ref.at[t], out_ref.at[t], out_sems.at[t]))
+        stores[t].start()
+    for store in stores:
+        store.wait()
+
+
+def halve_last(factor, tile_rows, after):
     tiles = factor.shape[0] // tile_rows - 1
     return pl.pallas_call(
-        functools.partial(ready_kernel, tile_rows),
-        out_shape=[weight, weight] + [shaped(tiles * tile_rows, PANEL, dtype=BF16)] * 2,
-        in_specs=[IN_SMEM, pl.BlockSpec(memory_space=pl.ANY), IN_HBM] + [IN_VMEM] * len(pivots),
-        out_specs=[IN_VMEM] * 4,
-        scratch_shapes=[pltpu.VMEM((tiles, tile_rows, PANEL), F32), pltpu.SemaphoreType.DMA((tiles,))],
-        compiler_params=params(12),
-        cost_estimate=cost(HEAVY, 0),
-        name="make_ready",
-    )(place, after, factor, *pivots)
+        functools.partial(halve_kernel, tile_rows),
+        out_shape=[shaped(tiles, 2, tile_rows, PANEL, dtype=BF16), shaped(8, HALF)],
+        in_specs=[IN_HBM, pl.BlockSpec(memory_space=pl.ANY)],
+        out_specs=[IN_HBM, IN_VMEM],
+        scratch_shapes=[
+            pltpu.VMEM((tiles, tile_rows, PANEL), F32),
+            pltpu.VMEM((tiles, 2, tile_rows, PANEL), BF16),
+            pltpu.SemaphoreType.DMA((tiles,)),
+            pltpu.SemaphoreType.DMA((tiles,)),
+        ],
+        compiler_params=params(18),
+        cost_estimate=cost(LIGHT, 12 * MIB),
+        name="halve_last",
+    )(factor, after)
 
 
 def middle_kernel(tile_rows, factor_ref, rest_ref, y_ref, out_ref, wide_ref, left_ref, sems):
@@ -437,17 +479,17 @@
     )(factor, rest, y)
 
 
-def last_kernel(owners, tile_rows, place_ref, *refs):
+def last_kernel(owners, tile_rows, place_ref, left_ref, *refs):
     pieces = refs[:owners]
-    high, low, inv_high, inv_low, y_ref, keep_ref, swap_ref = refs[owners : owners + 7]
-    left_high, left_low, rest_ref, out_ref, rhs_ref, wide_ref, second_ref, stage_ref, sems = refs[owners + 7 :]
+    high, low, inv_high, inv_low, y_ref, keep_ref, swap_ref, rest_ref = refs[owners : owners + 8]
+    out_ref, rhs_ref, wide_ref, second_ref, stage_ref, sems = refs[owners + 8 :]
     me = place_ref[0]
     solve_into(me, owners, pieces, high, low, inv_high, inv_low, rhs_ref, wide_ref, second_ref)
     stores = []
     for t in range(stage_ref.shape[0]):
         if t:
             rows = slice((t - 1) * tile_rows, t * tile_rows)
-            stage_ref[t] = rest_ref[rows] - parts_times(left_high[rows], left_low[rows], wide_ref[...])
+            stage_ref[t] = rest_ref[rows] - parts_times(left_ref[t - 1, 0], left_ref[t - 1, 1], wide_ref[...])
         else:
             scale_own_rows(me, owners, y_ref, second_ref, keep_ref, swap_ref, stage_ref)
         target = out_ref.at[pl.ds(t * tile_rows, tile_rows)]
@@ -473,14 +515,14 @@
             stage_ref[0, at * CYC : (at + 1) * CYC] = mixed
 
 
-def last_solve(place, pieces, prepared, y, weights, left, rest, tile_rows):
+def last_solve(place, parts, pieces, prepared, y, weights, rest, tile_rows):
     owners = len(pieces)
     columns = rest.shape[1]
     rows = rest.shape[0] + tile_rows
     return pl.pallas_call(
         functools.partial(last_kernel, owners, tile_rows),
         out_shape=shaped(rows, columns),
-        in_specs=[IN_SMEM] + [IN_VMEM] * (owners + 10),
+        in_specs=[IN_SMEM] + [IN_VMEM] * (owners + 9),
         out_specs=IN_HBM,
         scratch_shapes=[
             pltpu.VMEM((PANEL // CYC, CYC, columns), F32),
@@ -489,10 +531,10 @@
             pltpu.VMEM((rows // tile_rows, tile_rows, columns), F32),
             pltpu.SemaphoreType.DMA((rows // tile_rows,)),
         ],
-        compiler_params=params(12),
+        compiler_params=params(16),
         cost_estimate=cost(8 * rows * PANEL * columns, 12 * MIB),
         name="last_solve",
-    )(place, *pieces, *prepared, y, *weights, *left, rest)
+    )(place, parts, *pieces, *prepared, y, *weights, rest)
 
 
 def swap_with(value, axis, distance):
@@ -517,30 +559,31 @@
     up = [(i, i + 1) for i in range(owners - 1)]
     down = [(j, i) for i, j in up]
     halo = lax.ppermute(last, "row", up), lax.ppermute(first, "row", down)
-    direct = from_all(share, "row")[1:]
     product = band_product_split(intersection, vectors, halo, owners)
     grouped = lax.all_to_all(product, "row", 0, 0, tiled=True).reshape(vectors.shape)
 
-    def share_out(panel, after, after_crossing):
-        stacked = stack(panel, direct, after)
-        mine = pair(stacked, swap_with(stacked, "vec", 2), after_crossing)
-        return mine, swap_with(mine, "vec", 1)
+    def share_out(stacked, after):
+        across = pass_on(swap_with(stacked, "vec", 2), after)
+        return stacked, swap_with(stacked, "vec", 1), across, swap_with(across, "vec", 1)
 
     tile_rows = PANELS * panel_rows
     pivots = [a.reshape(pivot_diag.shape[0] // DIAG, -1) for a in (pivot_sizes, pivot_diag, pivot_off)]
-    keep, swap, *left = make_ready(place, factor, pivots, tile_rows, product)
-    shared = share_out(0, keep, ())
-    (first,) = order_rows(0, [panel_rows], pivot_rows, grouped, place)
+    keep, swap = own_weights(place, pivots, product)
+    direct = from_others(share, keep)
+    parts, halved = halve_last(factor, tile_rows, keep)
+    (first,) = order_rows(0, [panel_rows], pivot_rows, grouped, halved)
+    stacked = stack(place, direct, keep)
+    shared = share_out(stacked[0], first)
     prepared = invert_panel(0, place, factor, shared, owners, shares, panel_rows, first, HEAVY)
     rest_rows = factor.shape[0] - tile_rows
-    second, rest = order_rows(panel_rows, [tile_rows - panel_rows, rest_rows], pivot_rows, grouped, first)
-    later = share_out(1, first, (prepared[2], second))
+    second, rest = order_rows(panel_rows, [tile_rows - panel_rows, rest_rows], pivot_rows, grouped, prepared[2])
+    later = share_out(stacked[1], second)
     pieces = from_all(first, "row")
     y, second = first_solve(place, pieces, prepared, factor, second, panel_rows)
     pieces = from_all(second, "row")
     rest = middle_update(rest, y, factor, tile_rows)
     prepared = invert_panel(1, place, factor, later, owners, shares, panel_rows, y, LIGHT)
-    return last_solve(place, pieces, prepared, y, (keep, swap), left, rest, tile_rows)
+    return last_solve(place, parts, pieces, prepared, y, (keep, swap), rest, tile_rows)
 
 
 def padded_2(shard, sides, width):

time: 107 us -> 101 us (0.944)
  waiting for transfers between devices: 37 us -> 20.3 us
  starting transfers between devices: 27.2 us -> 34.4 us
  Pallas kernels: 40.6 us -> 42.3 us
    ppermute x0 -> x2, waiting for transfers between devices: none -> 12.5 us  [the longest x1 12.5 us: from_others(): outer = lax.ppermute(across, 'row', [(i, i ^ 1) for i, _ in middle])]
    all_to_all x1, waiting for transfers between devices: 14.3 us -> 2.31 us  [local(): lax.all_to_all(product, 'row', 0, 0, tiled=True).reshape(vectors.shape)]
    ppermute x13 -> x14, waiting for transfers between devices: 12.2 us -> 0.63 us  [swap_with(): return lax.ppermute(value, axis, [(i, i ^ distance) for i in range(size)])]
    ppermute x2, waiting for transfers between devices: 10.5 us -> 4.8 us  [local(): halo = (lax.ppermute(last, 'row', up), lax.ppermute(first, 'row', down))]
    all_to_all x1, starting transfers between devices: 3.52 us -> 7.94 us  [local(): lax.all_to_all(product, 'row', 0, 0, tiled=True).reshape(vectors.shape)]
    ppermute x0 -> x2, starting transfers between devices: none -> 1.96 us  [the longest x1 1.29 us: from_others(): outer = lax.ppermute(across, 'row', [(i, i ^ 1) for i, _ in middle])]
    pallas_call x5 -> x6, Pallas kernels: 3.93 us -> 5.73 us  [the longest x1 3.37 us: halve_last(): pl.pallas_call(functools.partial(halve_kernel, tile_rows), out_shape=[sha...]
    unnamed x22 -> x20, local copies, waits for them, and re-layouts: 1.67 us -> 2.67 us
  transfers between devices with their start and end apart: 16 -> 19, of which waited for: 5 -> 5; matrix products, arithmetic and copies ran while one was open for 0% -> 0% of each run, Pallas kernels for 32% -> 36%
where the time goes in v1:
time: 101 us; the launch traced here: 100 us
  Pallas kernels  42.3 us (42%)
  starting transfers between devices  34.4 us (34%)
  waiting for transfers between devices  20.3 us (20%)
  local copies, waits for them, and re-layouts  2.67 us (3%)
    ppermute x14, starting transfers between devices, swap_with(): return lax.ppermute(value, axis, [(i, i ^ distance) for i in range(size)])  18.2 us
    ppermute x1, waiting for transfers between devices, from_others(): outer = lax.ppermute(across, 'row', [(i, i ^ 1) for i, _ in middle])  12.5 us
    pallas_call x2, Pallas kernels, invert_panel(): pl.pallas_call(functools.partial(invert_kernel, panel, owners, shares), o...  11.2 us
    pallas_call x1, Pallas kernels, band_product_split(): pl.pallas_call(band_kernel, out_shape=shaped(owners, rows // owners, colu...  8.04 us
    all_to_all x1, starting transfers between devices, local(): lax.all_to_all(product, 'row', 0, 0, tiled=True).reshape(vectors.shape)  7.94 us
    ppermute x2, starting transfers between devices, local(): halo = (lax.ppermute(last, 'row', up), lax.ppermute(first, 'row', down))  6.24 us
    ppermute x2, waiting for transfers between devices, local(): halo = (lax.ppermute(last, 'row', up), lax.ppermute(first, 'row', down))  4.8 us
    pallas_call x1, Pallas kernels, last_solve(): pl.pallas_call(functools.partial(last_kernel, owners, tile_rows), out_sha...  4.51 us
  transfers between devices with their start and end apart: 19, of which 5 were waited for; matrix products, arithmetic and copies ran while one was open for 0% of the time, Pallas kernels for 36%

profile of v1, /device:TPU:0, one launch (start us, length us, event | category | flops | bytes accessed | tf_op | source)
XLA Modules:
  0.0 100.3 jit_solution(3112290114097483504)
XLA Ops:
  0.0 0.1 pad_add_fusion.place_ref
  0.1 1.8 %first_sends.1 = (f32[2,10,16,256]{3,2,1,0:T(8,128)S(1)}, f32[512,128]{1,0:T(8,128)S(1)}, f32[512,128]{1,0:T(8,128)S(1)}) custom-call(s32[2]{0:T(128)S(1)} %pad_add_fusion.place_ref, f32[2048,2048]{1,0:T(8,128)} %factor_ref.11, f32[2048,128]{1,0:T(8,128)} %vec_ref.3), custom_call_target="tpu_custom_call" | custom-call | bytes 4194304 | tf_op jit(solution)/shard_map/first_sends/pallas_call | solution.py:98
  1.9 4.9 %collective-permute-start = (f32[512,128]{1,0:T(8,128)S(1)}, f32[512,128]{1,0:T(8,128)S(1)}, u32[]{:S(2)}, u32[]{:S(2)}) collective-permute-start(f32[512,128]{1,0:T(8,128)S(1)} %get-tuple-element.26), channel_id=1, source_target_pairs={{0,4},{4,8},{8,12},{1,5},{5,9},{9,13},{2,6},{6,10},{10,14},{3,7},{... | collective-permute-start | bytes 786440 | tf_op jit(solution)/shard_map/ppermute | solution.py:561
  6.8 1.3 %collective-permute-start.1 = (f32[512,128]{1,0:T(8,128)S(1)}, f32[512,128]{1,0:T(8,128)S(1)}, u32[]{:S(2)}, u32[]{:S(2)}) collective-permute-start(f32[512,128]{1,0:T(8,128)S(1)} %get-tuple-element.27), channel_id=1, source_target_pairs={{4,0},{8,4},{12,8},{5,1},{9,5},{13,9},{6,2},{10,6},{14,10},{7,3},{... | collective-permute-start | bytes 786440 | tf_op jit(solution)/shard_map/ppermute | solution.py:561
  8.1 3.7 %collective-permute-start.6 = (f32[2,10,16,256]{3,2,1,0:T(8,128)S(1)}, f32[2,10,16,256]{3,2,1,0:T(8,128)S(1)}, u32[]{:S(2)}, u32[]{:S(2)}) collective-permute-start(f32[2,10,16,256]{3,2,1,0:T(8,128)S(1)} %get-tuple-element.31), channel_id=1, source_target_pairs={{0,8},{4,12},{8,0},{12,4},{1,9},{5,13},{9,1},{13,5},{2,10},{6,14},... | collective-permute-start | bytes 983048 | tf_op jit(solution)/shard_map/ppermute | solution.py:542
  11.8 1.6 %collective-permute-start.5 = (f32[2,10,16,256]{3,2,1,0:T(8,128)S(1)}, f32[2,10,16,256]{3,2,1,0:T(8,128)S(1)}, u32[]{:S(2)}, u32[]{:S(2)}) collective-permute-start(f32[2,10,16,256]{3,2,1,0:T(8,128)S(1)} %get-tuple-element.31), channel_id=1, source_target_pairs={{0,4},{4,0},{8,12},{12,8},{1,5},{5,1},{9,13},{13,9},{2,6},{6,2},{1... | collective-permute-start | bytes 983048 | tf_op jit(solution)/shard_map/ppermute | solution.py:542
  13.4 0.7 collective-permute-start.7
  14.1 0.0 collective-permute-done.before_ref
  14.1 4.8 %collective-permute-done.1.after_ref = f32[512,128]{1,0:T(8,128)S(1)} collective-permute-done((f32[512,128]{1,0:T(8,128)S(1)}, f32[512,128]{1,0:T(8,128)S(1)}, u32[]{:S(2)}, u32[]{:S(2)}) %collective-permute-start.1) | collective-permute-done | bytes 262176 | tf_op jit(solution)/shard_map/ppermute | solution.py:561
  18.9 8.0 %band_product_split.1.after_ref = f32[4,512,128]{2,1,0:T(8,128)} custom-call(f32[2048,1536]{1,0:T(8,128)} %inter_ref.1, f32[2048,128]{1,0:T(8,128)S(1)} %copy-done.1, f32[512,128]{1,0:T(8,128)S(1)} %collective-permute-done.before_ref, f32[512,128]{1,0:T(8,128)S(1)} %collective-permute-done.1.after_ref), custom_call_target="tpu_custom_call" | custom-call | flops 3221225472 | bytes 12582912 | tf_op jit(solution)/shard_map/band_product_split/pallas_call | solution.py:137
  27.0 7.9 %all-to-all-start = ((f32[4,512,128]{2,1,0:T(8,128)}), f32[4,512,128]{2,1,0:T(8,128)S(1)}, u32[]{:S(2)}, u32[]{:S(2)}) async-start(f32[4,512,128]{2,1,0:T(8,128)} %band_product_split.1.after_ref), calls=%async_computation | async-start | bytes 2097152 | tf_op jit(solution)/shard_map/all_to_all | solution.py:563
  34.9 1.0 own_weights.1
  35.9 0.0 collective-permute-done.6.value_ref
  35.9 1.3 %collective-permute-start.8 = (f32[2,10,16,256]{3,2,1,0:T(8,128)S(1)}, f32[2,10,16,256]{3,2,1,0:T(8,128)S(1)}, u32[]{:S(2)}, u32[]{:S(2)}) collective-permute-start(f32[2,10,16,256]{3,2,1,0:T(8,128)S(1)} %pass_on.3.across_ref), channel_id=1, source_target_pairs={{4,0},{8,12},{5,1},{9,13},{6,2},{10,14},{7,3},{11,15},{20,16},{24,... | collective-permute-start | bytes 983048 | tf_op jit(solution)/shard_map/ppermute | solution.py:177
  37.2 0.0 collective-permute-done.5.near_ref
  37.2 0.0 collective-permute-done.7.inner_ref
  37.3 12.5 %collective-permute-done.8.outer_ref = f32[2,10,16,256]{3,2,1,0:T(8,128)S(1)} collective-permute-done((f32[2,10,16,256]{3,2,1,0:T(8,128)S(1)}, f32[2,10,16,256]{3,2,1,0:T(8,128)S(1)}, u32[]{:S(2)}, u32[]{:S(2)}) %collective-permute-start.8) | collective-permute-done | bytes 327712 | tf_op jit(solution)/shard_map/ppermute | solution.py:177
  49.8 1.4 %stack.13 = (f32[3,10,16,256]{3,2,1,0:T(8,128)S(1)}, f32[3,10,16,256]{3,2,1,0:T(8,128)}) custom-call(s32[2]{0:T(128)S(1)} %pad_add_fusion.place_ref, f32[2,10,16,256]{3,2,1,0:T(8,128)S(1)} %collective-permute-done.5.near_ref, f32[2,10,16,256]{3,2,1,0:T(8,128)S(1)} %pass_on.3.across_ref, f32[2,10,16,256]{3,2,1,0:T(8,128)S(1)} %collective-permute-done.7.inner_ref, ...), custom_call_target="tpu_custom_call" | custom-call | tf_op jit(solution)/shard_map/stack/pallas_call | solution.py:200
  51.2 1.5 %collective-permute-start.10 = (f32[3,10,16,256]{3,2,1,0:T(8,128)S(1)}, f32[3,10,16,256]{3,2,1,0:T(8,128)S(1)}, u32[]{:S(2)}, u32[]{:S(2)}) collective-permute-start(f32[3,10,16,256]{3,2,1,0:T(8,128)S(1)} %get-tuple-element.32.refs_0_), channel_id=1, source_target_pairs={{0,2},{1,3},{2,0},{3,1},{4,6},{5,7},{6,4},{7,5},{8,10},{9,11},{10,... | collective-permute-start | bytes 1474568 | tf_op jit(solution)/shard_map/ppermute | solution.py:542
  52.7 3.4 %halve_last.1 = (bf16[3,2,512,1024]{3,2,1,0:T(8,128)(2,1)S(1)}, f32[8,128]{1,0:T(8,128)S(1)}) custom-call(f32[2048,2048]{1,0:T(8,128)} %factor_ref.11, f32[256,128]{1,0:T(8,128)S(1)} %get-tuple-element.28.after_ref.refs_9_), custom_call_target="tpu_custom_call" | custom-call | flops 1073741824 | bytes 12582912 | tf_op jit(solution)/shard_map/halve_last/pallas_call | solution.py:432
  56.1 2.6 %copy-done = bf16[3,2,512,1024]{3,2,1,0:T(8,128)(2,1)} copy-done((bf16[3,2,512,1024]{3,2,1,0:T(8,128)(2,1)}, bf16[3,2,512,1024]{3,2,1,0:T(8,128)(2,1)S(1)}, u32[]{:S(2)}) %copy-start) | copy-done | bytes 6291480
  58.7 0.0 collective-permute-start.9
  58.7 2.3 %all-to-all-done = f32[4,512,128]{2,1,0:T(8,128)S(1)} async-done(((f32[4,512,128]{2,1,0:T(8,128)}), f32[4,512,128]{2,1,0:T(8,128)S(1)}, u32[]{:S(2)}, u32[]{:S(2)}) %all-to-all-start) | async-done | bytes 1048608 | tf_op jit(solution)/shard_map/all_to_all | solution.py:563
  61.0 0.9 order_rows.2.after_ref.refs_0_
  62.0 0.0 collective-permute-done.10.value_ref
  62.0 0.1 collective-permute-start.11
  62.1 1.6 %collective-permute-start.16 = (f32[3,10,16,256]{3,2,1,0:T(8,128)}, f32[3,10,16,256]{3,2,1,0:T(8,128)S(1)}, u32[]{:S(2)}, u32[]{:S(2)}) collective-permute-start(f32[3,10,16,256]{3,2,1,0:T(8,128)} %get-tuple-element.40.refs_0_), channel_id=1, source_target_pairs={{0,2},{1,3},{2,0},{3,1},{4,6},{5,7},{6,4},{7,5},{8,10},{9,11},{10,... | collective-permute-start | bytes 1474568 | tf_op jit(solution)/shard_map/ppermute | solution.py:542
  63.6 0.2 collective-permute-start.15
  63.8 0.0 collective-permute-start.2
  63.8 0.0 collective-permute-done.9.refs_1_
  63.8 0.0 collective-permute-start.3
  63.8 0.1 collective-permute-done.11.refs_3_
  63.9 4.3 %collective-permute-start.4 = (f32[256,128]{1,0:T(8,128)S(1)}, f32[256,128]{1,0:T(8,128)S(1)}, u32[]{:S(2)}, u32[]{:S(2)}) collective-permute-start(f32[256,128]{1,0:T(8,128)S(1)} %order_rows.2.after_ref.refs_0_), channel_id=1, source_target_pairs={{0,12},{4,8},{8,4},{12,0},{1,13},{5,9},{9,5},{13,1},{2,14},{6,10},... | collective-permute-start | bytes 393224 | tf_op jit(solution)/shard_map/ppermute | solution.py:542
  68.2 5.3 %invert_panel.2 = (bf16[1024,1024]{1,0:T(8,128)(2,1)S(1)}, bf16[1024,1024]{1,0:T(8,128)(2,1)S(1)}, bf16[4,256,256]{2,1,0:T(8,128)(2,1)S(1)}, bf16[4,256,256]{2,1,0:T(8,128)(2,1)S(1)}) custom-call(s32[2]{0:T(128)S(1)} %pad_add_fusion.place_ref, f32[256,128]{1,0:T(8,128)S(1)} %order_rows.2.after_ref.refs_0_, f32[2048,2048]{1,0:T(8,128)} %factor_ref.11, ...), custom_call_target="tpu_custom_call" | custom-call | flops 137438953472 | bytes 12582912 | tf_op jit(solution)/shard_map/invert_panel/pallas_call | solution.py:278
  73.4 2.6 %order_rows.3 = (f32[256,128]{1,0:T(8,128)S(1)}, f32[1536,128]{1,0:T(8,128)S(1)}) custom-call(s32[2048]{0:T(1024)S(1)} %copy-done.4, f32[2048,128]{1,0:T(8,128)S(1)} %bitcast.6, bf16[4,256,256]{2,1,0:T(8,128)(2,1)S(1)} %get-tuple-element.35.after_ref.refs_6_), custom_call_target="tpu_custom_call" | custom-call | bytes 2097152 | tf_op jit(solution)/shard_map/order_rows/pallas_call | solution.py:313
  76.1 0.0 collective-permute-done.16.value_ref
  76.1 0.1 collective-permute-start.17
  76.2 0.0 collective-permute-done.2.refs_1_
  76.2 0.5 collective-permute-done.3.refs_2_
  76.7 3.5 %first_solve.1 = (f32[64,16,128]{2,1,0:T(8,128)S(1)}, f32[256,128]{1,0:T(8,128)S(1)}) custom-call(s32[2]{0:T(128)S(1)} %pad_add_fusion.place_ref, f32[2048,2048]{1,0:T(8,128)} %factor_ref.11, f32[256,128]{1,0:T(8,128)S(1)} %order_rows.2.after_ref.refs_0_, f32[256,128]{1,0:T(8,128)S(1)} %collective-permute-done.2.refs_1_, ...), custom_call_target="tpu_custom_call" | custom-call | flops 137438953472 | bytes 6291456 | tf_op jit(solution)/shard_map/first_solve/pallas_call | solution.py:357
  80.2 2.9 %collective-permute-start.12 = (f32[256,128]{1,0:T(8,128)S(1)}, f32[256,128]{1,0:T(8,128)S(1)}, u32[]{:S(2)}, u32[]{:S(2)}) collective-permute-start(f32[256,128]{1,0:T(8,128)S(1)} %get-tuple-element.38.refs_0_), channel_id=1, source_target_pairs={{0,4},{4,0},{8,12},{12,8},{1,5},{5,1},{9,13},{13,9},{2,6},{6,2},{1... | collective-permute-start | bytes 393224 | tf_op jit(solution)/shard_map/ppermute | solution.py:542
  83.1 0.0 collective-permute-start.13
  83.1 2.4 %collective-permute-start.14 = (f32[256,128]{1,0:T(8,128)S(1)}, f32[256,128]{1,0:T(8,128)S(1)}, u32[]{:S(2)}, u32[]{:S(2)}) collective-permute-start(f32[256,128]{1,0:T(8,128)S(1)} %get-tuple-element.38.refs_0_), channel_id=1, source_target_pairs={{0,12},{4,8},{8,4},{12,0},{1,13},{5,9},{9,5},{13,1},{2,14},{6,10},... | collective-permute-start | bytes 393224 | tf_op jit(solution)/shard_map/ppermute | solution.py:542
  85.5 3.9 %middle_update.1.refs_11_ = f32[1536,128]{1,0:T(8,128)S(1)} custom-call(f32[2048,2048]{1,0:T(8,128)} %factor_ref.11, f32[1536,128]{1,0:T(8,128)S(1)} %get-tuple-element.46.rest_ref, f32[64,16,128]{2,1,0:T(8,128)S(1)} %get-tuple-element.39.after_ref.y_ref.refs_8_), custom_call_target="tpu_custom_call" | custom-call | flops 1610612736 | bytes 8388608 | tf_op jit(solution)/shard_map/middle_update/pallas_call | solution.py:466
  89.5 0.0 slice-start.1
  89.5 6.0 %invert_panel.3 = (bf16[1024,1024]{1,0:T(8,128)(2,1)S(1)}, bf16[1024,1024]{1,0:T(8,128)(2,1)S(1)}, bf16[4,256,256]{2,1,0:T(8,128)(2,1)S(1)}, bf16[4,256,256]{2,1,0:T(8,128)(2,1)S(1)}) custom-call(s32[2]{0:T(128)S(1)} %pad_add_fusion.place_ref, f32[64,16,128]{2,1,0:T(8,128)S(1)} %get-tuple-element.39.after_ref.y_ref.refs_8_, f32[2048,2048]{1,0:T(8,128)} %factor_ref.11, ...), custom_call_target="tpu_custom_call" | custom-call | flops 1073741824 | bytes 12582912 | tf_op jit(solution)/shard_map/invert_panel/pallas_call | solution.py:278
  95.5 0.0 collective-permute-done.12.refs_1_
  95.6 4.5 %last_solve.1 = f32[2048,128]{1,0:T(8,128)} custom-call(s32[2]{0:T(128)S(1)} %pad_add_fusion.place_ref, bf16[3,2,512,1024]{3,2,1,0:T(8,128)(2,1)S(1)} %bitcast.8, f32[256,128]{1,0:T(8,128)S(1)} %get-tuple-element.38.refs_0_, f32[256,128]{1,0:T(8,128)S(1)} %collective-permute-done.12.refs_1_, f32[256,128]{1,0:T(8,128)S(1)} %collective-permute-done.13.refs_2_, ...), custom_call_target="tpu_custom_call" | custom-call | flops 2147483648 | bytes 12582912 | tf_op jit(solution)/shard_map/last_solve/pallas_call | solution.py:522
  (28 shorter events, 0.1 us)
Async XLA Ops:
  0.1 14.0 %copy-start.7 = (f32[2048]{0:T(1024)S(1)}, f32[2048]{0:T(1024)}, u32[]{:S(2)}) copy-start(f32[2048]{0:T(1024)} %param.12) | copy-start | bytes 24580
  0.1 18.9 %copy-start.1 = (f32[2048,128]{1,0:T(8,128)S(1)}, f32[2048,128]{1,0:T(8,128)}, u32[]{:S(2)}) copy-start(f32[2048,128]{1,0:T(8,128)} %vec_ref.3) | copy-start | bytes 3145732
  1.9 12.3 %collective-permute-start = (f32[512,128]{1,0:T(8,128)S(1)}, f32[512,128]{1,0:T(8,128)S(1)}, u32[]{:S(2)}, u32[]{:S(2)}) collective-permute-start(f32[512,128]{1,0:T(8,128)S(1)} %get-tuple-element.26), channel_id=1, source_target_pairs={{0,4},{4,8},{8,12},{1,5},{5,9},{9,13},{2,6},{6,10},{10,14},{3,7},{... | collective-permute-start | bytes 786440 | tf_op jit(solution)/shard_map/ppermute | solution.py:561
  6.8 12.1 %collective-permute-start.1 = (f32[512,128]{1,0:T(8,128)S(1)}, f32[512,128]{1,0:T(8,128)S(1)}, u32[]{:S(2)}, u32[]{:S(2)}) collective-permute-start(f32[512,128]{1,0:T(8,128)S(1)} %get-tuple-element.27), channel_id=1, source_target_pairs={{4,0},{8,4},{12,8},{5,1},{9,5},{13,9},{6,2},{10,6},{14,10},{7,3},{... | collective-permute-start | bytes 786440 | tf_op jit(solution)/shard_map/ppermute | solution.py:561
  8.1 27.8 %collective-permute-start.6 = (f32[2,10,16,256]{3,2,1,0:T(8,128)S(1)}, f32[2,10,16,256]{3,2,1,0:T(8,128)S(1)}, u32[]{:S(2)}, u32[]{:S(2)}) collective-permute-start(f32[2,10,16,256]{3,2,1,0:T(8,128)S(1)} %get-tuple-element.31), channel_id=1, source_target_pairs={{0,8},{4,12},{8,0},{12,4},{1,9},{5,13},{9,1},{13,5},{2,10},{6,14},... | collective-permute-start | bytes 983048 | tf_op jit(solution)/shard_map/ppermute | solution.py:542
  11.8 25.4 %collective-permute-start.5 = (f32[2,10,16,256]{3,2,1,0:T(8,128)S(1)}, f32[2,10,16,256]{3,2,1,0:T(8,128)S(1)}, u32[]{:S(2)}, u32[]{:S(2)}) collective-permute-start(f32[2,10,16,256]{3,2,1,0:T(8,128)S(1)} %get-tuple-element.31), channel_id=1, source_target_pairs={{0,4},{4,0},{8,12},{12,8},{1,5},{5,1},{9,13},{13,9},{2,6},{6,2},{1... | collective-permute-start | bytes 983048 | tf_op jit(solution)/shard_map/ppermute | solution.py:542
  13.4 23.8 %collective-permute-start.7 = (f32[2,10,16,256]{3,2,1,0:T(8,128)S(1)}, f32[2,10,16,256]{3,2,1,0:T(8,128)S(1)}, u32[]{:S(2)}, u32[]{:S(2)}) collective-permute-start(f32[2,10,16,256]{3,2,1,0:T(8,128)S(1)} %get-tuple-element.31), channel_id=1, source_target_pairs={{4,8},{8,4},{5,9},{9,5},{6,10},{10,6},{7,11},{11,7},{20,24},{24,20... | collective-permute-start | bytes 983048 | tf_op jit(solution)/shard_map/ppermute | solution.py:176
  27.0 7.9 %copy-start.5 = (s32[1024]{0:T(1024)S(1)}, s32[1024]{0:T(1024)}, u32[]{:S(2)}) copy-start(s32[1024]{0:T(1024)} %param.11) | copy-start | bytes 12292
  27.0 7.9 %copy-start.6 = (f32[1024]{0:T(1024)S(1)}, f32[1024]{0:T(1024)}, u32[]{:S(2)}) copy-start(f32[1024]{0:T(1024)} %param.13) | copy-start | bytes 12292
  27.0 34.0 %all-to-all-start = ((f32[4,512,128]{2,1,0:T(8,128)}), f32[4,512,128]{2,1,0:T(8,128)S(1)}, u32[]{:S(2)}, u32[]{:S(2)}) async-start(f32[4,512,128]{2,1,0:T(8,128)} %band_product_split.1.after_ref), calls=%async_computation | async-start | bytes 2097152 | tf_op jit(solution)/shard_map/all_to_all | solution.py:563
  35.9 20.2 %copy-start.2 = (f32[256,128]{1,0:T(8,128)}, f32[256,128]{1,0:T(8,128)S(1)}, u32[]{:S(2)}) copy-start(f32[256,128]{1,0:T(8,128)S(1)} %get-tuple-element.28.after_ref.refs_9_) | copy-start | bytes 393220
  35.9 13.9 %collective-permute-start.8 = (f32[2,10,16,256]{3,2,1,0:T(8,128)S(1)}, f32[2,10,16,256]{3,2,1,0:T(8,128)S(1)}, u32[]{:S(2)}, u32[]{:S(2)}) collective-permute-start(f32[2,10,16,256]{3,2,1,0:T(8,128)S(1)} %pass_on.3.across_ref), channel_id=1, source_target_pairs={{4,0},{8,12},{5,1},{9,13},{6,2},{10,14},{7,3},{11,15},{20,16},{24,... | collective-permute-start | bytes 983048 | tf_op jit(solution)/shard_map/ppermute | solution.py:177
  51.2 9.8 %copy-start.4 = (s32[2048]{0:T(1024)S(1)}, s32[2048]{0:T(1024)}, u32[]{:S(2)}) copy-start(s32[2048]{0:T(1024)} %pivot_ref.3) | copy-start | bytes 24580
  51.2 10.8 %collective-permute-start.10 = (f32[3,10,16,256]{3,2,1,0:T(8,128)S(1)}, f32[3,10,16,256]{3,2,1,0:T(8,128)S(1)}, u32[]{:S(2)}, u32[]{:S(2)}) collective-permute-start(f32[3,10,16,256]{3,2,1,0:T(8,128)S(1)} %get-tuple-element.32.refs_0_), channel_id=1, source_target_pairs={{0,2},{1,3},{2,0},{3,1},{4,6},{5,7},{6,4},{7,5},{8,10},{9,11},{10,... | collective-permute-start | bytes 1474568 | tf_op jit(solution)/shard_map/ppermute | solution.py:542
  56.1 2.6 %copy-start = (bf16[3,2,512,1024]{3,2,1,0:T(8,128)(2,1)}, bf16[3,2,512,1024]{3,2,1,0:T(8,128)(2,1)S(1)}, u32[]{:S(2)}) copy-start(bf16[3,2,512,1024]{3,2,1,0:T(8,128)(2,1)S(1)} %get-tuple-element.29.left_ref) | copy-start | bytes 18874372
  58.7 5.1 %collective-permute-start.9 = (f32[3,10,16,256]{3,2,1,0:T(8,128)S(1)}, f32[3,10,16,256]{3,2,1,0:T(8,128)S(1)}, u32[]{:S(2)}, u32[]{:S(2)}) collective-permute-start(f32[3,10,16,256]{3,2,1,0:T(8,128)S(1)} %get-tuple-element.32.refs_0_), channel_id=1, source_target_pairs={{0,1},{1,0},{2,3},{3,2},{4,5},{5,4},{6,7},{7,6},{8,9},{9,8},{10,11... | collective-permute-start | bytes 1474568 | tf_op jit(solution)/shard_map/ppermute | solution.py:542
  62.0 1.9 %collective-permute-start.11 = (f32[3,10,16,256]{3,2,1,0:T(8,128)S(1)}, f32[3,10,16,256]{3,2,1,0:T(8,128)S(1)}, u32[]{:S(2)}, u32[]{:S(2)}) collective-permute-start(f32[3,10,16,256]{3,2,1,0:T(8,128)S(1)} %pass_on.4.refs_2_), channel_id=1, source_target_pairs={{0,1},{1,0},{2,3},{3,2},{4,5},{5,4},{6,7},{7,6},{8,9},{9,8},{10,11... | collective-permute-start | bytes 1474568 | tf_op jit(solution)/shard_map/ppermute | solution.py:542
  62.1 14.0 %collective-permute-start.16 = (f32[3,10,16,256]{3,2,1,0:T(8,128)}, f32[3,10,16,256]{3,2,1,0:T(8,128)S(1)}, u32[]{:S(2)}, u32[]{:S(2)}) collective-permute-start(f32[3,10,16,256]{3,2,1,0:T(8,128)} %get-tuple-element.40.refs_0_), channel_id=1, source_target_pairs={{0,2},{1,3},{2,0},{3,1},{4,6},{5,7},{6,4},{7,5},{8,10},{9,11},{10,... | collective-permute-start | bytes 1474568 | tf_op jit(solution)/shard_map/ppermute | solution.py:542
  63.6 25.9 %collective-permute-start.15 = (f32[3,10,16,256]{3,2,1,0:T(8,128)}, f32[3,10,16,256]{3,2,1,0:T(8,128)}, u32[]{:S(2)}, u32[]{:S(2)}) collective-permute-start(f32[3,10,16,256]{3,2,1,0:T(8,128)} %get-tuple-element.40.refs_0_), channel_id=1, source_target_pairs={{0,1},{1,0},{2,3},{3,2},{4,5},{5,4},{6,7},{7,6},{8,9},{9,8},{10,11... | collective-permute-start | bytes 1474568 | tf_op jit(solution)/shard_map/ppermute | solution.py:542
  63.8 12.4 %collective-permute-start.2 = (f32[256,128]{1,0:T(8,128)S(1)}, f32[256,128]{1,0:T(8,128)S(1)}, u32[]{:S(2)}, u32[]{:S(2)}) collective-permute-start(f32[256,128]{1,0:T(8,128)S(1)} %order_rows.2.after_ref.refs_0_), channel_id=1, source_target_pairs={{0,4},{4,0},{8,12},{12,8},{1,5},{5,1},{9,13},{13,9},{2,6},{6,2},{1... | collective-permute-start | bytes 393224 | tf_op jit(solution)/shard_map/ppermute | solution.py:542
  63.8 12.9 %collective-permute-start.3 = (f32[256,128]{1,0:T(8,128)S(1)}, f32[256,128]{1,0:T(8,128)S(1)}, u32[]{:S(2)}, u32[]{:S(2)}) collective-permute-start(f32[256,128]{1,0:T(8,128)S(1)} %order_rows.2.after_ref.refs_0_), channel_id=1, source_target_pairs={{0,8},{4,12},{8,0},{12,4},{1,9},{5,13},{9,1},{13,5},{2,10},{6,14},... | collective-permute-start | bytes 393224 | tf_op jit(solution)/shard_map/ppermute | solution.py:542
  63.9 12.8 %collective-permute-start.4 = (f32[256,128]{1,0:T(8,128)S(1)}, f32[256,128]{1,0:T(8,128)S(1)}, u32[]{:S(2)}, u32[]{:S(2)}) collective-permute-start(f32[256,128]{1,0:T(8,128)S(1)} %order_rows.2.after_ref.refs_0_), channel_id=1, source_target_pairs={{0,12},{4,8},{8,4},{12,0},{1,13},{5,9},{9,5},{13,1},{2,14},{6,10},... | collective-permute-start | bytes 393224 | tf_op jit(solution)/shard_map/ppermute | solution.py:542
  76.1 13.4 %collective-permute-start.17 = (f32[3,10,16,256]{3,2,1,0:T(8,128)S(1)}, f32[3,10,16,256]{3,2,1,0:T(8,128)S(1)}, u32[]{:S(2)}, u32[]{:S(2)}) collective-permute-start(f32[3,10,16,256]{3,2,1,0:T(8,128)S(1)} %pass_on.5.refs_2_), channel_id=1, source_target_pairs={{0,1},{1,0},{2,3},{3,2},{4,5},{5,4},{6,7},{7,6},{8,9},{9,8},{10,11... | collective-permute-start | bytes 1474568 | tf_op jit(solution)/shard_map/ppermute | solution.py:542
  80.2 15.3 %collective-permute-start.12 = (f32[256,128]{1,0:T(8,128)S(1)}, f32[256,128]{1,0:T(8,128)S(1)}, u32[]{:S(2)}, u32[]{:S(2)}) collective-permute-start(f32[256,128]{1,0:T(8,128)S(1)} %get-tuple-element.38.refs_0_), channel_id=1, source_target_pairs={{0,4},{4,0},{8,12},{12,8},{1,5},{5,1},{9,13},{13,9},{2,6},{6,2},{1... | collective-permute-start | bytes 393224 | tf_op jit(solution)/shard_map/ppermute | solution.py:542
  83.1 12.4 %collective-permute-start.13 = (f32[256,128]{1,0:T(8,128)S(1)}, f32[256,128]{1,0:T(8,128)S(1)}, u32[]{:S(2)}, u32[]{:S(2)}) collective-permute-start(f32[256,128]{1,0:T(8,128)S(1)} %get-tuple-element.38.refs_0_), channel_id=1, source_target_pairs={{0,8},{4,12},{8,0},{12,4},{1,9},{5,13},{9,1},{13,5},{2,10},{6,14},... | collective-permute-start | bytes 393224 | tf_op jit(solution)/shard_map/ppermute | solution.py:542
  83.1 12.4 %collective-permute-start.14 = (f32[256,128]{1,0:T(8,128)S(1)}, f32[256,128]{1,0:T(8,128)S(1)}, u32[]{:S(2)}, u32[]{:S(2)}) collective-permute-start(f32[256,128]{1,0:T(8,128)S(1)} %get-tuple-element.38.refs_0_), channel_id=1, source_target_pairs={{0,12},{4,8},{8,4},{12,0},{1,13},{5,9},{9,5},{13,1},{2,14},{6,10},... | collective-permute-start | bytes 393224 | tf_op jit(solution)/shard_map/ppermute | solution.py:542
  85.5 10.0 %slice-start = ((s8[6291456]{0:T(1024)(128)(4,1)}), s8[4194304]{0:T(1024)(128)(4,1)S(1)}, s32[]{:S(2)}) async-start(s8[6291456]{0:T(1024)(128)(4,1)} %bitcast.7), calls=%async_computation.1 | async-start | bytes 8388608
  89.5 6.1 %slice-start.1 = ((s8[6291456]{0:T(1024)(128)(4,1)}), s8[2097152]{0:T(1024)(128)(4,1)S(1)}, s32[]{:S(2)}) async-start(s8[6291456]{0:T(1024)(128)(4,1)} %bitcast.7), calls=%async_computation.2 | async-start | bytes 4194304
  89.5 6.1 %copy-start.3 = (f32[256,128]{1,0:T(8,128)S(1)}, f32[256,128]{1,0:T(8,128)}, u32[]{:S(2)}) copy-start(f32[256,128]{1,0:T(8,128)} %copy-done.2) | copy-start | bytes 393220

commit v2 on v1

--- a/solution.py
+++ b/solution.py
@@ -70,20 +70,35 @@
     return fold(dot(left_wide, jnp.concatenate([wide, wide], axis=0)))
 
 
-def start_kernel(slots, shares, place_ref, factor_ref, vec_ref, *refs):
-    share_ref, first_ref, last_ref, sems = refs
-    groups = PANEL // DIAG
+def fold_back(run, part, shares):
+    return part if run % 2 == 0 else shares - 1 - part
+
+
+def lower_run(pair, part, shares):
+    early = part < shares // 2
+    return 2 * pair + jnp.where(early, 1, 0), jnp.where(early, shares - 1 - part, part)
+
+
+def start_kernel(slots, shares, place_ref, factor_ref, vec_ref, share_ref, first_ref, last_ref, sems):
     part = place_ref[1]
     rows = vec_ref.shape[0]
     copies = [(vec_ref.at[pl.ds(rows - BS, BS)], last_ref), (vec_ref.at[pl.ds(0, BS)], first_ref)]
+    runs = PANEL // DIAG
+
+    def source(panel, run, block, column, width):
+        row = pl.multiple_of((panel * slots + run * shares + block) * CYC, CYC)
+        column = pl.multiple_of(panel * PANEL + column, HALF)
+        return factor_ref.at[pl.ds(row, CYC), pl.ds(column, width)]
+
     for panel in range(PANELS):
-        at = 0
-        for k in range(groups):
-            row = pl.multiple_of((panel * slots + k * shares + part) * CYC, CYC)
-            for j in range(k + 1):
-                source = factor_ref.at[pl.ds(row, CYC), pl.ds(panel * PANEL + j * DIAG, DIAG)]
-                copies.append((source, share_ref.at[panel, at]))
-                at += 1
+        for run in range(runs):
+            width = (2 * run + 1) * HALF
+            target = share_ref.at[panel, :, pl.ds(run * run * HALF, width)]
+            copies.append((source(panel, run, fold_back(run, part, shares), 0, width), target))
+        for pair in range(runs // 2):
+            run, block = lower_run(pair, part, shares)
+            target = share_ref.at[panel, :, pl.ds((runs * runs + pair) * HALF, HALF)]
+            copies.append((source(panel, run, block, (2 * run + 1) * HALF, HALF), target))
     started = [pltpu.make_async_copy(a, b, sems.at[i]) for i, (a, b) in enumerate(copies)]
     for copy in started:
         copy.start()
@@ -92,15 +107,14 @@
 
 
 def first_sends(place, factor, vectors, slots, shares):
-    groups = PANEL // DIAG
-    blocks = groups * (groups + 1) // 2
+    runs = PANEL // DIAG
     edge = shaped(BS, vectors.shape[1])
     return pl.pallas_call(
         functools.partial(start_kernel, slots, shares),
-        out_shape=[shaped(PANELS, blocks, CYC, DIAG), edge, edge],
+        out_shape=[shaped(PANELS, CYC, (runs * runs + runs // 2) * HALF), edge, edge],
         in_specs=[IN_SMEM, IN_HBM, IN_HBM],
         out_specs=[IN_VMEM] * 3,
-        scratch_shapes=[pltpu.SemaphoreType.DMA((PANELS * blocks + 2,))],
+        scratch_shapes=[pltpu.SemaphoreType.DMA((PANELS * (runs + runs // 2) + 2,))],
         compiler_params=params(4),
         cost_estimate=cost(0, 4 * MIB),
         name="first_sends",
@@ -207,41 +221,44 @@
     )(place, *pieces, after)
 
 
-def invert_kernel(panel, owners, shares, place_ref, after_ref, factor_ref, *refs):
+def invert_kernel(panel, owners, shares, place_ref, after_ref, own_ref, *refs):
     pieces = refs[:shares]
-    high_ref, low_ref, inv_high_ref, inv_low_ref, own_ref, tri_ref, sem = refs[-7:]
-    groups = PANEL // DIAG
+    high_ref, low_ref, inv_high_ref, inv_low_ref, near_ref = refs[shares:]
+    runs = PANEL // DIAG
     me, part = place_ref[0], place_ref[1]
-    rows = own_ref.shape[0]
-    copy = pltpu.make_async_copy(
-        factor_ref.at[pl.ds(panel * rows, rows), pl.ds(panel * PANEL, PANEL)], own_ref, sem
-    )
-    copy.start()
+
+    def place_left(run, row_block, values):
+        if run:
+            rows = pl.ds(pl.multiple_of(row_block * CYC, CYC), CYC)
+            high_ref[rows, : run * DIAG], low_ref[rows, : run * DIAG] = split(values)
+
+    for run in range(runs):
+        for s in range(shares):
+            row_block = (run * shares + s) * owners + me
+            rows = slice((run * shares + s) * CYC, (run * shares + s + 1) * CYC)
+            place_left(run, row_block, own_ref[panel, rows, : run * DIAG])
+            near_ref[row_block] = own_ref[panel, rows, run * DIAG : (run + 1) * DIAG]
     for other in range(1, owners):
         owner = me ^ other
         for turn in range(shares):
-            at = 0
-            for k in range(groups):
-                for j in range(k + 1):
-                    piece = pieces[turn][other - 1, at]
-                    to = (k * shares + (part ^ turn)) * owners + owner
-                    tri_ref[to, :, j * DIAG : (j + 1) * DIAG] = piece
-                    at += 1
-    copy.wait()
-    for k in range(groups):
-        reach = (k + 1) * DIAG
-        for s in range(shares):
-            row = (k * shares + s) * CYC
-            tri_ref[(k * shares + s) * owners + me, :, :reach] = own_ref[row : row + CYC, :reach]
-
-    def block(row, column, size):
-        part_rows = tri_ref[row // CYC : (row + size) // CYC, :, column : column + size]
-        return part_rows.reshape(size, size)
-
-    for k in range(1, groups):
-        rows = slice(k * DIAG, (k + 1) * DIAG)
-        left = tri_ref[rows.start // CYC : rows.stop // CYC, :, : k * DIAG].reshape(DIAG, k * DIAG)
-        high_ref[rows, : k * DIAG], low_ref[rows, : k * DIAG] = split(left)
+            piece = pieces[turn]
+            sender = part ^ turn
+            for run in range(runs):
+                row_block = (run * shares + fold_back(run, sender, shares)) * owners + owner
+                first = run * run * HALF
+                middle = first + run * DIAG
+                place_left(run, row_block, piece[other - 1, :, first:middle])
+                near_ref[row_block, :, :HALF] = piece[other - 1, :, middle : middle + HALF]
+            for pair in range(runs // 2):
+                run, block = lower_run(pair, sender, shares)
+                first = (runs * runs + pair) * HALF
+                near_ref[(run * shares + block) * owners + owner, :, HALF:] = piece[
+                    other - 1, :, first : first + HALF
+                ]
+
+    def near(i, side):
+        blocks = HALF // CYC
+        return near_ref[i * blocks : (i + 1) * blocks, :, side * HALF : (side + 1) * HALF].reshape(HALF, HALF)
 
     down = lax.broadcasted_iota(jnp.int32, (HALF, HALF), 0)
     along = lax.broadcasted_iota(jnp.int32, (HALF, HALF), 1)
@@ -251,7 +268,7 @@
         return (down // size == along // size + 1) & ((down // size) % 2 == 1)
 
     count = PANEL // HALF
-    diagonal = [block(i * HALF, i * HALF, HALF) for i in range(count)]
+    diagonal = [near(i, i % 2) for i in range(count)]
     wides = [side_by_side(d) for d in diagonal]
     inverse = [eye - jnp.where(below(1), d, 0.0) for d in diagonal]
     size = 2
@@ -261,34 +278,32 @@
         right = [small_times(wides[i] * keep, inverse[i]) for i in range(count)]
         inverse = [inverse[i] - small_times(side_by_side(inverse[i]), right[i]) for i in range(count)]
         size *= 2
-    for k in range(groups):
-        first, second = inverse[2 * k], inverse[2 * k + 1]
-        corner = block(k * DIAG + HALF, k * DIAG, HALF)
-        right = small_times(side_by_side(corner), first)
+    for run in range(runs):
+        first, second = inverse[2 * run], inverse[2 * run + 1]
+        right = small_times(side_by_side(near(2 * run + 1, 0)), first)
         corner = -small_times(side_by_side(second), right)
-        empty = jnp.zeros((HALF, HALF), F32)
-        whole = jnp.concatenate(
-            [jnp.concatenate([first, empty], axis=1), jnp.concatenate([corner, second], axis=1)], axis=0
-        )
-        inv_high_ref[k], inv_low_ref[k] = split(whole)
-
-
-def invert_panel(panel, place, factor, pieces, owners, shares, panel_rows, after, flops):
+        inv_high_ref[run, :HALF, :HALF], inv_low_ref[run, :HALF, :HALF] = split(first)
+        inv_high_ref[run, HALF:, HALF:], inv_low_ref[run, HALF:, HALF:] = split(second)
+        inv_high_ref[run, HALF:, :HALF], inv_low_ref[run, HALF:, :HALF] = split(corner)
+        empty = jnp.zeros((HALF, HALF), BF16)
+        inv_high_ref[run, :HALF, HALF:] = empty
+        inv_low_ref[run, :HALF, HALF:] = empty
+
+
+def invert_panel(panel, place, own, pieces, owners, shares, after, flops):
     groups = PANEL // DIAG
     return pl.pallas_call(
         functools.partial(invert_kernel, panel, owners, shares),
         out_shape=[shaped(PANEL, PANEL, dtype=BF16)] * 2 + [shaped(groups, DIAG, DIAG, dtype=BF16)] * 2,
-        in_specs=[IN_SMEM, pl.BlockSpec(memory_space=pl.ANY), IN_HBM] + [IN_VMEM] * len(pieces),
+        in_specs=[IN_SMEM, pl.BlockSpec(memory_space=pl.ANY)] + [IN_VMEM] * (len(pieces) + 1),
         out_specs=[IN_VMEM] * 4,
         scratch_shapes=[
-            pltpu.VMEM((panel_rows, PANEL), F32),
-            pltpu.VMEM((PANEL // CYC, CYC, PANEL), F32),
-            pltpu.SemaphoreType.DMA,
+            pltpu.VMEM((PANEL // CYC, CYC, DIAG), F32),
         ],
         compiler_params=params(16),
         cost_estimate=cost(flops, 12 * MIB),
         name="invert_panel",
-    )(place, after, factor, *pieces)
+    )(place, after, own, *pieces)
 
 
 def order_kernel(first, pivot_ref, grouped_ref, after_ref, *out_refs):
@@ -321,54 +336,57 @@
     )(pivot_rows, grouped, after)
 
 
-def solve_into(me, owners, pieces, high_ref, low_ref, inv_high_ref, inv_low_ref, rhs_ref, wide_ref, y_ref):
+def solve_into(me, owners, pieces, high_ref, low_ref, inv_high_ref, inv_low_ref, rhs_ref, y_ref, use):
     slots = pieces[0].shape[0] // CYC
     columns = pieces[0].shape[1]
     for k in range(owners):
         for s in range(slots):
             rhs_ref[s * owners + (me ^ k)] = pieces[k][s * CYC : (s + 1) * CYC]
-    for k in range(PANEL // DIAG):
-        rows = slice(k * DIAG, (k + 1) * DIAG)
-        rhs = rhs_ref[rows.start // CYC : rows.stop // CYC].reshape(DIAG, columns)
+    runs = [slice(k * DIAG, (k + 1) * DIAG) for k in range(PANEL // DIAG)]
+    rhs = [rhs_ref[r.start // CYC : r.stop // CYC].reshape(DIAG, columns) for r in runs]
+
+    def take_off(row, k, wide):
+        rhs[row] = rhs[row] - parts_times(high_ref[runs[row], runs[k]], low_ref[runs[row], runs[k]], wide)
+
+    wide = None
+    for k in range(len(runs)):
+        block = parts_times(inv_high_ref[k], inv_low_ref[k], side_by_side(rhs[k]))
         if k:
-            done = wide_ref[: k * DIAG]
-            rhs = rhs - parts_times(high_ref[rows, : k * DIAG], low_ref[rows, : k * DIAG], done)
-        wide = side_by_side(rhs)
-        block = parts_times(inv_high_ref[k], inv_low_ref[k], wide)
-        wide_ref[rows] = side_by_side(block)
-        y_ref[rows.start // CYC : rows.stop // CYC] = block.reshape(DIAG // CYC, CYC, columns)
-
-
-def first_kernel(owners, place_ref, factor_ref, *refs):
+            for row in range(k + 1, len(runs)):
+                take_off(row, k - 1, wide)
+            use(k - 1, wide)
+        wide = side_by_side(block)
+        if k + 1 < len(runs):
+            take_off(k + 1, k, wide)
+        y_ref[runs[k].start // CYC : runs[k].stop // CYC] = block.reshape(DIAG // CYC, CYC, columns)
+    use(len(runs) - 1, wide)
+
+
+def first_kernel(owners, place_ref, *refs):
     pieces = refs[:owners]
-    high, low, inv_high, inv_low, current_ref = refs[owners : owners + 5]
-    y_ref, next_ref, rhs_ref, wide_ref, left_ref, sem = refs[owners + 5 :]
-    rows = left_ref.shape[0]
-    copy = pltpu.make_async_copy(factor_ref.at[pl.ds(rows, rows), pl.ds(0, PANEL)], left_ref, sem)
-    copy.start()
-    solve_into(place_ref[0], owners, pieces, high, low, inv_high, inv_low, rhs_ref, wide_ref, y_ref)
-    copy.wait()
-    next_ref[...] = current_ref[...] - times(left_ref[...], wide_ref[...])
-
-
-def first_solve(place, pieces, prepared, factor, current, panel_rows):
+    high, low, inv_high, inv_low, left_ref, current_ref, y_ref, next_ref, rhs_ref = refs[owners:]
+    next_ref[...] = current_ref[...]
+
+    def use(k, wide):
+        columns = slice(k * DIAG, (k + 1) * DIAG)
+        next_ref[...] -= parts_times(left_ref[0, :, columns], left_ref[1, :, columns], wide)
+
+    solve_into(place_ref[0], owners, pieces, high, low, inv_high, inv_low, rhs_ref, y_ref, use)
+
+
+def first_solve(place, pieces, prepared, left, current):
     owners = len(pieces)
-    columns = current.shape[1]
+    panel_rows, columns = current.shape
     return pl.pallas_call(
         functools.partial(first_kernel, owners),
         out_shape=[shaped(PANEL // CYC, CYC, columns), shaped(panel_rows, columns)],
-        in_specs=[IN_SMEM, IN_HBM] + [IN_VMEM] * (owners + 5),
+        in_specs=[IN_SMEM] + [IN_VMEM] * (owners + 6),
         out_specs=[IN_VMEM] * 2,
-        scratch_shapes=[
-            pltpu.VMEM((PANEL // CYC, CYC, columns), F32),
-            pltpu.VMEM((PANEL, 2 * columns), BF16),
-            pltpu.VMEM((panel_rows, PANEL), F32),
-            pltpu.SemaphoreType.DMA,
-        ],
+        scratch_shapes=[pltpu.VMEM((PANEL // CYC, CYC, columns), F32)],
         compiler_params=params(8),
         cost_estimate=cost(HEAVY, 6 * MIB),
         name="first_solve",
-    )(place, factor, *pieces, *prepared, current)
+    )(place, *pieces, *prepared, left, current)
 
 
 def pivot_weights(me, sizes, diag, off):
@@ -410,35 +428,53 @@
     )(place, after, *pivots)
 
 
-def halve_kernel(tile_rows, factor_ref, after_ref, out_ref, token_ref, left_ref, parts_ref, in_sems, out_sems):
-    token_ref[...] = jnp.zeros_like(token_ref)
+def halve_kernel(
+    tile_rows, factor_ref, after_ref, out_ref, own_ref, next_ref, left_ref, below_ref, parts_ref, in_sems, out_sems,
+    own_sems,
+):
     tiles = left_ref.shape[0]
-    loads, stores = [], []
+    rows = own_ref.shape[1]
+    below = pltpu.make_async_copy(factor_ref.at[pl.ds(rows, rows), pl.ds(0, PANEL)], below_ref, own_sems.at[PANELS])
+    below.start()
+    loads, stores, owns = [], [], []
     for t in range(tiles):
         source = factor_ref.at[pl.ds((t + 1) * tile_rows, tile_rows), pl.ds((PANELS - 1) * PANEL, PANEL)]
         loads.append(pltpu.make_async_copy(source, left_ref.at[t], in_sems.at[t]))
         loads[t].start()
+    for panel in range(PANELS):
+        source = factor_ref.at[pl.ds(panel * rows, rows), pl.ds(panel * PANEL, PANEL)]
+        owns.append(pltpu.make_async_copy(source, own_ref.at[panel], own_sems.at[panel]))
+        owns[panel].start()
+    below.wait()
+    next_ref[0], next_ref[1] = split(below_ref[...])
     for t in range(tiles):
         loads[t].wait()
         parts_ref[t, 0], parts_ref[t, 1] = split(left_ref[t])
         stores.append(pltpu.make_async_copy(parts_ref.at[t], out_ref.at[t], out_sems.at[t]))
         stores[t].start()
-    for store in stores:
-        store.wait()
-
-
-def halve_last(factor, tile_rows, after):
+    for copy in owns + stores:
+        copy.wait()
+
+
+def halve_last(factor, panel_rows, after):
+    tile_rows = PANELS * panel_rows
     tiles = factor.shape[0] // tile_rows - 1
     return pl.pallas_call(
         functools.partial(halve_kernel, tile_rows),
-        out_shape=[shaped(tiles, 2, tile_rows, PANEL, dtype=BF16), shaped(8, HALF)],
+        out_shape=[
+            shaped(tiles, 2, tile_rows, PANEL, dtype=BF16),
+            shaped(PANELS, panel_rows, PANEL),
+            shaped(2, panel_rows, PANEL, dtype=BF16),
+        ],
         in_specs=[IN_HBM, pl.BlockSpec(memory_space=pl.ANY)],
-        out_specs=[IN_HBM, IN_VMEM],
+        out_specs=[IN_HBM, IN_VMEM, IN_VMEM],
         scratch_shapes=[
             pltpu.VMEM((tiles, tile_rows, PANEL), F32),
+            pltpu.VMEM((panel_rows, PANEL), F32),
             pltpu.VMEM((tiles, 2, tile_rows, PANEL), BF16),
             pltpu.SemaphoreType.DMA((tiles,)),
             pltpu.SemaphoreType.DMA((tiles,)),
+            pltpu.SemaphoreType.DMA((PANELS + 1,)),
         ],
         compiler_params=params(18),
         cost_estimate=cost(LIGHT, 12 * MIB),
@@ -482,21 +518,30 @@
 def last_kernel(owners, tile_rows, place_ref, left_ref, *refs):
     pieces = refs[:owners]
     high, low, inv_high, inv_low, y_ref, keep_ref, swap_ref, rest_ref = refs[owners : owners + 8]
-    out_ref, rhs_ref, wide_ref, second_ref, stage_ref, sems = refs[owners + 8 :]
+    out_ref, rhs_ref, second_ref, stage_ref, sems = refs[owners + 8 :]
     me = place_ref[0]
-    solve_into(me, owners, pieces, high, low, inv_high, inv_low, rhs_ref, wide_ref, second_ref)
+    last = PANEL // DIAG - 1
     stores = []
-    for t in range(stage_ref.shape[0]):
-        if t:
-            rows = slice((t - 1) * tile_rows, t * tile_rows)
-            stage_ref[t] = rest_ref[rows] - parts_times(left_ref[t - 1, 0], left_ref[t - 1, 1], wide_ref[...])
-        else:
-            scale_own_rows(me, owners, y_ref, second_ref, keep_ref, swap_ref, stage_ref)
+
+    def store(t):
         target = out_ref.at[pl.ds(t * tile_rows, tile_rows)]
         stores.append(pltpu.make_async_copy(stage_ref.at[t], target, sems.at[t]))
-        stores[t].start()
-    for store in stores:
-        store.wait()
+        stores[-1].start()
+
+    def use(k, wide):
+        columns = slice(k * DIAG, (k + 1) * DIAG)
+        for t in range(left_ref.shape[0]):
+            rows = slice(t * tile_rows, (t + 1) * tile_rows)
+            before = stage_ref[t + 1] if k else rest_ref[rows]
+            stage_ref[t + 1] = before - parts_times(left_ref[t, 0, :, columns], left_ref[t, 1, :, columns], wide)
+            if k == last:
+                store(t + 1)
+
+    solve_into(me, owners, pieces, high, low, inv_high, inv_low, rhs_ref, second_ref, use)
+    scale_own_rows(me, owners, y_ref, second_ref, keep_ref, swap_ref, stage_ref)
+    store(0)
+    for copy in stores:
+        copy.wait()
 
 
 def scale_own_rows(me, owners, first_ref, second_ref, keep_ref, swap_ref, stage_ref):
@@ -526,7 +571,6 @@
         out_specs=IN_HBM,
         scratch_shapes=[
             pltpu.VMEM((PANEL // CYC, CYC, columns), F32),
-            pltpu.VMEM((PANEL, 2 * columns), BF16),
             pltpu.VMEM((PANEL // CYC, CYC, columns), F32),
             pltpu.VMEM((rows // tile_rows, tile_rows, columns), F32),
             pltpu.SemaphoreType.DMA((rows // tile_rows,)),
@@ -570,19 +614,19 @@
     pivots = [a.reshape(pivot_diag.shape[0] // DIAG, -1) for a in (pivot_sizes, pivot_diag, pivot_off)]
     keep, swap = own_weights(place, pivots, product)
     direct = from_others(share, keep)
-    parts, halved = halve_last(factor, tile_rows, keep)
-    (first,) = order_rows(0, [panel_rows], pivot_rows, grouped, halved)
-    stacked = stack(place, direct, keep)
+    (first,) = order_rows(0, [panel_rows], pivot_rows, grouped, place)
+    parts, own, left = halve_last(factor, panel_rows, keep)
+    stacked = stack(place, direct, own)
     shared = share_out(stacked[0], first)
-    prepared = invert_panel(0, place, factor, shared, owners, shares, panel_rows, first, HEAVY)
+    prepared = invert_panel(0, place, own, shared, owners, shares, first, HEAVY)
     rest_rows = factor.shape[0] - tile_rows
     second, rest = order_rows(panel_rows, [tile_rows - panel_rows, rest_rows], pivot_rows, grouped, prepared[2])
     later = share_out(stacked[1], second)
     pieces = from_all(first, "row")
-    y, second = first_solve(place, pieces, prepared, factor, second, panel_rows)
+    y, second = first_solve(place, pieces, prepared, left, second)
     pieces = from_all(second, "row")
     rest = middle_update(rest, y, factor, tile_rows)
-    prepared = invert_panel(1, place, factor, later, owners, shares, panel_rows, y, LIGHT)
+    prepared = invert_panel(1, place, own, later, owners, shares, y, LIGHT)
     return last_solve(place, parts, pieces, prepared, y, (keep, swap), rest, tile_rows)
 
 

time: 101 us -> 97.8 us (0.968)
  waiting for transfers between devices: 20.3 us -> 18.7 us
  Pallas kernels: 42.3 us -> 40.7 us
    ppermute x1, waiting for transfers between devices: 12.5 us -> 4.32 us  [from_others(): outer = lax.ppermute(across, 'row', [(i, i ^ 1) for i, _ in middle])]
    all_to_all x1, waiting for transfers between devices: 2.31 us -> 7.09 us  [local(): lax.all_to_all(product, 'row', 0, 0, tiled=True).reshape(vectors.shape)]
    ppermute x14, waiting for transfers between devices: 0.63 us -> 3.18 us  [swap_with(): return lax.ppermute(value, axis, [(i, i ^ distance) for i in range(size)])]
    pallas_call x2, Pallas kernels: 11.2 us -> 8.72 us  [invert_panel(): pl.pallas_call(functools.partial(invert_kernel, panel, owners, shares), o...]
    pallas_call x1, Pallas kernels: 3.54 us -> 2.34 us  [first_solve(): pl.pallas_call(functools.partial(first_kernel, owners), out_shape=[shaped...]
    unnamed x20 -> x28, local copies, waits for them, and re-layouts: 2.67 us -> 3.32 us
  transfers between devices with their start and end apart: 19 -> 19, of which waited for: 5 -> 5; matrix products, arithmetic and copies ran while one was open for 0% -> 0% of each run, Pallas kernels for 36% -> 35%
where the time goes in v2:
time: 97.8 us; the launch traced here: 97.4 us
  Pallas kernels  40.7 us (42%)
  starting transfers between devices  34.1 us (35%)
  waiting for transfers between devices  18.7 us (19%)
  local copies, waits for them, and re-layouts  3.33 us (3%)
    ppermute x14, starting transfers between devices, swap_with(): return lax.ppermute(value, axis, [(i, i ^ distance) for i in range(size)])  18 us
    pallas_call x2, Pallas kernels, invert_panel(): pl.pallas_call(functools.partial(invert_kernel, panel, owners, shares), o...  8.72 us
    pallas_call x1, Pallas kernels, band_product_split(): pl.pallas_call(band_kernel, out_shape=shaped(owners, rows // owners, colu...  8.04 us
    all_to_all x1, starting transfers between devices, local(): lax.all_to_all(product, 'row', 0, 0, tiled=True).reshape(vectors.shape)  7.24 us
    all_to_all x1, waiting for transfers between devices, local(): lax.all_to_all(product, 'row', 0, 0, tiled=True).reshape(vectors.shape)  7.09 us
    ppermute x2, starting transfers between devices, local(): halo = (lax.ppermute(last, 'row', up), lax.ppermute(first, 'row', down))  6.24 us
    pallas_call x1, Pallas kernels, last_solve(): pl.pallas_call(functools.partial(last_kernel, owners, tile_rows), out_sha...  4.54 us
    ppermute x1, waiting for transfers between devices, from_others(): outer = lax.ppermute(across, 'row', [(i, i ^ 1) for i, _ in middle])  4.32 us
  transfers between devices with their start and end apart: 19, of which 5 were waited for; matrix products, arithmetic and copies ran while one was open for 0% of the time, Pallas kernels for 35%

profile of v2, /device:TPU:0, one launch (start us, length us, event | category | flops | bytes accessed | tf_op | source)
XLA Modules:
  0.0 97.4 jit_solution(3898315010238903232)
XLA Ops:
  0.0 0.1 pad_add_fusion.place_ref.after_ref
  0.1 2.5 %first_sends.1 = (f32[2,16,2304]{2,1,0:T(8,128)}, f32[512,128]{1,0:T(8,128)S(1)}, f32[512,128]{1,0:T(8,128)S(1)}) custom-call(s32[2]{0:T(128)S(1)} %pad_add_fusion.place_ref.after_ref, f32[2048,2048]{1,0:T(8,128)} %factor_ref.5, f32[2048,128]{1,0:T(8,128)} %vec_ref.3), custom_call_target="tpu_custom_call" | custom-call | bytes 4194304 | tf_op jit(solution)/shard_map/first_sends/pallas_call | solution.py:112
  2.6 4.9 %collective-permute-start = (f32[512,128]{1,0:T(8,128)S(1)}, f32[512,128]{1,0:T(8,128)S(1)}, u32[]{:S(2)}, u32[]{:S(2)}) collective-permute-start(f32[512,128]{1,0:T(8,128)S(1)} %get-tuple-element.27), channel_id=1, source_target_pairs={{0,4},{4,8},{8,12},{1,5},{5,9},{9,13},{2,6},{6,10},{10,14},{3,7},{... | collective-permute-start | bytes 786440 | tf_op jit(solution)/shard_map/ppermute | solution.py:605
  7.5 1.3 %collective-permute-start.1 = (f32[512,128]{1,0:T(8,128)S(1)}, f32[512,128]{1,0:T(8,128)S(1)}, u32[]{:S(2)}, u32[]{:S(2)}) collective-permute-start(f32[512,128]{1,0:T(8,128)S(1)} %get-tuple-element.28), channel_id=1, source_target_pairs={{4,0},{8,4},{12,8},{5,1},{9,5},{13,9},{6,2},{10,6},{14,10},{7,3},{... | collective-permute-start | bytes 786440 | tf_op jit(solution)/shard_map/ppermute | solution.py:605
  8.8 3.7 %collective-permute-start.6 = (f32[2,16,2304]{2,1,0:T(8,128)}, f32[2,16,2304]{2,1,0:T(8,128)S(1)}, u32[]{:S(2)}, u32[]{:S(2)}) collective-permute-start(f32[2,16,2304]{2,1,0:T(8,128)} %get-tuple-element.32), channel_id=1, source_target_pairs={{0,8},{4,12},{8,0},{12,4},{1,9},{5,13},{9,1},{13,5},{2,10},{6,14},... | collective-permute-start | bytes 884744 | tf_op jit(solution)/shard_map/ppermute | solution.py:586
  12.5 1.6 %collective-permute-start.5 = (f32[2,16,2304]{2,1,0:T(8,128)}, f32[2,16,2304]{2,1,0:T(8,128)}, u32[]{:S(2)}, u32[]{:S(2)}) collective-permute-start(f32[2,16,2304]{2,1,0:T(8,128)} %get-tuple-element.32), channel_id=1, source_target_pairs={{0,4},{4,0},{8,12},{12,8},{1,5},{5,1},{9,13},{13,9},{2,6},{6,2},{1... | collective-permute-start | bytes 884744 | tf_op jit(solution)/shard_map/ppermute | solution.py:586
  14.1 1.4 %collective-permute-start.7 = (f32[2,16,2304]{2,1,0:T(8,128)}, f32[2,16,2304]{2,1,0:T(8,128)}, u32[]{:S(2)}, u32[]{:S(2)}) collective-permute-start(f32[2,16,2304]{2,1,0:T(8,128)} %get-tuple-element.32), channel_id=1, source_target_pairs={{4,8},{8,4},{5,9},{9,5},{6,10},{10,6},{7,11},{11,7},{20,24},{24,20... | collective-permute-start | bytes 884744 | tf_op jit(solution)/shard_map/ppermute | solution.py:190
  15.5 0.0 collective-permute-done.before_ref
  15.5 4.1 %collective-permute-done.1.after_ref = f32[512,128]{1,0:T(8,128)S(1)} collective-permute-done((f32[512,128]{1,0:T(8,128)S(1)}, f32[512,128]{1,0:T(8,128)S(1)}, u32[]{:S(2)}, u32[]{:S(2)}) %collective-permute-start.1) | collective-permute-done | bytes 262176 | tf_op jit(solution)/shard_map/ppermute | solution.py:605
  19.6 8.0 %band_product_split.1.after_ref = f32[4,512,128]{2,1,0:T(8,128)} custom-call(f32[2048,1536]{1,0:T(8,128)} %inter_ref.1, f32[2048,128]{1,0:T(8,128)S(1)} %copy-done.1, f32[512,128]{1,0:T(8,128)S(1)} %collective-permute-done.before_ref, f32[512,128]{1,0:T(8,128)S(1)} %collective-permute-done.1.after_ref), custom_call_target="tpu_custom_call" | custom-call | flops 3221225472 | bytes 12582912 | tf_op jit(solution)/shard_map/band_product_split/pallas_call | solution.py:151
  27.7 7.2 %all-to-all-start = ((f32[4,512,128]{2,1,0:T(8,128)}), f32[4,512,128]{2,1,0:T(8,128)S(1)}, u32[]{:S(2)}, u32[]{:S(2)}) async-start(f32[4,512,128]{2,1,0:T(8,128)} %band_product_split.1.after_ref), calls=%async_computation | async-start | bytes 2097152 | tf_op jit(solution)/shard_map/all_to_all | solution.py:607
  34.9 1.0 own_weights.1
  35.9 0.0 collective-permute-done.6.value_ref
  35.9 0.6 copy-done.4
  36.6 1.3 %collective-permute-start.8 = (f32[2,16,2304]{2,1,0:T(8,128)S(1)}, f32[2,16,2304]{2,1,0:T(8,128)S(1)}, u32[]{:S(2)}, u32[]{:S(2)}) collective-permute-start(f32[2,16,2304]{2,1,0:T(8,128)S(1)} %pass_on.3.across_ref), channel_id=1, source_target_pairs={{4,0},{8,12},{5,1},{9,13},{6,2},{10,14},{7,3},{11,15},{20,16},{24,... | collective-permute-start | bytes 884744 | tf_op jit(solution)/shard_map/ppermute | solution.py:191
  37.8 4.0 %halve_last.1 = (bf16[3,2,512,1024]{3,2,1,0:T(8,128)(2,1)S(1)}, f32[2,256,1024]{2,1,0:T(8,128)S(1)}, bf16[2,256,1024]{2,1,0:T(8,128)(2,1)S(1)}) custom-call(f32[2048,2048]{1,0:T(8,128)} %factor_ref.5, f32[256,128]{1,0:T(8,128)S(1)} %get-tuple-element.29.after_ref.refs_9_), custom_call_target="tpu_custom_call" | custom-call | flops 1073741824 | bytes 12582912 | tf_op jit(solution)/shard_map/halve_last/pallas_call | solution.py:462
  41.9 2.7 %copy-done = bf16[3,2,512,1024]{3,2,1,0:T(8,128)(2,1)} copy-done((bf16[3,2,512,1024]{3,2,1,0:T(8,128)(2,1)}, bf16[3,2,512,1024]{3,2,1,0:T(8,128)(2,1)S(1)}, u32[]{:S(2)}) %copy-start) | copy-done | bytes 6291480
  44.6 0.0 collective-permute-done.5.near_ref
  44.6 0.0 collective-permute-done.7.inner_ref
  44.6 4.3 %collective-permute-done.8.outer_ref = f32[2,16,2304]{2,1,0:T(8,128)S(1)} collective-permute-done((f32[2,16,2304]{2,1,0:T(8,128)S(1)}, f32[2,16,2304]{2,1,0:T(8,128)S(1)}, u32[]{:S(2)}, u32[]{:S(2)}) %collective-permute-start.8) | collective-permute-done | bytes 294944 | tf_op jit(solution)/shard_map/ppermute | solution.py:191
  48.9 2.1 %stack.13 = (f32[3,16,2304]{2,1,0:T(8,128)}, f32[3,16,2304]{2,1,0:T(8,128)}) custom-call(s32[2]{0:T(128)S(1)} %pad_add_fusion.place_ref.after_ref, f32[2,16,2304]{2,1,0:T(8,128)} %collective-permute-done.5.near_ref, f32[2,16,2304]{2,1,0:T(8,128)S(1)} %pass_on.3.across_ref, f32[2,16,2304]{2,1,0:T(8,128)} %collective-permute-done.7.inner_ref, ...), custom_call_target="tpu_custom_call" | custom-call | tf_op jit(solution)/shard_map/stack/pallas_call | solution.py:214
  51.0 1.5 %collective-permute-start.10 = (f32[3,16,2304]{2,1,0:T(8,128)}, f32[3,16,2304]{2,1,0:T(8,128)}, u32[]{:S(2)}, u32[]{:S(2)}) collective-permute-start(f32[3,16,2304]{2,1,0:T(8,128)} %get-tuple-element.33.refs_0_), channel_id=1, source_target_pairs={{0,2},{1,3},{2,0},{3,1},{4,6},{5,7},{6,4},{7,5},{8,10},{9,11},{10,... | collective-permute-start | bytes 1327112 | tf_op jit(solution)/shard_map/ppermute | solution.py:586
  52.5 7.1 %all-to-all-done = f32[4,512,128]{2,1,0:T(8,128)S(1)} async-done(((f32[4,512,128]{2,1,0:T(8,128)}), f32[4,512,128]{2,1,0:T(8,128)S(1)}, u32[]{:S(2)}, u32[]{:S(2)}) %all-to-all-start) | async-done | bytes 1048608 | tf_op jit(solution)/shard_map/all_to_all | solution.py:607
  59.6 0.9 order_rows.2.after_ref.refs_0_
  60.5 0.0 collective-permute-done.10.value_ref
  60.6 0.1 collective-permute-start.11
  60.6 1.6 %collective-permute-start.16 = (f32[3,16,2304]{2,1,0:T(8,128)}, f32[3,16,2304]{2,1,0:T(8,128)S(1)}, u32[]{:S(2)}, u32[]{:S(2)}) collective-permute-start(f32[3,16,2304]{2,1,0:T(8,128)} %get-tuple-element.42.refs_0_), channel_id=1, source_target_pairs={{0,2},{1,3},{2,0},{3,1},{4,6},{5,7},{6,4},{7,5},{8,10},{9,11},{10,... | collective-permute-start | bytes 1327112 | tf_op jit(solution)/shard_map/ppermute | solution.py:586
  62.2 0.2 collective-permute-start.15
  62.4 0.6 collective-permute-start.2
  63.0 0.3 collective-permute-start.3
  63.3 0.0 collective-permute-done.11.refs_3_
  63.3 3.4 %collective-permute-start.4 = (f32[256,128]{1,0:T(8,128)S(1)}, f32[256,128]{1,0:T(8,128)S(1)}, u32[]{:S(2)}, u32[]{:S(2)}) collective-permute-start(f32[256,128]{1,0:T(8,128)S(1)} %order_rows.2.after_ref.refs_0_), channel_id=1, source_target_pairs={{0,12},{4,8},{8,4},{12,0},{1,13},{5,9},{9,5},{13,1},{2,14},{6,10},... | collective-permute-start | bytes 393224 | tf_op jit(solution)/shard_map/ppermute | solution.py:586
  66.8 4.4 %invert_panel.2 = (bf16[1024,1024]{1,0:T(8,128)(2,1)S(1)}, bf16[1024,1024]{1,0:T(8,128)(2,1)S(1)}, bf16[4,256,256]{2,1,0:T(8,128)(2,1)S(1)}, bf16[4,256,256]{2,1,0:T(8,128)(2,1)S(1)}) custom-call(s32[2]{0:T(128)S(1)} %pad_add_fusion.place_ref.after_ref, f32[256,128]{1,0:T(8,128)S(1)} %order_rows.2.after_ref.refs_0_, ...), custom_call_target="tpu_custom_call" | custom-call | flops 137438953472 | bytes 12582912 | tf_op jit(solution)/shard_map/invert_panel/pallas_call | solution.py:295
  71.2 2.6 %order_rows.3 = (f32[256,128]{1,0:T(8,128)S(1)}, f32[1536,128]{1,0:T(8,128)S(1)}) custom-call(s32[2048]{0:T(1024)S(1)} %copy-done.6, f32[2048,128]{1,0:T(8,128)S(1)} %bitcast.6, bf16[4,256,256]{2,1,0:T(8,128)(2,1)S(1)} %get-tuple-element.36.after_ref.refs_6_), custom_call_target="tpu_custom_call" | custom-call | bytes 2097152 | tf_op jit(solution)/shard_map/order_rows/pallas_call | solution.py:328
  73.8 0.0 collective-permute-done.16.value_ref
  73.8 0.1 collective-permute-start.17
  73.9 2.0 %collective-permute-done.3.refs_2_ = f32[256,128]{1,0:T(8,128)S(1)} collective-permute-done((f32[256,128]{1,0:T(8,128)S(1)}, f32[256,128]{1,0:T(8,128)S(1)}, u32[]{:S(2)}, u32[]{:S(2)}) %collective-permute-start.3) | collective-permute-done | bytes 131104 | tf_op jit(solution)/shard_map/ppermute | solution.py:586
  75.9 2.3 %first_solve.1 = (f32[64,16,128]{2,1,0:T(8,128)S(1)}, f32[256,128]{1,0:T(8,128)S(1)}) custom-call(s32[2]{0:T(128)S(1)} %pad_add_fusion.place_ref.after_ref, f32[256,128]{1,0:T(8,128)S(1)} %order_rows.2.after_ref.refs_0_, f32[256,128]{1,0:T(8,128)S(1)} %collective-permute-done.2.refs_1_, f32[256,128]{1,0:T(8,128)S(1)} %collective-permute-done.3.refs_2_, ...), custom_call_target="tpu_custom_call" | custom-call | flops 137438953472 | bytes 6291456 | tf_op jit(solution)/shard_map/first_solve/pallas_call | solution.py:380
  78.2 2.5 %collective-permute-start.12 = (f32[256,128]{1,0:T(8,128)S(1)}, f32[256,128]{1,0:T(8,128)S(1)}, u32[]{:S(2)}, u32[]{:S(2)}) collective-permute-start(f32[256,128]{1,0:T(8,128)S(1)} %get-tuple-element.40.refs_0_), channel_id=1, source_target_pairs={{0,4},{4,0},{8,12},{12,8},{1,5},{5,1},{9,13},{13,9},{2,6},{6,2},{1... | collective-permute-start | bytes 393224 | tf_op jit(solution)/shard_map/ppermute | solution.py:586
  80.7 0.0 collective-permute-start.13
  80.7 2.4 %collective-permute-start.14 = (f32[256,128]{1,0:T(8,128)S(1)}, f32[256,128]{1,0:T(8,128)S(1)}, u32[]{:S(2)}, u32[]{:S(2)}) collective-permute-start(f32[256,128]{1,0:T(8,128)S(1)} %get-tuple-element.40.refs_0_), channel_id=1, source_target_pairs={{0,12},{4,8},{8,4},{12,0},{1,13},{5,9},{9,5},{13,1},{2,14},{6,10},... | collective-permute-start | bytes 393224 | tf_op jit(solution)/shard_map/ppermute | solution.py:586
  83.2 3.9 %middle_update.1.refs_11_ = f32[1536,128]{1,0:T(8,128)S(1)} custom-call(f32[2048,2048]{1,0:T(8,128)} %factor_ref.5, f32[1536,128]{1,0:T(8,128)S(1)} %get-tuple-element.48.rest_ref, f32[64,16,128]{2,1,0:T(8,128)S(1)} %get-tuple-element.41.after_ref.y_ref.refs_8_), custom_call_target="tpu_custom_call" | custom-call | flops 1610612736 | bytes 8388608 | tf_op jit(solution)/shard_map/middle_update/pallas_call | solution.py:502
  87.1 0.0 collective-permute-done.15.refs_1_
  87.2 4.3 %invert_panel.3 = (bf16[1024,1024]{1,0:T(8,128)(2,1)S(1)}, bf16[1024,1024]{1,0:T(8,128)(2,1)S(1)}, bf16[4,256,256]{2,1,0:T(8,128)(2,1)S(1)}, bf16[4,256,256]{2,1,0:T(8,128)(2,1)S(1)}) custom-call(s32[2]{0:T(128)S(1)} %pad_add_fusion.place_ref.after_ref, f32[64,16,128]{2,1,0:T(8,128)S(1)} %get-tuple-element.41.after_ref.y_ref.refs_8_, ...), custom_call_target="tpu_custom_call" | custom-call | flops 1073741824 | bytes 12582912 | tf_op jit(solution)/shard_map/invert_panel/pallas_call | solution.py:295
  91.5 0.0 collective-permute-done.12.refs_1_
  91.5 1.2 %collective-permute-done.13.refs_2_ = f32[256,128]{1,0:T(8,128)S(1)} collective-permute-done((f32[256,128]{1,0:T(8,128)S(1)}, f32[256,128]{1,0:T(8,128)S(1)}, u32[]{:S(2)}, u32[]{:S(2)}) %collective-permute-start.13) | collective-permute-done | bytes 131104 | tf_op jit(solution)/shard_map/ppermute | solution.py:586
  92.7 0.0 collective-permute-done.14.refs_3_
  92.7 4.5 %last_solve.1 = f32[2048,128]{1,0:T(8,128)} custom-call(s32[2]{0:T(128)S(1)} %pad_add_fusion.place_ref.after_ref, bf16[3,2,512,1024]{3,2,1,0:T(8,128)(2,1)S(1)} %bitcast.8, f32[256,128]{1,0:T(8,128)S(1)} %get-tuple-element.40.refs_0_, f32[256,128]{1,0:T(8,128)S(1)} %collective-permute-done.12.refs_1_, f32[256,128]{1,0:T(8,128)S(1)} %collective-permute-done.13.refs_2_, ...), custom_call_target="tpu_custom_call" | custom-call | flops 2147483648 | bytes 12582912 | tf_op jit(solution)/shard_map/last_solve/pallas_call | solution.py:567
  (36 shorter events, 0.1 us)
Async XLA Ops:
  0.1 15.5 %copy-start.11 = (f32[2048]{0:T(1024)S(1)}, f32[2048]{0:T(1024)}, u32[]{:S(2)}) copy-start(f32[2048]{0:T(1024)} %param.12) | copy-start | bytes 24580
  0.1 19.6 %copy-start.1 = (f32[2048,128]{1,0:T(8,128)S(1)}, f32[2048,128]{1,0:T(8,128)}, u32[]{:S(2)}) copy-start(f32[2048,128]{1,0:T(8,128)} %vec_ref.3) | copy-start | bytes 3145732
  2.6 13.0 %collective-permute-start = (f32[512,128]{1,0:T(8,128)S(1)}, f32[512,128]{1,0:T(8,128)S(1)}, u32[]{:S(2)}, u32[]{:S(2)}) collective-permute-start(f32[512,128]{1,0:T(8,128)S(1)} %get-tuple-element.27), channel_id=1, source_target_pairs={{0,4},{4,8},{8,12},{1,5},{5,9},{9,13},{2,6},{6,10},{10,14},{3,7},{... | collective-permute-start | bytes 786440 | tf_op jit(solution)/shard_map/ppermute | solution.py:605
  7.5 12.1 %collective-permute-start.1 = (f32[512,128]{1,0:T(8,128)S(1)}, f32[512,128]{1,0:T(8,128)S(1)}, u32[]{:S(2)}, u32[]{:S(2)}) collective-permute-start(f32[512,128]{1,0:T(8,128)S(1)} %get-tuple-element.28), channel_id=1, source_target_pairs={{4,0},{8,4},{12,8},{5,1},{9,5},{13,9},{6,2},{10,6},{14,10},{7,3},{... | collective-permute-start | bytes 786440 | tf_op jit(solution)/shard_map/ppermute | solution.py:605
  8.8 27.1 %collective-permute-start.6 = (f32[2,16,2304]{2,1,0:T(8,128)}, f32[2,16,2304]{2,1,0:T(8,128)S(1)}, u32[]{:S(2)}, u32[]{:S(2)}) collective-permute-start(f32[2,16,2304]{2,1,0:T(8,128)} %get-tuple-element.32), channel_id=1, source_target_pairs={{0,8},{4,12},{8,0},{12,4},{1,9},{5,13},{9,1},{13,5},{2,10},{6,14},... | collective-permute-start | bytes 884744 | tf_op jit(solution)/shard_map/ppermute | solution.py:586
  12.5 32.0 %collective-permute-start.5 = (f32[2,16,2304]{2,1,0:T(8,128)}, f32[2,16,2304]{2,1,0:T(8,128)}, u32[]{:S(2)}, u32[]{:S(2)}) collective-permute-start(f32[2,16,2304]{2,1,0:T(8,128)} %get-tuple-element.32), channel_id=1, source_target_pairs={{0,4},{4,0},{8,12},{12,8},{1,5},{5,1},{9,13},{13,9},{2,6},{6,2},{1... | collective-permute-start | bytes 884744 | tf_op jit(solution)/shard_map/ppermute | solution.py:586
  14.1 30.4 %collective-permute-start.7 = (f32[2,16,2304]{2,1,0:T(8,128)}, f32[2,16,2304]{2,1,0:T(8,128)}, u32[]{:S(2)}, u32[]{:S(2)}) collective-permute-start(f32[2,16,2304]{2,1,0:T(8,128)} %get-tuple-element.32), channel_id=1, source_target_pairs={{4,8},{8,4},{5,9},{9,5},{6,10},{10,6},{7,11},{11,7},{20,24},{24,20... | collective-permute-start | bytes 884744 | tf_op jit(solution)/shard_map/ppermute | solution.py:190
  27.7 7.2 %copy-start.9 = (s32[1024]{0:T(1024)S(1)}, s32[1024]{0:T(1024)}, u32[]{:S(2)}) copy-start(s32[1024]{0:T(1024)} %param.11) | copy-start | bytes 12292
  27.7 7.2 %copy-start.10 = (f32[1024]{0:T(1024)S(1)}, f32[1024]{0:T(1024)}, u32[]{:S(2)}) copy-start(f32[1024]{0:T(1024)} %param.13) | copy-start | bytes 12292
  27.7 31.9 %all-to-all-start = ((f32[4,512,128]{2,1,0:T(8,128)}), f32[4,512,128]{2,1,0:T(8,128)S(1)}, u32[]{:S(2)}, u32[]{:S(2)}) async-start(f32[4,512,128]{2,1,0:T(8,128)} %band_product_split.1.after_ref), calls=%async_computation | async-start | bytes 2097152 | tf_op jit(solution)/shard_map/all_to_all | solution.py:607
  35.9 0.7 copy-start.4
  35.9 6.0 %copy-start.2 = (f32[256,128]{1,0:T(8,128)}, f32[256,128]{1,0:T(8,128)S(1)}, u32[]{:S(2)}) copy-start(f32[256,128]{1,0:T(8,128)S(1)} %get-tuple-element.29.after_ref.refs_9_) | copy-start | bytes 393220
  36.6 12.3 %collective-permute-start.8 = (f32[2,16,2304]{2,1,0:T(8,128)S(1)}, f32[2,16,2304]{2,1,0:T(8,128)S(1)}, u32[]{:S(2)}, u32[]{:S(2)}) collective-permute-start(f32[2,16,2304]{2,1,0:T(8,128)S(1)} %pass_on.3.across_ref), channel_id=1, source_target_pairs={{4,0},{8,12},{5,1},{9,13},{6,2},{10,14},{7,3},{11,15},{20,16},{24,... | collective-permute-start | bytes 884744 | tf_op jit(solution)/shard_map/ppermute | solution.py:191
  41.9 2.7 %copy-start = (bf16[3,2,512,1024]{3,2,1,0:T(8,128)(2,1)}, bf16[3,2,512,1024]{3,2,1,0:T(8,128)(2,1)S(1)}, u32[]{:S(2)}) copy-start(bf16[3,2,512,1024]{3,2,1,0:T(8,128)(2,1)S(1)} %get-tuple-element.30.left_ref) | copy-start | bytes 18874372
  44.6 8.0 %copy-start.7 = (bf16[2,256,1024]{2,1,0:T(8,128)(2,1)}, bf16[2,256,1024]{2,1,0:T(8,128)(2,1)S(1)}, u32[]{:S(2)}) copy-start(bf16[2,256,1024]{2,1,0:T(8,128)(2,1)S(1)} %get-tuple-element.38.refs_8_) | copy-start | bytes 3145732
  44.6 15.1 %copy-start.6 = (s32[2048]{0:T(1024)S(1)}, s32[2048]{0:T(1024)}, u32[]{:S(2)}) copy-start(s32[2048]{0:T(1024)} %pivot_ref.3) | copy-start | bytes 24580
  51.0 9.5 %collective-permute-start.10 = (f32[3,16,2304]{2,1,0:T(8,128)}, f32[3,16,2304]{2,1,0:T(8,128)}, u32[]{:S(2)}, u32[]{:S(2)}) collective-permute-start(f32[3,16,2304]{2,1,0:T(8,128)} %get-tuple-element.33.refs_0_), channel_id=1, source_target_pairs={{0,2},{1,3},{2,0},{3,1},{4,6},{5,7},{6,4},{7,5},{8,10},{9,11},{10,... | collective-permute-start | bytes 1327112 | tf_op jit(solution)/shard_map/ppermute | solution.py:586
  52.5 10.5 %collective-permute-start.9 = (f32[3,16,2304]{2,1,0:T(8,128)}, f32[3,16,2304]{2,1,0:T(8,128)}, u32[]{:S(2)}, u32[]{:S(2)}) collective-permute-start(f32[3,16,2304]{2,1,0:T(8,128)} %get-tuple-element.33.refs_0_), channel_id=1, source_target_pairs={{0,1},{1,0},{2,3},{3,2},{4,5},{5,4},{6,7},{7,6},{8,9},{9,8},{10,11... | collective-permute-start | bytes 1327112 | tf_op jit(solution)/shard_map/ppermute | solution.py:586
  60.6 2.8 %collective-permute-start.11 = (f32[3,16,2304]{2,1,0:T(8,128)}, f32[3,16,2304]{2,1,0:T(8,128)S(1)}, u32[]{:S(2)}, u32[]{:S(2)}) collective-permute-start(f32[3,16,2304]{2,1,0:T(8,128)} %pass_on.4.refs_2_), channel_id=1, source_target_pairs={{0,1},{1,0},{2,3},{3,2},{4,5},{5,4},{6,7},{7,6},{8,9},{9,8},{10,11... | collective-permute-start | bytes 1327112 | tf_op jit(solution)/shard_map/ppermute | solution.py:586
  60.6 13.2 %collective-permute-start.16 = (f32[3,16,2304]{2,1,0:T(8,128)}, f32[3,16,2304]{2,1,0:T(8,128)S(1)}, u32[]{:S(2)}, u32[]{:S(2)}) collective-permute-start(f32[3,16,2304]{2,1,0:T(8,128)} %get-tuple-element.42.refs_0_), channel_id=1, source_target_pairs={{0,2},{1,3},{2,0},{3,1},{4,6},{5,7},{6,4},{7,5},{8,10},{9,11},{10,... | collective-permute-start | bytes 1327112 | tf_op jit(solution)/shard_map/ppermute | solution.py:586
  62.2 25.0 %collective-permute-start.15 = (f32[3,16,2304]{2,1,0:T(8,128)}, f32[3,16,2304]{2,1,0:T(8,128)}, u32[]{:S(2)}, u32[]{:S(2)}) collective-permute-start(f32[3,16,2304]{2,1,0:T(8,128)} %get-tuple-element.42.refs_0_), channel_id=1, source_target_pairs={{0,1},{1,0},{2,3},{3,2},{4,5},{5,4},{6,7},{7,6},{8,9},{9,8},{10,11... | collective-permute-start | bytes 1327112 | tf_op jit(solution)/shard_map/ppermute | solution.py:586
  62.4 11.5 %collective-permute-start.2 = (f32[256,128]{1,0:T(8,128)S(1)}, f32[256,128]{1,0:T(8,128)S(1)}, u32[]{:S(2)}, u32[]{:S(2)}) collective-permute-start(f32[256,128]{1,0:T(8,128)S(1)} %order_rows.2.after_ref.refs_0_), channel_id=1, source_target_pairs={{0,4},{4,0},{8,12},{12,8},{1,5},{5,1},{9,13},{13,9},{2,6},{6,2},{1... | collective-permute-start | bytes 393224 | tf_op jit(solution)/shard_map/ppermute | solution.py:586
  63.0 12.9 %collective-permute-start.3 = (f32[256,128]{1,0:T(8,128)S(1)}, f32[256,128]{1,0:T(8,128)S(1)}, u32[]{:S(2)}, u32[]{:S(2)}) collective-permute-start(f32[256,128]{1,0:T(8,128)S(1)} %order_rows.2.after_ref.refs_0_), channel_id=1, source_target_pairs={{0,8},{4,12},{8,0},{12,4},{1,9},{5,13},{9,1},{13,5},{2,10},{6,14},... | collective-permute-start | bytes 393224 | tf_op jit(solution)/shard_map/ppermute | solution.py:586
  63.3 12.6 %collective-permute-start.4 = (f32[256,128]{1,0:T(8,128)S(1)}, f32[256,128]{1,0:T(8,128)S(1)}, u32[]{:S(2)}, u32[]{:S(2)}) collective-permute-start(f32[256,128]{1,0:T(8,128)S(1)} %order_rows.2.after_ref.refs_0_), channel_id=1, source_target_pairs={{0,12},{4,8},{8,4},{12,0},{1,13},{5,9},{9,5},{13,1},{2,14},{6,10},... | collective-permute-start | bytes 393224 | tf_op jit(solution)/shard_map/ppermute | solution.py:586
  71.2 4.7 %copy-start.8 = (bf16[2,256,1024]{2,1,0:T(8,128)(2,1)S(1)}, bf16[2,256,1024]{2,1,0:T(8,128)(2,1)}, u32[]{:S(2)}) copy-start(bf16[2,256,1024]{2,1,0:T(8,128)(2,1)} %copy-done.7) | copy-start | bytes 3145732
  73.8 13.3 %collective-permute-start.17 = (f32[3,16,2304]{2,1,0:T(8,128)S(1)}, f32[3,16,2304]{2,1,0:T(8,128)S(1)}, u32[]{:S(2)}, u32[]{:S(2)}) collective-permute-start(f32[3,16,2304]{2,1,0:T(8,128)S(1)} %pass_on.5.refs_2_), channel_id=1, source_target_pairs={{0,1},{1,0},{2,3},{3,2},{4,5},{5,4},{6,7},{7,6},{8,9},{9,8},{10,11... | collective-permute-start | bytes 1327112 | tf_op jit(solution)/shard_map/ppermute | solution.py:586
  78.2 13.2 %collective-permute-start.12 = (f32[256,128]{1,0:T(8,128)S(1)}, f32[256,128]{1,0:T(8,128)S(1)}, u32[]{:S(2)}, u32[]{:S(2)}) collective-permute-start(f32[256,128]{1,0:T(8,128)S(1)} %get-tuple-element.40.refs_0_), channel_id=1, source_target_pairs={{0,4},{4,0},{8,12},{12,8},{1,5},{5,1},{9,13},{13,9},{2,6},{6,2},{1... | collective-permute-start | bytes 393224 | tf_op jit(solution)/shard_map/ppermute | solution.py:586
  80.7 11.9 %collective-permute-start.13 = (f32[256,128]{1,0:T(8,128)S(1)}, f32[256,128]{1,0:T(8,128)S(1)}, u32[]{:S(2)}, u32[]{:S(2)}) collective-permute-start(f32[256,128]{1,0:T(8,128)S(1)} %get-tuple-element.40.refs_0_), channel_id=1, source_target_pairs={{0,8},{4,12},{8,0},{12,4},{1,9},{5,13},{9,1},{13,5},{2,10},{6,14},... | collective-permute-start | bytes 393224 | tf_op jit(solution)/shard_map/ppermute | solution.py:586
  80.7 11.9 %collective-permute-start.14 = (f32[256,128]{1,0:T(8,128)S(1)}, f32[256,128]{1,0:T(8,128)S(1)}, u32[]{:S(2)}, u32[]{:S(2)}) collective-permute-start(f32[256,128]{1,0:T(8,128)S(1)} %get-tuple-element.40.refs_0_), channel_id=1, source_target_pairs={{0,12},{4,8},{8,4},{12,0},{1,13},{5,9},{9,5},{13,1},{2,14},{6,10},... | collective-permute-start | bytes 393224 | tf_op jit(solution)/shard_map/ppermute | solution.py:586
  83.2 9.5 %slice-start = ((s8[6291456]{0:T(1024)(128)(4,1)}), s8[4194304]{0:T(1024)(128)(4,1)S(1)}, s32[]{:S(2)}) async-start(s8[6291456]{0:T(1024)(128)(4,1)} %bitcast.7), calls=%async_computation.1 | async-start | bytes 8388608
  83.2 9.5 %slice-start.1 = ((s8[6291456]{0:T(1024)(128)(4,1)}), s8[2097152]{0:T(1024)(128)(4,1)S(1)}, s32[]{:S(2)}) async-start(s8[6291456]{0:T(1024)(128)(4,1)} %bitcast.7), calls=%async_computation.2 | async-start | bytes 4194304
  87.1 5.6 %copy-start.3 = (f32[256,128]{1,0:T(8,128)S(1)}, f32[256,128]{1,0:T(8,128)}, u32[]{:S(2)}) copy-start(f32[256,128]{1,0:T(8,128)} %copy-done.2) | copy-start | bytes 393220
  87.1 5.6 %copy-start.5 = (f32[256,128]{1,0:T(8,128)S(1)}, f32[256,128]{1,0:T(8,128)}, u32[]{:S(2)}) copy-start(f32[256,128]{1,0:T(8,128)} %copy-done.4) | copy-start | bytes 393220

commit v3 on v2

--- a/solution.py
+++ b/solution.py
@@ -121,7 +121,7 @@
     )(place, factor, vectors)
 
 
-def band_kernel(inter_ref, vec_ref, before_ref, after_ref, out_ref, wide_ref):
+def band_kernel(inter_ref, vec_ref, after_ref, before_ref, out_ref, wide_ref):
     tile = pl.program_id(0)
     rows = vec_ref.shape[0]
     tile_rows = inter_ref.shape[0]
@@ -339,9 +339,9 @@
 def solve_into(me, owners, pieces, high_ref, low_ref, inv_high_ref, inv_low_ref, rhs_ref, y_ref, use):
     slots = pieces[0].shape[0] // CYC
     columns = pieces[0].shape[1]
-    for k in range(owners):
+    for piece, distance in zip(pieces, (0, *far_first(owners))):
         for s in range(slots):
-            rhs_ref[s * owners + (me ^ k)] = pieces[k][s * CYC : (s + 1) * CYC]
+            rhs_ref[s * owners + (me ^ distance)] = piece[s * CYC : (s + 1) * CYC]
     runs = [slice(k * DIAG, (k + 1) * DIAG) for k in range(PANEL // DIAG)]
     rhs = [rhs_ref[r.start // CYC : r.stop // CYC].reshape(DIAG, columns) for r in runs]
 
@@ -586,8 +586,12 @@
     return lax.ppermute(value, axis, [(i, i ^ distance) for i in range(size)])
 
 
+def far_first(owners):
+    return [*range(2, owners), 1]
+
+
 def from_all(value, axis):
-    return [value] + [swap_with(value, axis, k) for k in range(1, lax.axis_size(axis))]
+    return [value] + [swap_with(value, axis, k) for k in far_first(lax.axis_size(axis))]
 
 
 def local(vectors, intersection, factor, pivot_rows, pivot_sizes, pivot_diag, pivot_off):
@@ -595,14 +599,14 @@
     slots = PANEL // owners // CYC
     panel_rows = slots * CYC
     place = jnp.stack([lax.axis_index("row"), lax.axis_index("vec")]).astype(jnp.int32)
-    intersection, factor = (pltpu.with_memory_space_constraint(a, pltpu.HBM) for a in (intersection, factor))
-
-    share, first, last = first_sends(
-        place, factor, pltpu.with_memory_space_constraint(vectors, pltpu.HBM), slots, shares
+    vectors, intersection, factor = (
+        pltpu.with_memory_space_constraint(a, pltpu.HBM) for a in (vectors, intersection, factor)
     )
+
+    share, first, last = first_sends(place, factor, vectors, slots, shares)
     up = [(i, i + 1) for i in range(owners - 1)]
     down = [(j, i) for i, j in up]
-    halo = lax.ppermute(last, "row", up), lax.ppermute(first, "row", down)
+    halo = lax.ppermute(first, "row", down), lax.ppermute(last, "row", up)
     product = band_product_split(intersection, vectors, halo, owners)
     grouped = lax.all_to_all(product, "row", 0, 0, tiled=True).reshape(vectors.shape)
 

time: 97.8 us -> 95.7 us (0.979)
  waiting for transfers between devices: 18.7 us -> 15.1 us
  starting transfers between devices: 34.1 us -> 35.4 us
    all_to_all x1, starting transfers between devices: 7.24 us -> 11.7 us  [local(): lax.all_to_all(product, 'row', 0, 0, tiled=True).reshape(vectors.shape)]
    ppermute x14, starting transfers between devices: 18 us -> 14.2 us  [swap_with(): return lax.ppermute(value, axis, [(i, i ^ distance) for i in range(size)])]
    all_to_all x1, waiting for transfers between devices: 7.09 us -> 3.6 us  [local(): lax.all_to_all(product, 'row', 0, 0, tiled=True).reshape(vectors.shape)]
    ppermute x14, waiting for transfers between devices: 3.18 us -> 5.87 us  [swap_with(): return lax.ppermute(value, axis, [(i, i ^ distance) for i in range(size)])]
    ppermute x2, waiting for transfers between devices: 4.1 us -> 2.19 us  [local(): halo = (lax.ppermute(first, 'row', down), lax.ppermute(last, 'row', up))]
    unnamed x28 -> x26, local copies, waits for them, and re-layouts: 3.32 us -> 3.31 us
  transfers between devices with their start and end apart: 19 -> 19, of which waited for: 5 -> 9; matrix products, arithmetic and copies ran while one was open for 0% -> 0% of each run, Pallas kernels for 35% -> 36%
where the time goes in v3:
time: 95.7 us; the launch traced here: 95.3 us
  Pallas kernels  41 us (43%)
  starting transfers between devices  35.4 us (37%)
  waiting for transfers between devices  15.1 us (16%)
  local copies, waits for them, and re-layouts  3.31 us (3%)
    ppermute x14, starting transfers between devices, swap_with(): return lax.ppermute(value, axis, [(i, i ^ distance) for i in range(size)])  14.2 us
    all_to_all x1, starting transfers between devices, local(): lax.all_to_all(product, 'row', 0, 0, tiled=True).reshape(vectors.shape)  11.7 us
    pallas_call x2, Pallas kernels, invert_panel(): pl.pallas_call(functools.partial(invert_kernel, panel, owners, shares), o...  8.72 us
    pallas_call x1, Pallas kernels, band_product_split(): pl.pallas_call(band_kernel, out_shape=shaped(owners, rows // owners, colu...  8.32 us
    ppermute x2, starting transfers between devices, local(): halo = (lax.ppermute(first, 'row', down), lax.ppermute(last, 'row', up))  6.86 us
    ppermute x14, waiting for transfers between devices, swap_with(): return lax.ppermute(value, axis, [(i, i ^ distance) for i in range(size)])  5.87 us
    pallas_call x1, Pallas kernels, last_solve(): pl.pallas_call(functools.partial(last_kernel, owners, tile_rows), out_sha...  4.52 us
    pallas_call x1, Pallas kernels, halve_last(): pl.pallas_call(functools.partial(halve_kernel, tile_rows), out_shape=[sha...  4.03 us
  transfers between devices with their start and end apart: 19, of which 9 were waited for; matrix products, arithmetic and copies ran while one was open for 0% of the time, Pallas kernels for 36%

profile of v3, /device:TPU:0, one launch (start us, length us, event | category | flops | bytes accessed | tf_op | source)
XLA Modules:
  0.0 95.3 jit_solution(11388225551290232687)
XLA Ops:
  0.0 0.1 pad_add_fusion.place_ref.after_ref
  0.1 2.5 %first_sends.1 = (f32[2,16,2304]{2,1,0:T(8,128)}, f32[512,128]{1,0:T(8,128)S(1)}, f32[512,128]{1,0:T(8,128)S(1)}) custom-call(s32[2]{0:T(128)S(1)} %pad_add_fusion.place_ref.after_ref, f32[2048,2048]{1,0:T(8,128)} %factor_ref.5, f32[2048,128]{1,0:T(8,128)} %vec_ref.3), custom_call_target="tpu_custom_call" | custom-call | bytes 4194304 | tf_op jit(solution)/shard_map/first_sends/pallas_call | solution.py:112
  2.6 1.3 %collective-permute-start = (f32[512,128]{1,0:T(8,128)S(1)}, f32[512,128]{1,0:T(8,128)S(1)}, u32[]{:S(2)}, u32[]{:S(2)}) collective-permute-start(f32[512,128]{1,0:T(8,128)S(1)} %get-tuple-element.27), channel_id=1, source_target_pairs={{4,0},{8,4},{12,8},{5,1},{9,5},{13,9},{6,2},{10,6},{14,10},{7,3},{... | collective-permute-start | bytes 786440 | tf_op jit(solution)/shard_map/ppermute | solution.py:609
  3.9 5.6 %collective-permute-start.1 = (f32[512,128]{1,0:T(8,128)S(1)}, f32[512,128]{1,0:T(8,128)S(1)}, u32[]{:S(2)}, u32[]{:S(2)}) collective-permute-start(f32[512,128]{1,0:T(8,128)S(1)} %get-tuple-element.28), channel_id=1, source_target_pairs={{0,4},{4,8},{8,12},{1,5},{5,9},{9,13},{2,6},{6,10},{10,14},{3,7},{... | collective-permute-start | bytes 786440 | tf_op jit(solution)/shard_map/ppermute | solution.py:609
  9.5 3.1 %collective-permute-start.6 = (f32[2,16,2304]{2,1,0:T(8,128)}, f32[2,16,2304]{2,1,0:T(8,128)S(1)}, u32[]{:S(2)}, u32[]{:S(2)}) collective-permute-start(f32[2,16,2304]{2,1,0:T(8,128)} %get-tuple-element.32), channel_id=1, source_target_pairs={{0,8},{4,12},{8,0},{12,4},{1,9},{5,13},{9,1},{13,5},{2,10},{6,14},... | collective-permute-start | bytes 884744 | tf_op jit(solution)/shard_map/ppermute | solution.py:586
  12.5 0.0 collective-permute-start.5
  12.6 1.4 %collective-permute-start.7 = (f32[2,16,2304]{2,1,0:T(8,128)}, f32[2,16,2304]{2,1,0:T(8,128)}, u32[]{:S(2)}, u32[]{:S(2)}) collective-permute-start(f32[2,16,2304]{2,1,0:T(8,128)} %get-tuple-element.32), channel_id=1, source_target_pairs={{4,8},{8,4},{5,9},{9,5},{6,10},{10,6},{7,11},{11,7},{20,24},{24,20... | collective-permute-start | bytes 884744 | tf_op jit(solution)/shard_map/ppermute | solution.py:190
  13.9 0.0 collective-permute-done.after_ref
  13.9 2.2 %collective-permute-done.1.before_ref = f32[512,128]{1,0:T(8,128)S(1)} collective-permute-done((f32[512,128]{1,0:T(8,128)S(1)}, f32[512,128]{1,0:T(8,128)S(1)}, u32[]{:S(2)}, u32[]{:S(2)}) %collective-permute-start.1) | collective-permute-done | bytes 262176 | tf_op jit(solution)/shard_map/ppermute | solution.py:609
  16.1 8.3 %band_product_split.1.after_ref = f32[4,512,128]{2,1,0:T(8,128)} custom-call(f32[2048,1536]{1,0:T(8,128)} %inter_ref.1, f32[2048,128]{1,0:T(8,128)} %vec_ref.3, f32[512,128]{1,0:T(8,128)S(1)} %collective-permute-done.after_ref, f32[512,128]{1,0:T(8,128)S(1)} %collective-permute-done.1.before_ref), custom_call_target="tpu_custom_call" | custom-call | flops 3221225472 | bytes 12582912 | tf_op jit(solution)/shard_map/band_product_split/pallas_call | solution.py:151
  24.5 11.7 %all-to-all-start = ((f32[4,512,128]{2,1,0:T(8,128)}), f32[4,512,128]{2,1,0:T(8,128)S(1)}, u32[]{:S(2)}, u32[]{:S(2)}) async-start(f32[4,512,128]{2,1,0:T(8,128)} %band_product_split.1.after_ref), calls=%async_computation | async-start | bytes 2097152 | tf_op jit(solution)/shard_map/all_to_all | solution.py:611
  36.2 1.0 %own_weights.1 = (f32[256,128]{1,0:T(8,128)S(1)}, f32[256,128]{1,0:T(8,128)S(1)}) custom-call(s32[2]{0:T(128)S(1)} %pad_add_fusion.place_ref.after_ref, f32[4,512,128]{2,1,0:T(8,128)} %band_product_split.1.after_ref, s32[8,128]{1,0:T(8,128)S(1)} %bitcast.9, f32[8,256]{1,0:T(8,128)S(1)} %reshape.13.diag_ref, f32[8,128]{1,0:T(8,128)S(1)} %bitcast.10), custom_call_target="tpu_custom_call" | custom-call | flops 137438953472 | tf_op jit(solution)/shard_map/own_weights/pallas_call | solution.py:420
  37.1 0.0 collective-permute-done.6.value_ref
  37.2 0.6 copy-done.3
  37.8 1.3 %collective-permute-start.8 = (f32[2,16,2304]{2,1,0:T(8,128)S(1)}, f32[2,16,2304]{2,1,0:T(8,128)S(1)}, u32[]{:S(2)}, u32[]{:S(2)}) collective-permute-start(f32[2,16,2304]{2,1,0:T(8,128)S(1)} %pass_on.3.across_ref), channel_id=1, source_target_pairs={{4,0},{8,12},{5,1},{9,13},{6,2},{10,14},{7,3},{11,15},{20,16},{24,... | collective-permute-start | bytes 884744 | tf_op jit(solution)/shard_map/ppermute | solution.py:191
  39.1 4.0 %halve_last.1 = (bf16[3,2,512,1024]{3,2,1,0:T(8,128)(2,1)S(1)}, f32[2,256,1024]{2,1,0:T(8,128)S(1)}, bf16[2,256,1024]{2,1,0:T(8,128)(2,1)S(1)}) custom-call(f32[2048,2048]{1,0:T(8,128)} %factor_ref.5, f32[256,128]{1,0:T(8,128)S(1)} %get-tuple-element.29.after_ref.refs_9_), custom_call_target="tpu_custom_call" | custom-call | flops 1073741824 | bytes 12582912 | tf_op jit(solution)/shard_map/halve_last/pallas_call | solution.py:462
  43.1 2.6 %copy-done = bf16[3,2,512,1024]{3,2,1,0:T(8,128)(2,1)} copy-done((bf16[3,2,512,1024]{3,2,1,0:T(8,128)(2,1)}, bf16[3,2,512,1024]{3,2,1,0:T(8,128)(2,1)S(1)}, u32[]{:S(2)}) %copy-start) | copy-done | bytes 6291480
  45.8 0.0 collective-permute-done.5.near_ref
  45.8 0.0 collective-permute-done.7.inner_ref
  45.8 3.4 %collective-permute-done.8.outer_ref = f32[2,16,2304]{2,1,0:T(8,128)S(1)} collective-permute-done((f32[2,16,2304]{2,1,0:T(8,128)S(1)}, f32[2,16,2304]{2,1,0:T(8,128)S(1)}, u32[]{:S(2)}, u32[]{:S(2)}) %collective-permute-start.8) | collective-permute-done | bytes 294944 | tf_op jit(solution)/shard_map/ppermute | solution.py:191
  49.2 2.1 %stack.13 = (f32[3,16,2304]{2,1,0:T(8,128)}, f32[3,16,2304]{2,1,0:T(8,128)}) custom-call(s32[2]{0:T(128)S(1)} %pad_add_fusion.place_ref.after_ref, f32[2,16,2304]{2,1,0:T(8,128)} %collective-permute-done.5.near_ref, f32[2,16,2304]{2,1,0:T(8,128)S(1)} %pass_on.3.across_ref, f32[2,16,2304]{2,1,0:T(8,128)} %collective-permute-done.7.inner_ref, ...), custom_call_target="tpu_custom_call" | custom-call | tf_op jit(solution)/shard_map/stack/pallas_call | solution.py:214
  51.3 1.5 %collective-permute-start.10 = (f32[3,16,2304]{2,1,0:T(8,128)}, f32[3,16,2304]{2,1,0:T(8,128)}, u32[]{:S(2)}, u32[]{:S(2)}) collective-permute-start(f32[3,16,2304]{2,1,0:T(8,128)} %get-tuple-element.33.refs_0_), channel_id=1, source_target_pairs={{0,2},{1,3},{2,0},{3,1},{4,6},{5,7},{6,4},{7,5},{8,10},{9,11},{10,... | collective-permute-start | bytes 1327112 | tf_op jit(solution)/shard_map/ppermute | solution.py:586
  52.8 3.6 %all-to-all-done = f32[4,512,128]{2,1,0:T(8,128)S(1)} async-done(((f32[4,512,128]{2,1,0:T(8,128)}), f32[4,512,128]{2,1,0:T(8,128)S(1)}, u32[]{:S(2)}, u32[]{:S(2)}) %all-to-all-start) | async-done | bytes 1048608 | tf_op jit(solution)/shard_map/all_to_all | solution.py:611
  56.4 0.9 order_rows.2.after_ref.refs_0_
  57.3 2.6 %collective-permute-done.10.value_ref = f32[3,16,2304]{2,1,0:T(8,128)} collective-permute-done((f32[3,16,2304]{2,1,0:T(8,128)}, f32[3,16,2304]{2,1,0:T(8,128)}, u32[]{:S(2)}, u32[]{:S(2)}) %collective-permute-start.10) | collective-permute-done | bytes 442400 | tf_op jit(solution)/shard_map/ppermute | solution.py:586
  60.0 0.0 collective-permute-start.11
  60.0 1.5 %collective-permute-start.16 = (f32[3,16,2304]{2,1,0:T(8,128)}, f32[3,16,2304]{2,1,0:T(8,128)S(1)}, u32[]{:S(2)}, u32[]{:S(2)}) collective-permute-start(f32[3,16,2304]{2,1,0:T(8,128)} %get-tuple-element.42.refs_0_), channel_id=1, source_target_pairs={{0,2},{1,3},{2,0},{3,1},{4,6},{5,7},{6,4},{7,5},{8,10},{9,11},{10,... | collective-permute-start | bytes 1327112 | tf_op jit(solution)/shard_map/ppermute | solution.py:586
  61.4 0.2 collective-permute-start.15
  61.7 2.0 %collective-permute-start.2 = (f32[256,128]{1,0:T(8,128)S(1)}, f32[256,128]{1,0:T(8,128)S(1)}, u32[]{:S(2)}, u32[]{:S(2)}) collective-permute-start(f32[256,128]{1,0:T(8,128)S(1)} %order_rows.2.after_ref.refs_0_), channel_id=1, source_target_pairs={{0,8},{4,12},{8,0},{12,4},{1,9},{5,13},{9,1},{13,5},{2,10},{6,14},... | collective-permute-start | bytes 393224 | tf_op jit(solution)/shard_map/ppermute | solution.py:586
  63.7 0.1 collective-permute-start.3
  63.8 0.0 collective-permute-done.11.refs_3_
  63.8 1.4 %collective-permute-start.4 = (f32[256,128]{1,0:T(8,128)S(1)}, f32[256,128]{1,0:T(8,128)S(1)}, u32[]{:S(2)}, u32[]{:S(2)}) collective-permute-start(f32[256,128]{1,0:T(8,128)S(1)} %order_rows.2.after_ref.refs_0_), channel_id=1, source_target_pairs={{0,4},{4,0},{8,12},{12,8},{1,5},{5,1},{9,13},{13,9},{2,6},{6,2},{1... | collective-permute-start | bytes 393224 | tf_op jit(solution)/shard_map/ppermute | solution.py:586
  65.2 4.4 %invert_panel.2 = (bf16[1024,1024]{1,0:T(8,128)(2,1)S(1)}, bf16[1024,1024]{1,0:T(8,128)(2,1)S(1)}, bf16[4,256,256]{2,1,0:T(8,128)(2,1)S(1)}, bf16[4,256,256]{2,1,0:T(8,128)(2,1)S(1)}) custom-call(s32[2]{0:T(128)S(1)} %pad_add_fusion.place_ref.after_ref, f32[256,128]{1,0:T(8,128)S(1)} %order_rows.2.after_ref.refs_0_, ...), custom_call_target="tpu_custom_call" | custom-call | flops 137438953472 | bytes 12582912 | tf_op jit(solution)/shard_map/invert_panel/pallas_call | solution.py:295
  69.6 2.6 %order_rows.3 = (f32[256,128]{1,0:T(8,128)S(1)}, f32[1536,128]{1,0:T(8,128)S(1)}) custom-call(s32[2048]{0:T(1024)S(1)} %copy-done.5, f32[2048,128]{1,0:T(8,128)S(1)} %bitcast.6, bf16[4,256,256]{2,1,0:T(8,128)(2,1)S(1)} %get-tuple-element.36.after_ref.refs_6_), custom_call_target="tpu_custom_call" | custom-call | bytes 2097152 | tf_op jit(solution)/shard_map/order_rows/pallas_call | solution.py:328
  72.2 0.6 collective-permute-done.16.value_ref
  72.8 0.7 collective-permute-done.2.refs_1_
  73.5 1.3 %collective-permute-done.4.refs_3_ = f32[256,128]{1,0:T(8,128)S(1)} collective-permute-done((f32[256,128]{1,0:T(8,128)S(1)}, f32[256,128]{1,0:T(8,128)S(1)}, u32[]{:S(2)}, u32[]{:S(2)}) %collective-permute-start.4) | collective-permute-done | bytes 131104 | tf_op jit(solution)/shard_map/ppermute | solution.py:586
  74.8 2.3 %first_solve.1 = (f32[64,16,128]{2,1,0:T(8,128)S(1)}, f32[256,128]{1,0:T(8,128)S(1)}) custom-call(s32[2]{0:T(128)S(1)} %pad_add_fusion.place_ref.after_ref, f32[256,128]{1,0:T(8,128)S(1)} %order_rows.2.after_ref.refs_0_, f32[256,128]{1,0:T(8,128)S(1)} %collective-permute-done.2.refs_1_, f32[256,128]{1,0:T(8,128)S(1)} %collective-permute-done.3.refs_2_, ...), custom_call_target="tpu_custom_call" | custom-call | flops 137438953472 | bytes 6291456 | tf_op jit(solution)/shard_map/first_solve/pallas_call | solution.py:380
  77.1 3.3 %collective-permute-start.12 = (f32[256,128]{1,0:T(8,128)S(1)}, f32[256,128]{1,0:T(8,128)S(1)}, u32[]{:S(2)}, u32[]{:S(2)}) collective-permute-start(f32[256,128]{1,0:T(8,128)S(1)} %get-tuple-element.40.refs_0_), channel_id=1, source_target_pairs={{0,8},{4,12},{8,0},{12,4},{1,9},{5,13},{9,1},{13,5},{2,10},{6,14},... | collective-permute-start | bytes 393224 | tf_op jit(solution)/shard_map/ppermute | solution.py:586
  80.4 1.2 %collective-permute-start.13 = (f32[256,128]{1,0:T(8,128)S(1)}, f32[256,128]{1,0:T(8,128)S(1)}, u32[]{:S(2)}, u32[]{:S(2)}) collective-permute-start(f32[256,128]{1,0:T(8,128)S(1)} %get-tuple-element.40.refs_0_), channel_id=1, source_target_pairs={{0,12},{4,8},{8,4},{12,0},{1,13},{5,9},{9,5},{13,1},{2,14},{6,10},... | collective-permute-start | bytes 393224 | tf_op jit(solution)/shard_map/ppermute | solution.py:586
  81.6 0.0 collective-permute-start.14
  81.6 3.9 %middle_update.1.refs_11_ = f32[1536,128]{1,0:T(8,128)S(1)} custom-call(f32[2048,2048]{1,0:T(8,128)} %factor_ref.5, f32[1536,128]{1,0:T(8,128)S(1)} %get-tuple-element.48.rest_ref, f32[64,16,128]{2,1,0:T(8,128)S(1)} %get-tuple-element.41.after_ref.y_ref.refs_8_), custom_call_target="tpu_custom_call" | custom-call | flops 1610612736 | bytes 8388608 | tf_op jit(solution)/shard_map/middle_update/pallas_call | solution.py:502
  85.6 0.0 collective-permute-done.15.refs_1_
  85.6 4.3 %invert_panel.3 = (bf16[1024,1024]{1,0:T(8,128)(2,1)S(1)}, bf16[1024,1024]{1,0:T(8,128)(2,1)S(1)}, bf16[4,256,256]{2,1,0:T(8,128)(2,1)S(1)}, bf16[4,256,256]{2,1,0:T(8,128)(2,1)S(1)}) custom-call(s32[2]{0:T(128)S(1)} %pad_add_fusion.place_ref.after_ref, f32[64,16,128]{2,1,0:T(8,128)S(1)} %get-tuple-element.41.after_ref.y_ref.refs_8_, ...), custom_call_target="tpu_custom_call" | custom-call | flops 1073741824 | bytes 12582912 | tf_op jit(solution)/shard_map/invert_panel/pallas_call | solution.py:295
  89.9 0.5 collective-permute-done.12.refs_1_
  90.4 0.0 collective-permute-done.13.refs_2_
  90.4 0.1 collective-permute-done.14.refs_3_
  90.6 4.5 %last_solve.1 = f32[2048,128]{1,0:T(8,128)} custom-call(s32[2]{0:T(128)S(1)} %pad_add_fusion.place_ref.after_ref, bf16[3,2,512,1024]{3,2,1,0:T(8,128)(2,1)S(1)} %bitcast.8, f32[256,128]{1,0:T(8,128)S(1)} %get-tuple-element.40.refs_0_, f32[256,128]{1,0:T(8,128)S(1)} %collective-permute-done.12.refs_1_, f32[256,128]{1,0:T(8,128)S(1)} %collective-permute-done.13.refs_2_, ...), custom_call_target="tpu_custom_call" | custom-call | flops 2147483648 | bytes 12582912 | tf_op jit(solution)/shard_map/last_solve/pallas_call | solution.py:567
  (34 shorter events, 0.1 us)
Async XLA Ops:
  0.1 13.9 %copy-start.10 = (f32[2048]{0:T(1024)S(1)}, f32[2048]{0:T(1024)}, u32[]{:S(2)}) copy-start(f32[2048]{0:T(1024)} %param.12) | copy-start | bytes 24580
  2.6 11.4 %collective-permute-start = (f32[512,128]{1,0:T(8,128)S(1)}, f32[512,128]{1,0:T(8,128)S(1)}, u32[]{:S(2)}, u32[]{:S(2)}) collective-permute-start(f32[512,128]{1,0:T(8,128)S(1)} %get-tuple-element.27), channel_id=1, source_target_pairs={{4,0},{8,4},{12,8},{5,1},{9,5},{13,9},{6,2},{10,6},{14,10},{7,3},{... | collective-permute-start | bytes 786440 | tf_op jit(solution)/shard_map/ppermute | solution.py:609
  3.9 12.3 %collective-permute-start.1 = (f32[512,128]{1,0:T(8,128)S(1)}, f32[512,128]{1,0:T(8,128)S(1)}, u32[]{:S(2)}, u32[]{:S(2)}) collective-permute-start(f32[512,128]{1,0:T(8,128)S(1)} %get-tuple-element.28), channel_id=1, source_target_pairs={{0,4},{4,8},{8,12},{1,5},{5,9},{9,13},{2,6},{6,10},{10,14},{3,7},{... | collective-permute-start | bytes 786440 | tf_op jit(solution)/shard_map/ppermute | solution.py:609
  9.5 27.7 %collective-permute-start.6 = (f32[2,16,2304]{2,1,0:T(8,128)}, f32[2,16,2304]{2,1,0:T(8,128)S(1)}, u32[]{:S(2)}, u32[]{:S(2)}) collective-permute-start(f32[2,16,2304]{2,1,0:T(8,128)} %get-tuple-element.32), channel_id=1, source_target_pairs={{0,8},{4,12},{8,0},{12,4},{1,9},{5,13},{9,1},{13,5},{2,10},{6,14},... | collective-permute-start | bytes 884744 | tf_op jit(solution)/shard_map/ppermute | solution.py:586
  12.5 33.2 %collective-permute-start.5 = (f32[2,16,2304]{2,1,0:T(8,128)}, f32[2,16,2304]{2,1,0:T(8,128)}, u32[]{:S(2)}, u32[]{:S(2)}) collective-permute-start(f32[2,16,2304]{2,1,0:T(8,128)} %get-tuple-element.32), channel_id=1, source_target_pairs={{0,4},{4,0},{8,12},{12,8},{1,5},{5,1},{9,13},{13,9},{2,6},{6,2},{1... | collective-permute-start | bytes 884744 | tf_op jit(solution)/shard_map/ppermute | solution.py:586
  12.6 33.2 %collective-permute-start.7 = (f32[2,16,2304]{2,1,0:T(8,128)}, f32[2,16,2304]{2,1,0:T(8,128)}, u32[]{:S(2)}, u32[]{:S(2)}) collective-permute-start(f32[2,16,2304]{2,1,0:T(8,128)} %get-tuple-element.32), channel_id=1, source_target_pairs={{4,8},{8,4},{5,9},{9,5},{6,10},{10,6},{7,11},{11,7},{20,24},{24,20... | collective-permute-start | bytes 884744 | tf_op jit(solution)/shard_map/ppermute | solution.py:190
  24.5 11.7 %copy-start.8 = (s32[1024]{0:T(1024)S(1)}, s32[1024]{0:T(1024)}, u32[]{:S(2)}) copy-start(s32[1024]{0:T(1024)} %param.11) | copy-start | bytes 12292
  24.5 11.7 %copy-start.9 = (f32[1024]{0:T(1024)S(1)}, f32[1024]{0:T(1024)}, u32[]{:S(2)}) copy-start(f32[1024]{0:T(1024)} %param.13) | copy-start | bytes 12292
  24.5 31.9 %all-to-all-start = ((f32[4,512,128]{2,1,0:T(8,128)}), f32[4,512,128]{2,1,0:T(8,128)S(1)}, u32[]{:S(2)}, u32[]{:S(2)}) async-start(f32[4,512,128]{2,1,0:T(8,128)} %band_product_split.1.after_ref), calls=%async_computation | async-start | bytes 2097152 | tf_op jit(solution)/shard_map/all_to_all | solution.py:611
  37.1 0.7 copy-start.3
  37.1 6.0 %copy-start.1 = (f32[256,128]{1,0:T(8,128)}, f32[256,128]{1,0:T(8,128)S(1)}, u32[]{:S(2)}) copy-start(f32[256,128]{1,0:T(8,128)S(1)} %get-tuple-element.29.after_ref.refs_9_) | copy-start | bytes 393220
  37.8 11.4 %collective-permute-start.8 = (f32[2,16,2304]{2,1,0:T(8,128)S(1)}, f32[2,16,2304]{2,1,0:T(8,128)S(1)}, u32[]{:S(2)}, u32[]{:S(2)}) collective-permute-start(f32[2,16,2304]{2,1,0:T(8,128)S(1)} %pass_on.3.across_ref), channel_id=1, source_target_pairs={{4,0},{8,12},{5,1},{9,13},{6,2},{10,14},{7,3},{11,15},{20,16},{24,... | collective-permute-start | bytes 884744 | tf_op jit(solution)/shard_map/ppermute | solution.py:191
  43.1 2.7 %copy-start = (bf16[3,2,512,1024]{3,2,1,0:T(8,128)(2,1)}, bf16[3,2,512,1024]{3,2,1,0:T(8,128)(2,1)S(1)}, u32[]{:S(2)}) copy-start(bf16[3,2,512,1024]{3,2,1,0:T(8,128)(2,1)S(1)} %get-tuple-element.30.left_ref) | copy-start | bytes 18874372
  45.8 7.0 %copy-start.6 = (bf16[2,256,1024]{2,1,0:T(8,128)(2,1)}, bf16[2,256,1024]{2,1,0:T(8,128)(2,1)S(1)}, u32[]{:S(2)}) copy-start(bf16[2,256,1024]{2,1,0:T(8,128)(2,1)S(1)} %get-tuple-element.38.refs_8_) | copy-start | bytes 3145732
  45.8 10.6 %copy-start.5 = (s32[2048]{0:T(1024)S(1)}, s32[2048]{0:T(1024)}, u32[]{:S(2)}) copy-start(s32[2048]{0:T(1024)} %pivot_ref.3) | copy-start | bytes 24580
  51.3 8.6 %collective-permute-start.10 = (f32[3,16,2304]{2,1,0:T(8,128)}, f32[3,16,2304]{2,1,0:T(8,128)}, u32[]{:S(2)}, u32[]{:S(2)}) collective-permute-start(f32[3,16,2304]{2,1,0:T(8,128)} %get-tuple-element.33.refs_0_), channel_id=1, source_target_pairs={{0,2},{1,3},{2,0},{3,1},{4,6},{5,7},{6,4},{7,5},{8,10},{9,11},{10,... | collective-permute-start | bytes 1327112 | tf_op jit(solution)/shard_map/ppermute | solution.py:586
  52.8 10.9 %collective-permute-start.9 = (f32[3,16,2304]{2,1,0:T(8,128)}, f32[3,16,2304]{2,1,0:T(8,128)}, u32[]{:S(2)}, u32[]{:S(2)}) collective-permute-start(f32[3,16,2304]{2,1,0:T(8,128)} %get-tuple-element.33.refs_0_), channel_id=1, source_target_pairs={{0,1},{1,0},{2,3},{3,2},{4,5},{5,4},{6,7},{7,6},{8,9},{9,8},{10,11... | collective-permute-start | bytes 1327112 | tf_op jit(solution)/shard_map/ppermute | solution.py:586
  60.0 3.8 %collective-permute-start.11 = (f32[3,16,2304]{2,1,0:T(8,128)}, f32[3,16,2304]{2,1,0:T(8,128)S(1)}, u32[]{:S(2)}, u32[]{:S(2)}) collective-permute-start(f32[3,16,2304]{2,1,0:T(8,128)} %pass_on.4.refs_2_), channel_id=1, source_target_pairs={{0,1},{1,0},{2,3},{3,2},{4,5},{5,4},{6,7},{7,6},{8,9},{9,8},{10,11... | collective-permute-start | bytes 1327112 | tf_op jit(solution)/shard_map/ppermute | solution.py:586
  60.0 12.8 %collective-permute-start.16 = (f32[3,16,2304]{2,1,0:T(8,128)}, f32[3,16,2304]{2,1,0:T(8,128)S(1)}, u32[]{:S(2)}, u32[]{:S(2)}) collective-permute-start(f32[3,16,2304]{2,1,0:T(8,128)} %get-tuple-element.42.refs_0_), channel_id=1, source_target_pairs={{0,2},{1,3},{2,0},{3,1},{4,6},{5,7},{6,4},{7,5},{8,10},{9,11},{10,... | collective-permute-start | bytes 1327112 | tf_op jit(solution)/shard_map/ppermute | solution.py:586
  61.4 24.1 %collective-permute-start.15 = (f32[3,16,2304]{2,1,0:T(8,128)}, f32[3,16,2304]{2,1,0:T(8,128)}, u32[]{:S(2)}, u32[]{:S(2)}) collective-permute-start(f32[3,16,2304]{2,1,0:T(8,128)} %get-tuple-element.42.refs_0_), channel_id=1, source_target_pairs={{0,1},{1,0},{2,3},{3,2},{4,5},{5,4},{6,7},{7,6},{8,9},{9,8},{10,11... | collective-permute-start | bytes 1327112 | tf_op jit(solution)/shard_map/ppermute | solution.py:586
  61.7 11.8 %collective-permute-start.2 = (f32[256,128]{1,0:T(8,128)S(1)}, f32[256,128]{1,0:T(8,128)S(1)}, u32[]{:S(2)}, u32[]{:S(2)}) collective-permute-start(f32[256,128]{1,0:T(8,128)S(1)} %order_rows.2.after_ref.refs_0_), channel_id=1, source_target_pairs={{0,8},{4,12},{8,0},{12,4},{1,9},{5,13},{9,1},{13,5},{2,10},{6,14},... | collective-permute-start | bytes 393224 | tf_op jit(solution)/shard_map/ppermute | solution.py:586
  63.7 9.8 %collective-permute-start.3 = (f32[256,128]{1,0:T(8,128)S(1)}, f32[256,128]{1,0:T(8,128)S(1)}, u32[]{:S(2)}, u32[]{:S(2)}) collective-permute-start(f32[256,128]{1,0:T(8,128)S(1)} %order_rows.2.after_ref.refs_0_), channel_id=1, source_target_pairs={{0,12},{4,8},{8,4},{12,0},{1,13},{5,9},{9,5},{13,1},{2,14},{6,10},... | collective-permute-start | bytes 393224 | tf_op jit(solution)/shard_map/ppermute | solution.py:586
  63.8 11.0 %collective-permute-start.4 = (f32[256,128]{1,0:T(8,128)S(1)}, f32[256,128]{1,0:T(8,128)S(1)}, u32[]{:S(2)}, u32[]{:S(2)}) collective-permute-start(f32[256,128]{1,0:T(8,128)S(1)} %order_rows.2.after_ref.refs_0_), channel_id=1, source_target_pairs={{0,4},{4,0},{8,12},{12,8},{1,5},{5,1},{9,13},{13,9},{2,6},{6,2},{1... | collective-permute-start | bytes 393224 | tf_op jit(solution)/shard_map/ppermute | solution.py:586
  69.6 5.2 %copy-start.7 = (bf16[2,256,1024]{2,1,0:T(8,128)(2,1)S(1)}, bf16[2,256,1024]{2,1,0:T(8,128)(2,1)}, u32[]{:S(2)}) copy-start(bf16[2,256,1024]{2,1,0:T(8,128)(2,1)} %copy-done.6) | copy-start | bytes 3145732
  72.8 12.8 %collective-permute-start.17 = (f32[3,16,2304]{2,1,0:T(8,128)S(1)}, f32[3,16,2304]{2,1,0:T(8,128)S(1)}, u32[]{:S(2)}, u32[]{:S(2)}) collective-permute-start(f32[3,16,2304]{2,1,0:T(8,128)S(1)} %pass_on.5.refs_2_), channel_id=1, source_target_pairs={{0,1},{1,0},{2,3},{3,2},{4,5},{5,4},{6,7},{7,6},{8,9},{9,8},{10,11... | collective-permute-start | bytes 1327112 | tf_op jit(solution)/shard_map/ppermute | solution.py:586
  77.1 13.3 %collective-permute-start.12 = (f32[256,128]{1,0:T(8,128)S(1)}, f32[256,128]{1,0:T(8,128)S(1)}, u32[]{:S(2)}, u32[]{:S(2)}) collective-permute-start(f32[256,128]{1,0:T(8,128)S(1)} %get-tuple-element.40.refs_0_), channel_id=1, source_target_pairs={{0,8},{4,12},{8,0},{12,4},{1,9},{5,13},{9,1},{13,5},{2,10},{6,14},... | collective-permute-start | bytes 393224 | tf_op jit(solution)/shard_map/ppermute | solution.py:586
  80.4 10.0 %collective-permute-start.13 = (f32[256,128]{1,0:T(8,128)S(1)}, f32[256,128]{1,0:T(8,128)S(1)}, u32[]{:S(2)}, u32[]{:S(2)}) collective-permute-start(f32[256,128]{1,0:T(8,128)S(1)} %get-tuple-element.40.refs_0_), channel_id=1, source_target_pairs={{0,12},{4,8},{8,4},{12,0},{1,13},{5,9},{9,5},{13,1},{2,14},{6,10},... | collective-permute-start | bytes 393224 | tf_op jit(solution)/shard_map/ppermute | solution.py:586
  81.6 9.0 %collective-permute-start.14 = (f32[256,128]{1,0:T(8,128)S(1)}, f32[256,128]{1,0:T(8,128)S(1)}, u32[]{:S(2)}, u32[]{:S(2)}) collective-permute-start(f32[256,128]{1,0:T(8,128)S(1)} %get-tuple-element.40.refs_0_), channel_id=1, source_target_pairs={{0,4},{4,0},{8,12},{12,8},{1,5},{5,1},{9,13},{13,9},{2,6},{6,2},{1... | collective-permute-start | bytes 393224 | tf_op jit(solution)/shard_map/ppermute | solution.py:586
  81.6 9.0 %slice-start = ((s8[6291456]{0:T(1024)(128)(4,1)}), s8[4194304]{0:T(1024)(128)(4,1)S(1)}, s32[]{:S(2)}) async-start(s8[6291456]{0:T(1024)(128)(4,1)} %bitcast.7), calls=%async_computation.1 | async-start | bytes 8388608
  81.6 9.0 %slice-start.1 = ((s8[6291456]{0:T(1024)(128)(4,1)}), s8[2097152]{0:T(1024)(128)(4,1)S(1)}, s32[]{:S(2)}) async-start(s8[6291456]{0:T(1024)(128)(4,1)} %bitcast.7), calls=%async_computation.2 | async-start | bytes 4194304
  85.6 5.0 %copy-start.2 = (f32[256,128]{1,0:T(8,128)S(1)}, f32[256,128]{1,0:T(8,128)}, u32[]{:S(2)}) copy-start(f32[256,128]{1,0:T(8,128)} %copy-done.1) | copy-start | bytes 393220
  85.6 5.0 %copy-start.4 = (f32[256,128]{1,0:T(8,128)S(1)}, f32[256,128]{1,0:T(8,128)}, u32[]{:S(2)}) copy-start(f32[256,128]{1,0:T(8,128)} %copy-done.3) | copy-start | bytes 393220

commit v4 on v3

--- a/solution.py
+++ b/solution.py
@@ -411,26 +411,25 @@
     return turned
 
 
-def weights_kernel(place_ref, after_ref, sizes_ref, diag_ref, off_ref, keep_ref, swap_ref):
-    keep_ref[...], swap_ref[...] = pivot_weights(place_ref[0], sizes_ref[...], diag_ref[...], off_ref[...])
-
-
-def own_weights(place, pivots, after):
-    weight = shaped(pivots[1].shape[1], HALF)
-    return pl.pallas_call(
-        weights_kernel,
-        out_shape=[weight, weight],
-        in_specs=[IN_SMEM, pl.BlockSpec(memory_space=pl.ANY)] + [IN_VMEM] * len(pivots),
-        out_specs=[IN_VMEM] * 2,
-        compiler_params=params(4),
+def mark_kernel(after_ref, out_ref):
+    out_ref[...] = jnp.zeros_like(out_ref)
+
+
+def mark(after):
+    return pl.pallas_call(
+        mark_kernel,
+        out_shape=shaped(8, HALF),
+        in_specs=[pl.BlockSpec(memory_space=pl.ANY)],
+        out_specs=IN_VMEM,
+        compiler_params=params(1),
         cost_estimate=cost(HEAVY, 0),
-        name="own_weights",
-    )(place, after, *pivots)
+        name="mark",
+    )(after)
 
 
 def halve_kernel(
-    tile_rows, factor_ref, after_ref, out_ref, own_ref, next_ref, left_ref, below_ref, parts_ref, in_sems, out_sems,
-    own_sems,
+    tile_rows, place_ref, factor_ref, sizes_ref, diag_ref, off_ref, after_ref, out_ref, own_ref, next_ref, keep_ref,
+    swap_ref, left_ref, below_ref, parts_ref, in_sems, out_sems, own_sems,
 ):
     tiles = left_ref.shape[0]
     rows = own_ref.shape[1]
@@ -445,6 +444,7 @@
         source = factor_ref.at[pl.ds(panel * rows, rows), pl.ds(panel * PANEL, PANEL)]
         owns.append(pltpu.make_async_copy(source, own_ref.at[panel], own_sems.at[panel]))
         owns[panel].start()
+    keep_ref[...], swap_ref[...] = pivot_weights(place_ref[0], sizes_ref[...], diag_ref[...], off_ref[...])
     below.wait()
     next_ref[0], next_ref[1] = split(below_ref[...])
     for t in range(tiles):
@@ -456,18 +456,21 @@
         copy.wait()
 
 
-def halve_last(factor, panel_rows, after):
+def halve_last(place, factor, pivots, panel_rows, after):
     tile_rows = PANELS * panel_rows
     tiles = factor.shape[0] // tile_rows - 1
+    weight = shaped(pivots[1].shape[1], HALF)
     return pl.pallas_call(
         functools.partial(halve_kernel, tile_rows),
         out_shape=[
             shaped(tiles, 2, tile_rows, PANEL, dtype=BF16),
             shaped(PANELS, panel_rows, PANEL),
             shaped(2, panel_rows, PANEL, dtype=BF16),
+            weight,
+            weight,
         ],
-        in_specs=[IN_HBM, pl.BlockSpec(memory_space=pl.ANY)],
-        out_specs=[IN_HBM, IN_VMEM, IN_VMEM],
+        in_specs=[IN_SMEM, IN_HBM] + [IN_VMEM] * len(pivots) + [pl.BlockSpec(memory_space=pl.ANY)],
+        out_specs=[IN_HBM] + [IN_VMEM] * 4,
         scratch_shapes=[
             pltpu.VMEM((tiles, tile_rows, PANEL), F32),
             pltpu.VMEM((panel_rows, PANEL), F32),
@@ -479,7 +482,7 @@
         compiler_params=params(18),
         cost_estimate=cost(LIGHT, 12 * MIB),
         name="halve_last",
-    )(factor, after)
+    )(place, factor, *pivots, after)
 
 
 def middle_kernel(tile_rows, factor_ref, rest_ref, y_ref, out_ref, wide_ref, left_ref, sems):
@@ -616,10 +619,10 @@
 
     tile_rows = PANELS * panel_rows
     pivots = [a.reshape(pivot_diag.shape[0] // DIAG, -1) for a in (pivot_sizes, pivot_diag, pivot_off)]
-    keep, swap = own_weights(place, pivots, product)
-    direct = from_others(share, keep)
+    started = mark(product)
+    direct = from_others(share, started)
     (first,) = order_rows(0, [panel_rows], pivot_rows, grouped, place)
-    parts, own, left = halve_last(factor, panel_rows, keep)
+    parts, own, left, keep, swap = halve_last(place, factor, pivots, panel_rows, started)
     stacked = stack(place, direct, own)
     shared = share_out(stacked[0], first)
     prepared = invert_panel(0, place, own, shared, owners, shares, first, HEAVY)

time: 95.7 us -> 95.7 us (level)
  waiting for transfers between devices: 15.1 us -> 16.1 us
    ppermute x1, waiting for transfers between devices: 3.41 us -> 4.38 us  [from_others(): outer = lax.ppermute(across, 'row', [(i, i ^ 1) for i, _ in middle])]
    pallas_call x1, Pallas kernels: 0.96 us -> 0.01 us  [mark(): pl.pallas_call(mark_kernel, out_shape=shaped(8, HALF), in_specs=[pl.Block...]
  transfers between devices with their start and end apart: 19 -> 19, of which waited for: 9 -> 9; matrix products, arithmetic and copies ran while one was open for 0% -> 0% of each run, Pallas kernels for 36% -> 35%
where the time goes in v4:
time: 95.7 us; the launch traced here: 95.3 us
  Pallas kernels  40.7 us (43%)
  starting transfers between devices  35.4 us (37%)
  waiting for transfers between devices  16.1 us (17%)
  local copies, waits for them, and re-layouts  2.68 us (3%)
    ppermute x14, starting transfers between devices, swap_with(): return lax.ppermute(value, axis, [(i, i ^ distance) for i in range(size)])  14.3 us
    all_to_all x1, starting transfers between devices, local(): lax.all_to_all(product, 'row', 0, 0, tiled=True).reshape(vectors.shape)  11.6 us
    pallas_call x2, Pallas kernels, invert_panel(): pl.pallas_call(functools.partial(invert_kernel, panel, owners, shares), o...  8.72 us
    pallas_call x1, Pallas kernels, band_product_split(): pl.pallas_call(band_kernel, out_shape=shaped(owners, rows // owners, colu...  8.32 us
    ppermute x2, starting transfers between devices, local(): halo = (lax.ppermute(first, 'row', down), lax.ppermute(last, 'row', up))  6.86 us
    ppermute x14, waiting for transfers between devices, swap_with(): return lax.ppermute(value, axis, [(i, i ^ distance) for i in range(size)])  5.89 us
    pallas_call x1, Pallas kernels, halve_last(): pl.pallas_call(functools.partial(halve_kernel, tile_rows), out_shape=[sha...  4.58 us
    pallas_call x1, Pallas kernels, last_solve(): pl.pallas_call(functools.partial(last_kernel, owners, tile_rows), out_sha...  4.54 us
  transfers between devices with their start and end apart: 19, of which 9 were waited for; matrix products, arithmetic and copies ran while one was open for 0% of the time, Pallas kernels for 35%

profile of v4, /device:TPU:0, one launch (start us, length us, event | category | flops | bytes accessed | tf_op | source)
XLA Modules:
  0.0 95.3 jit_solution(15760745167282827497)
XLA Ops:
  0.0 0.1 pad_add_fusion.place_ref.after_ref
  0.1 2.5 %first_sends.1 = (f32[2,16,2304]{2,1,0:T(8,128)}, f32[512,128]{1,0:T(8,128)S(1)}, f32[512,128]{1,0:T(8,128)S(1)}) custom-call(s32[2]{0:T(128)S(1)} %pad_add_fusion.place_ref.after_ref, f32[2048,2048]{1,0:T(8,128)} %factor_ref.5, f32[2048,128]{1,0:T(8,128)} %vec_ref.3), custom_call_target="tpu_custom_call" | custom-call | bytes 4194304 | tf_op jit(solution)/shard_map/first_sends/pallas_call | solution.py:112
  2.6 1.3 %collective-permute-start = (f32[512,128]{1,0:T(8,128)S(1)}, f32[512,128]{1,0:T(8,128)S(1)}, u32[]{:S(2)}, u32[]{:S(2)}) collective-permute-start(f32[512,128]{1,0:T(8,128)S(1)} %get-tuple-element.27), channel_id=1, source_target_pairs={{4,0},{8,4},{12,8},{5,1},{9,5},{13,9},{6,2},{10,6},{14,10},{7,3},{... | collective-permute-start | bytes 786440 | tf_op jit(solution)/shard_map/ppermute | solution.py:612
  3.9 5.6 %collective-permute-start.1 = (f32[512,128]{1,0:T(8,128)S(1)}, f32[512,128]{1,0:T(8,128)S(1)}, u32[]{:S(2)}, u32[]{:S(2)}) collective-permute-start(f32[512,128]{1,0:T(8,128)S(1)} %get-tuple-element.28), channel_id=1, source_target_pairs={{0,4},{4,8},{8,12},{1,5},{5,9},{9,13},{2,6},{6,10},{10,14},{3,7},{... | collective-permute-start | bytes 786440 | tf_op jit(solution)/shard_map/ppermute | solution.py:612
  9.4 3.1 %collective-permute-start.6 = (f32[2,16,2304]{2,1,0:T(8,128)}, f32[2,16,2304]{2,1,0:T(8,128)S(1)}, u32[]{:S(2)}, u32[]{:S(2)}) collective-permute-start(f32[2,16,2304]{2,1,0:T(8,128)} %get-tuple-element.31), channel_id=1, source_target_pairs={{0,8},{4,12},{8,0},{12,4},{1,9},{5,13},{9,1},{13,5},{2,10},{6,14},... | collective-permute-start | bytes 884744 | tf_op jit(solution)/shard_map/ppermute | solution.py:589
  12.5 0.0 collective-permute-start.5
  12.5 1.4 %collective-permute-start.7 = (f32[2,16,2304]{2,1,0:T(8,128)}, f32[2,16,2304]{2,1,0:T(8,128)}, u32[]{:S(2)}, u32[]{:S(2)}) collective-permute-start(f32[2,16,2304]{2,1,0:T(8,128)} %get-tuple-element.31), channel_id=1, source_target_pairs={{4,8},{8,4},{5,9},{9,5},{6,10},{10,6},{7,11},{11,7},{20,24},{24,20... | collective-permute-start | bytes 884744 | tf_op jit(solution)/shard_map/ppermute | solution.py:190
  13.9 0.0 collective-permute-done.after_ref
  13.9 2.2 %collective-permute-done.1.before_ref = f32[512,128]{1,0:T(8,128)S(1)} collective-permute-done((f32[512,128]{1,0:T(8,128)S(1)}, f32[512,128]{1,0:T(8,128)S(1)}, u32[]{:S(2)}, u32[]{:S(2)}) %collective-permute-start.1) | collective-permute-done | bytes 262176 | tf_op jit(solution)/shard_map/ppermute | solution.py:612
  16.1 8.3 %band_product_split.1.after_ref = f32[4,512,128]{2,1,0:T(8,128)} custom-call(f32[2048,1536]{1,0:T(8,128)} %inter_ref.1, f32[2048,128]{1,0:T(8,128)} %vec_ref.3, f32[512,128]{1,0:T(8,128)S(1)} %collective-permute-done.after_ref, f32[512,128]{1,0:T(8,128)S(1)} %collective-permute-done.1.before_ref), custom_call_target="tpu_custom_call" | custom-call | flops 3221225472 | bytes 12582912 | tf_op jit(solution)/shard_map/band_product_split/pallas_call | solution.py:151
  24.4 11.6 %all-to-all-start = ((f32[4,512,128]{2,1,0:T(8,128)}), f32[4,512,128]{2,1,0:T(8,128)S(1)}, u32[]{:S(2)}, u32[]{:S(2)}) async-start(f32[4,512,128]{2,1,0:T(8,128)} %band_product_split.1.after_ref), calls=%async_computation | async-start | bytes 2097152 | tf_op jit(solution)/shard_map/all_to_all | solution.py:614
  36.0 0.0 collective-permute-done.6.value_ref
  36.0 1.3 %collective-permute-start.8 = (f32[2,16,2304]{2,1,0:T(8,128)S(1)}, f32[2,16,2304]{2,1,0:T(8,128)}, u32[]{:S(2)}, u32[]{:S(2)}) collective-permute-start(f32[2,16,2304]{2,1,0:T(8,128)S(1)} %pass_on.3.across_ref), channel_id=1, source_target_pairs={{4,0},{8,12},{5,1},{9,13},{6,2},{10,14},{7,3},{11,15},{20,16},{24,... | collective-permute-start | bytes 884744 | tf_op jit(solution)/shard_map/ppermute | solution.py:191
  37.4 4.6 %halve_last.1 = (bf16[3,2,512,1024]{3,2,1,0:T(8,128)(2,1)S(1)}, f32[2,256,1024]{2,1,0:T(8,128)S(1)}, bf16[2,256,1024]{2,1,0:T(8,128)(2,1)S(1)}, f32[256,128]{1,0:T(8,128)S(1)}, f32[256,128]{1,0:T(8,128)S(1)}) custom-call(s32[2]{0:T(128)S(1)} %pad_add_fusion.place_ref.after_ref, f32[2048,2048]{1,0:T(8,128)} %factor_ref.5, s32[8,128]{1,0:T(8,128)S(1)} %bitcast.9, ...), custom_call_target="tpu_custom_call" | custom-call | flops 1073741824 | bytes 12582912 | tf_op jit(solution)/shard_map/halve_last/pallas_call | solution.py:463
  42.0 2.6 %copy-done = bf16[3,2,512,1024]{3,2,1,0:T(8,128)(2,1)} copy-done((bf16[3,2,512,1024]{3,2,1,0:T(8,128)(2,1)}, bf16[3,2,512,1024]{3,2,1,0:T(8,128)(2,1)S(1)}, u32[]{:S(2)}) %copy-start) | copy-done | bytes 6291480
  44.6 0.0 collective-permute-done.5.near_ref
  44.6 0.0 collective-permute-done.7.inner_ref
  44.6 4.4 %collective-permute-done.8.outer_ref = f32[2,16,2304]{2,1,0:T(8,128)} collective-permute-done((f32[2,16,2304]{2,1,0:T(8,128)S(1)}, f32[2,16,2304]{2,1,0:T(8,128)}, u32[]{:S(2)}, u32[]{:S(2)}) %collective-permute-start.8) | collective-permute-done | bytes 294944 | tf_op jit(solution)/shard_map/ppermute | solution.py:191
  49.0 2.2 %stack.13 = (f32[3,16,2304]{2,1,0:T(8,128)}, f32[3,16,2304]{2,1,0:T(8,128)}) custom-call(s32[2]{0:T(128)S(1)} %pad_add_fusion.place_ref.after_ref, f32[2,16,2304]{2,1,0:T(8,128)} %collective-permute-done.5.near_ref, f32[2,16,2304]{2,1,0:T(8,128)S(1)} %pass_on.3.across_ref, f32[2,16,2304]{2,1,0:T(8,128)} %collective-permute-done.7.inner_ref, ...), custom_call_target="tpu_custom_call" | custom-call | tf_op jit(solution)/shard_map/stack/pallas_call | solution.py:214
  51.2 1.5 %collective-permute-start.10 = (f32[3,16,2304]{2,1,0:T(8,128)}, f32[3,16,2304]{2,1,0:T(8,128)}, u32[]{:S(2)}, u32[]{:S(2)}) collective-permute-start(f32[3,16,2304]{2,1,0:T(8,128)} %get-tuple-element.32.refs_0_), channel_id=1, source_target_pairs={{0,2},{1,3},{2,0},{3,1},{4,6},{5,7},{6,4},{7,5},{8,10},{9,11},{10,... | collective-permute-start | bytes 1327112 | tf_op jit(solution)/shard_map/ppermute | solution.py:589
  52.7 0.1 collective-permute-start.9
  52.8 3.6 %all-to-all-done = f32[4,512,128]{2,1,0:T(8,128)S(1)} async-done(((f32[4,512,128]{2,1,0:T(8,128)}), f32[4,512,128]{2,1,0:T(8,128)S(1)}, u32[]{:S(2)}, u32[]{:S(2)}) %all-to-all-start) | async-done | bytes 1048608 | tf_op jit(solution)/shard_map/all_to_all | solution.py:614
  56.4 0.9 order_rows.2.after_ref.refs_0_
  57.3 2.5 %collective-permute-done.10.value_ref = f32[3,16,2304]{2,1,0:T(8,128)} collective-permute-done((f32[3,16,2304]{2,1,0:T(8,128)}, f32[3,16,2304]{2,1,0:T(8,128)}, u32[]{:S(2)}, u32[]{:S(2)}) %collective-permute-start.10) | collective-permute-done | bytes 442400 | tf_op jit(solution)/shard_map/ppermute | solution.py:589
  59.9 0.0 collective-permute-start.11
  59.9 1.5 %collective-permute-start.16 = (f32[3,16,2304]{2,1,0:T(8,128)}, f32[3,16,2304]{2,1,0:T(8,128)S(1)}, u32[]{:S(2)}, u32[]{:S(2)}) collective-permute-start(f32[3,16,2304]{2,1,0:T(8,128)} %get-tuple-element.41.refs_0_), channel_id=1, source_target_pairs={{0,2},{1,3},{2,0},{3,1},{4,6},{5,7},{6,4},{7,5},{8,10},{9,11},{10,... | collective-permute-start | bytes 1327112 | tf_op jit(solution)/shard_map/ppermute | solution.py:589
  61.3 0.2 collective-permute-start.15
  61.5 1.9 %collective-permute-start.2 = (f32[256,128]{1,0:T(8,128)S(1)}, f32[256,128]{1,0:T(8,128)S(1)}, u32[]{:S(2)}, u32[]{:S(2)}) collective-permute-start(f32[256,128]{1,0:T(8,128)S(1)} %order_rows.2.after_ref.refs_0_), channel_id=1, source_target_pairs={{0,8},{4,12},{8,0},{12,4},{1,9},{5,13},{9,1},{13,5},{2,10},{6,14},... | collective-permute-start | bytes 393224 | tf_op jit(solution)/shard_map/ppermute | solution.py:589
  63.5 0.0 collective-permute-done.9.refs_1_
  63.5 0.3 collective-permute-start.3
  63.8 0.0 collective-permute-done.11.refs_3_
  63.8 1.3 %collective-permute-start.4 = (f32[256,128]{1,0:T(8,128)S(1)}, f32[256,128]{1,0:T(8,128)S(1)}, u32[]{:S(2)}, u32[]{:S(2)}) collective-permute-start(f32[256,128]{1,0:T(8,128)S(1)} %order_rows.2.after_ref.refs_0_), channel_id=1, source_target_pairs={{0,4},{4,0},{8,12},{12,8},{1,5},{5,1},{9,13},{13,9},{2,6},{6,2},{1... | collective-permute-start | bytes 393224 | tf_op jit(solution)/shard_map/ppermute | solution.py:589
  65.0 4.4 %invert_panel.2 = (bf16[1024,1024]{1,0:T(8,128)(2,1)S(1)}, bf16[1024,1024]{1,0:T(8,128)(2,1)S(1)}, bf16[4,256,256]{2,1,0:T(8,128)(2,1)S(1)}, bf16[4,256,256]{2,1,0:T(8,128)(2,1)S(1)}) custom-call(s32[2]{0:T(128)S(1)} %pad_add_fusion.place_ref.after_ref, f32[256,128]{1,0:T(8,128)S(1)} %order_rows.2.after_ref.refs_0_, ...), custom_call_target="tpu_custom_call" | custom-call | flops 137438953472 | bytes 12582912 | tf_op jit(solution)/shard_map/invert_panel/pallas_call | solution.py:295
  69.5 2.6 %order_rows.3 = (f32[256,128]{1,0:T(8,128)S(1)}, f32[1536,128]{1,0:T(8,128)S(1)}) custom-call(s32[2048]{0:T(1024)S(1)} %copy-done.5, f32[2048,128]{1,0:T(8,128)S(1)} %bitcast.6, bf16[4,256,256]{2,1,0:T(8,128)(2,1)S(1)} %get-tuple-element.35.after_ref.refs_6_), custom_call_target="tpu_custom_call" | custom-call | bytes 2097152 | tf_op jit(solution)/shard_map/order_rows/pallas_call | solution.py:328
  72.1 0.6 collective-permute-done.16.value_ref
  72.6 0.0 collective-permute-start.17
  72.6 0.8 collective-permute-done.2.refs_1_
  73.5 1.3 %collective-permute-done.4.refs_3_ = f32[256,128]{1,0:T(8,128)S(1)} collective-permute-done((f32[256,128]{1,0:T(8,128)S(1)}, f32[256,128]{1,0:T(8,128)S(1)}, u32[]{:S(2)}, u32[]{:S(2)}) %collective-permute-start.4) | collective-permute-done | bytes 131104 | tf_op jit(solution)/shard_map/ppermute | solution.py:589
  74.7 2.3 %first_solve.1 = (f32[64,16,128]{2,1,0:T(8,128)S(1)}, f32[256,128]{1,0:T(8,128)S(1)}) custom-call(s32[2]{0:T(128)S(1)} %pad_add_fusion.place_ref.after_ref, f32[256,128]{1,0:T(8,128)S(1)} %order_rows.2.after_ref.refs_0_, f32[256,128]{1,0:T(8,128)S(1)} %collective-permute-done.2.refs_1_, f32[256,128]{1,0:T(8,128)S(1)} %collective-permute-done.3.refs_2_, ...), custom_call_target="tpu_custom_call" | custom-call | flops 137438953472 | bytes 6291456 | tf_op jit(solution)/shard_map/first_solve/pallas_call | solution.py:380
  77.1 3.3 %collective-permute-start.12 = (f32[256,128]{1,0:T(8,128)S(1)}, f32[256,128]{1,0:T(8,128)S(1)}, u32[]{:S(2)}, u32[]{:S(2)}) collective-permute-start(f32[256,128]{1,0:T(8,128)S(1)} %get-tuple-element.39.refs_0_), channel_id=1, source_target_pairs={{0,8},{4,12},{8,0},{12,4},{1,9},{5,13},{9,1},{13,5},{2,10},{6,14},... | collective-permute-start | bytes 393224 | tf_op jit(solution)/shard_map/ppermute | solution.py:589
  80.4 1.2 %collective-permute-start.13 = (f32[256,128]{1,0:T(8,128)S(1)}, f32[256,128]{1,0:T(8,128)S(1)}, u32[]{:S(2)}, u32[]{:S(2)}) collective-permute-start(f32[256,128]{1,0:T(8,128)S(1)} %get-tuple-element.39.refs_0_), channel_id=1, source_target_pairs={{0,12},{4,8},{8,4},{12,0},{1,13},{5,9},{9,5},{13,1},{2,14},{6,10},... | collective-permute-start | bytes 393224 | tf_op jit(solution)/shard_map/ppermute | solution.py:589
  81.6 3.9 %middle_update.1.refs_11_ = f32[1536,128]{1,0:T(8,128)S(1)} custom-call(f32[2048,2048]{1,0:T(8,128)} %factor_ref.5, f32[1536,128]{1,0:T(8,128)S(1)} %get-tuple-element.48.rest_ref, f32[64,16,128]{2,1,0:T(8,128)S(1)} %get-tuple-element.40.after_ref.y_ref.refs_8_), custom_call_target="tpu_custom_call" | custom-call | flops 1610612736 | bytes 8388608 | tf_op jit(solution)/shard_map/middle_update/pallas_call | solution.py:505
  85.5 0.0 collective-permute-done.15.refs_1_
  85.6 0.0 collective-permute-done.17.refs_3_
  85.6 4.3 %invert_panel.3 = (bf16[1024,1024]{1,0:T(8,128)(2,1)S(1)}, bf16[1024,1024]{1,0:T(8,128)(2,1)S(1)}, bf16[4,256,256]{2,1,0:T(8,128)(2,1)S(1)}, bf16[4,256,256]{2,1,0:T(8,128)(2,1)S(1)}) custom-call(s32[2]{0:T(128)S(1)} %pad_add_fusion.place_ref.after_ref, f32[64,16,128]{2,1,0:T(8,128)S(1)} %get-tuple-element.40.after_ref.y_ref.refs_8_, ...), custom_call_target="tpu_custom_call" | custom-call | flops 1073741824 | bytes 12582912 | tf_op jit(solution)/shard_map/invert_panel/pallas_call | solution.py:295
  89.9 0.5 collective-permute-done.12.refs_1_
  90.4 0.2 collective-permute-done.14.refs_3_
  90.6 4.5 %last_solve.1 = f32[2048,128]{1,0:T(8,128)} custom-call(s32[2]{0:T(128)S(1)} %pad_add_fusion.place_ref.after_ref, bf16[3,2,512,1024]{3,2,1,0:T(8,128)(2,1)S(1)} %bitcast.8, f32[256,128]{1,0:T(8,128)S(1)} %get-tuple-element.39.refs_0_, f32[256,128]{1,0:T(8,128)S(1)} %collective-permute-done.12.refs_1_, f32[256,128]{1,0:T(8,128)S(1)} %collective-permute-done.13.refs_2_, ...), custom_call_target="tpu_custom_call" | custom-call | flops 2147483648 | bytes 12582912 | tf_op jit(solution)/shard_map/last_solve/pallas_call | solution.py:570
  (34 shorter events, 0.1 us)
Async XLA Ops:
  2.6 11.4 %collective-permute-start = (f32[512,128]{1,0:T(8,128)S(1)}, f32[512,128]{1,0:T(8,128)S(1)}, u32[]{:S(2)}, u32[]{:S(2)}) collective-permute-start(f32[512,128]{1,0:T(8,128)S(1)} %get-tuple-element.27), channel_id=1, source_target_pairs={{4,0},{8,4},{12,8},{5,1},{9,5},{13,9},{6,2},{10,6},{14,10},{7,3},{... | collective-permute-start | bytes 786440 | tf_op jit(solution)/shard_map/ppermute | solution.py:612
  3.9 12.3 %collective-permute-start.1 = (f32[512,128]{1,0:T(8,128)S(1)}, f32[512,128]{1,0:T(8,128)S(1)}, u32[]{:S(2)}, u32[]{:S(2)}) collective-permute-start(f32[512,128]{1,0:T(8,128)S(1)} %get-tuple-element.28), channel_id=1, source_target_pairs={{0,4},{4,8},{8,12},{1,5},{5,9},{9,13},{2,6},{6,10},{10,14},{3,7},{... | collective-permute-start | bytes 786440 | tf_op jit(solution)/shard_map/ppermute | solution.py:612
  9.4 26.6 %collective-permute-start.6 = (f32[2,16,2304]{2,1,0:T(8,128)}, f32[2,16,2304]{2,1,0:T(8,128)S(1)}, u32[]{:S(2)}, u32[]{:S(2)}) collective-permute-start(f32[2,16,2304]{2,1,0:T(8,128)} %get-tuple-element.31), channel_id=1, source_target_pairs={{0,8},{4,12},{8,0},{12,4},{1,9},{5,13},{9,1},{13,5},{2,10},{6,14},... | collective-permute-start | bytes 884744 | tf_op jit(solution)/shard_map/ppermute | solution.py:589
  12.5 32.1 %collective-permute-start.5 = (f32[2,16,2304]{2,1,0:T(8,128)}, f32[2,16,2304]{2,1,0:T(8,128)}, u32[]{:S(2)}, u32[]{:S(2)}) collective-permute-start(f32[2,16,2304]{2,1,0:T(8,128)} %get-tuple-element.31), channel_id=1, source_target_pairs={{0,4},{4,0},{8,12},{12,8},{1,5},{5,1},{9,13},{13,9},{2,6},{6,2},{1... | collective-permute-start | bytes 884744 | tf_op jit(solution)/shard_map/ppermute | solution.py:589
  12.5 32.1 %collective-permute-start.7 = (f32[2,16,2304]{2,1,0:T(8,128)}, f32[2,16,2304]{2,1,0:T(8,128)}, u32[]{:S(2)}, u32[]{:S(2)}) collective-permute-start(f32[2,16,2304]{2,1,0:T(8,128)} %get-tuple-element.31), channel_id=1, source_target_pairs={{4,8},{8,4},{5,9},{9,5},{6,10},{10,6},{7,11},{11,7},{20,24},{24,20... | collective-permute-start | bytes 884744 | tf_op jit(solution)/shard_map/ppermute | solution.py:190
  24.4 31.9 %all-to-all-start = ((f32[4,512,128]{2,1,0:T(8,128)}), f32[4,512,128]{2,1,0:T(8,128)S(1)}, u32[]{:S(2)}, u32[]{:S(2)}) async-start(f32[4,512,128]{2,1,0:T(8,128)} %band_product_split.1.after_ref), calls=%async_computation | async-start | bytes 2097152 | tf_op jit(solution)/shard_map/all_to_all | solution.py:614
  36.0 1.3 %copy-start.10 = (f32[2048]{0:T(1024)S(1)}, f32[2048]{0:T(1024)}, u32[]{:S(2)}) copy-start(f32[2048]{0:T(1024)} %param.12) | copy-start | bytes 24580
  36.0 1.4 %copy-start.6 = (s32[1024]{0:T(1024)S(1)}, s32[1024]{0:T(1024)}, u32[]{:S(2)}) copy-start(s32[1024]{0:T(1024)} %param.11) | copy-start | bytes 12292
  36.0 1.4 %copy-start.7 = (f32[1024]{0:T(1024)S(1)}, f32[1024]{0:T(1024)}, u32[]{:S(2)}) copy-start(f32[1024]{0:T(1024)} %param.13) | copy-start | bytes 12292
  36.0 13.0 %collective-permute-start.8 = (f32[2,16,2304]{2,1,0:T(8,128)S(1)}, f32[2,16,2304]{2,1,0:T(8,128)}, u32[]{:S(2)}, u32[]{:S(2)}) collective-permute-start(f32[2,16,2304]{2,1,0:T(8,128)S(1)} %pass_on.3.across_ref), channel_id=1, source_target_pairs={{4,0},{8,12},{5,1},{9,13},{6,2},{10,14},{7,3},{11,15},{20,16},{24,... | collective-permute-start | bytes 884744 | tf_op jit(solution)/shard_map/ppermute | solution.py:191
  42.0 2.6 %copy-start = (bf16[3,2,512,1024]{3,2,1,0:T(8,128)(2,1)}, bf16[3,2,512,1024]{3,2,1,0:T(8,128)(2,1)S(1)}, u32[]{:S(2)}) copy-start(bf16[3,2,512,1024]{3,2,1,0:T(8,128)(2,1)S(1)} %get-tuple-element.29.left_ref) | copy-start | bytes 18874372
  44.6 8.1 %copy-start.1 = (f32[256,128]{1,0:T(8,128)}, f32[256,128]{1,0:T(8,128)S(1)}, u32[]{:S(2)}) copy-start(f32[256,128]{1,0:T(8,128)S(1)} %get-tuple-element.46.refs_9_) | copy-start | bytes 393220
  44.6 8.1 %copy-start.3 = (f32[256,128]{1,0:T(8,128)}, f32[256,128]{1,0:T(8,128)S(1)}, u32[]{:S(2)}) copy-start(f32[256,128]{1,0:T(8,128)S(1)} %get-tuple-element.47.refs_10_) | copy-start | bytes 393220
  44.6 8.1 %copy-start.8 = (bf16[2,256,1024]{2,1,0:T(8,128)(2,1)}, bf16[2,256,1024]{2,1,0:T(8,128)(2,1)S(1)}, u32[]{:S(2)}) copy-start(bf16[2,256,1024]{2,1,0:T(8,128)(2,1)S(1)} %get-tuple-element.37.refs_8_) | copy-start | bytes 3145732
  44.6 11.8 %copy-start.5 = (s32[2048]{0:T(1024)S(1)}, s32[2048]{0:T(1024)}, u32[]{:S(2)}) copy-start(s32[2048]{0:T(1024)} %pivot_ref.3) | copy-start | bytes 24580
  51.2 8.6 %collective-permute-start.10 = (f32[3,16,2304]{2,1,0:T(8,128)}, f32[3,16,2304]{2,1,0:T(8,128)}, u32[]{:S(2)}, u32[]{:S(2)}) collective-permute-start(f32[3,16,2304]{2,1,0:T(8,128)} %get-tuple-element.32.refs_0_), channel_id=1, source_target_pairs={{0,2},{1,3},{2,0},{3,1},{4,6},{5,7},{6,4},{7,5},{8,10},{9,11},{10,... | collective-permute-start | bytes 1327112 | tf_op jit(solution)/shard_map/ppermute | solution.py:589
  52.7 10.8 %collective-permute-start.9 = (f32[3,16,2304]{2,1,0:T(8,128)}, f32[3,16,2304]{2,1,0:T(8,128)}, u32[]{:S(2)}, u32[]{:S(2)}) collective-permute-start(f32[3,16,2304]{2,1,0:T(8,128)} %get-tuple-element.32.refs_0_), channel_id=1, source_target_pairs={{0,1},{1,0},{2,3},{3,2},{4,5},{5,4},{6,7},{7,6},{8,9},{9,8},{10,11... | collective-permute-start | bytes 1327112 | tf_op jit(solution)/shard_map/ppermute | solution.py:589
  59.9 3.9 %collective-permute-start.11 = (f32[3,16,2304]{2,1,0:T(8,128)}, f32[3,16,2304]{2,1,0:T(8,128)S(1)}, u32[]{:S(2)}, u32[]{:S(2)}) collective-permute-start(f32[3,16,2304]{2,1,0:T(8,128)} %pass_on.4.refs_2_), channel_id=1, source_target_pairs={{0,1},{1,0},{2,3},{3,2},{4,5},{5,4},{6,7},{7,6},{8,9},{9,8},{10,11... | collective-permute-start | bytes 1327112 | tf_op jit(solution)/shard_map/ppermute | solution.py:589
  59.9 12.8 %collective-permute-start.16 = (f32[3,16,2304]{2,1,0:T(8,128)}, f32[3,16,2304]{2,1,0:T(8,128)S(1)}, u32[]{:S(2)}, u32[]{:S(2)}) collective-permute-start(f32[3,16,2304]{2,1,0:T(8,128)} %get-tuple-element.41.refs_0_), channel_id=1, source_target_pairs={{0,2},{1,3},{2,0},{3,1},{4,6},{5,7},{6,4},{7,5},{8,10},{9,11},{10,... | collective-permute-start | bytes 1327112 | tf_op jit(solution)/shard_map/ppermute | solution.py:589
  61.3 24.2 %collective-permute-start.15 = (f32[3,16,2304]{2,1,0:T(8,128)}, f32[3,16,2304]{2,1,0:T(8,128)}, u32[]{:S(2)}, u32[]{:S(2)}) collective-permute-start(f32[3,16,2304]{2,1,0:T(8,128)} %get-tuple-element.41.refs_0_), channel_id=1, source_target_pairs={{0,1},{1,0},{2,3},{3,2},{4,5},{5,4},{6,7},{7,6},{8,9},{9,8},{10,11... | collective-permute-start | bytes 1327112 | tf_op jit(solution)/shard_map/ppermute | solution.py:589
  61.5 11.9 %collective-permute-start.2 = (f32[256,128]{1,0:T(8,128)S(1)}, f32[256,128]{1,0:T(8,128)S(1)}, u32[]{:S(2)}, u32[]{:S(2)}) collective-permute-start(f32[256,128]{1,0:T(8,128)S(1)} %order_rows.2.after_ref.refs_0_), channel_id=1, source_target_pairs={{0,8},{4,12},{8,0},{12,4},{1,9},{5,13},{9,1},{13,5},{2,10},{6,14},... | collective-permute-start | bytes 393224 | tf_op jit(solution)/shard_map/ppermute | solution.py:589
  63.5 10.0 %collective-permute-start.3 = (f32[256,128]{1,0:T(8,128)S(1)}, f32[256,128]{1,0:T(8,128)S(1)}, u32[]{:S(2)}, u32[]{:S(2)}) collective-permute-start(f32[256,128]{1,0:T(8,128)S(1)} %order_rows.2.after_ref.refs_0_), channel_id=1, source_target_pairs={{0,12},{4,8},{8,4},{12,0},{1,13},{5,9},{9,5},{13,1},{2,14},{6,10},... | collective-permute-start | bytes 393224 | tf_op jit(solution)/shard_map/ppermute | solution.py:589
  63.8 11.0 %collective-permute-start.4 = (f32[256,128]{1,0:T(8,128)S(1)}, f32[256,128]{1,0:T(8,128)S(1)}, u32[]{:S(2)}, u32[]{:S(2)}) collective-permute-start(f32[256,128]{1,0:T(8,128)S(1)} %order_rows.2.after_ref.refs_0_), channel_id=1, source_target_pairs={{0,4},{4,0},{8,12},{12,8},{1,5},{5,1},{9,13},{13,9},{2,6},{6,2},{1... | collective-permute-start | bytes 393224 | tf_op jit(solution)/shard_map/ppermute | solution.py:589
  69.5 5.3 %copy-start.9 = (bf16[2,256,1024]{2,1,0:T(8,128)(2,1)S(1)}, bf16[2,256,1024]{2,1,0:T(8,128)(2,1)}, u32[]{:S(2)}) copy-start(bf16[2,256,1024]{2,1,0:T(8,128)(2,1)} %copy-done.8) | copy-start | bytes 3145732
  72.6 12.9 %collective-permute-start.17 = (f32[3,16,2304]{2,1,0:T(8,128)S(1)}, f32[3,16,2304]{2,1,0:T(8,128)S(1)}, u32[]{:S(2)}, u32[]{:S(2)}) collective-permute-start(f32[3,16,2304]{2,1,0:T(8,128)S(1)} %pass_on.5.refs_2_), channel_id=1, source_target_pairs={{0,1},{1,0},{2,3},{3,2},{4,5},{5,4},{6,7},{7,6},{8,9},{9,8},{10,11... | collective-permute-start | bytes 1327112 | tf_op jit(solution)/shard_map/ppermute | solution.py:589
  77.1 13.3 %collective-permute-start.12 = (f32[256,128]{1,0:T(8,128)S(1)}, f32[256,128]{1,0:T(8,128)S(1)}, u32[]{:S(2)}, u32[]{:S(2)}) collective-permute-start(f32[256,128]{1,0:T(8,128)S(1)} %get-tuple-element.39.refs_0_), channel_id=1, source_target_pairs={{0,8},{4,12},{8,0},{12,4},{1,9},{5,13},{9,1},{13,5},{2,10},{6,14},... | collective-permute-start | bytes 393224 | tf_op jit(solution)/shard_map/ppermute | solution.py:589
  80.4 10.0 %collective-permute-start.13 = (f32[256,128]{1,0:T(8,128)S(1)}, f32[256,128]{1,0:T(8,128)S(1)}, u32[]{:S(2)}, u32[]{:S(2)}) collective-permute-start(f32[256,128]{1,0:T(8,128)S(1)} %get-tuple-element.39.refs_0_), channel_id=1, source_target_pairs={{0,12},{4,8},{8,4},{12,0},{1,13},{5,9},{9,5},{13,1},{2,14},{6,10},... | collective-permute-start | bytes 393224 | tf_op jit(solution)/shard_map/ppermute | solution.py:589
  81.6 9.0 %collective-permute-start.14 = (f32[256,128]{1,0:T(8,128)S(1)}, f32[256,128]{1,0:T(8,128)S(1)}, u32[]{:S(2)}, u32[]{:S(2)}) collective-permute-start(f32[256,128]{1,0:T(8,128)S(1)} %get-tuple-element.39.refs_0_), channel_id=1, source_target_pairs={{0,4},{4,0},{8,12},{12,8},{1,5},{5,1},{9,13},{13,9},{2,6},{6,2},{1... | collective-permute-start | bytes 393224 | tf_op jit(solution)/shard_map/ppermute | solution.py:589
  81.6 9.0 %slice-start = ((s8[6291456]{0:T(1024)(128)(4,1)}), s8[4194304]{0:T(1024)(128)(4,1)S(1)}, s32[]{:S(2)}) async-start(s8[6291456]{0:T(1024)(128)(4,1)} %bitcast.7), calls=%async_computation.1 | async-start | bytes 8388608
  81.6 9.0 %slice-start.1 = ((s8[6291456]{0:T(1024)(128)(4,1)}), s8[2097152]{0:T(1024)(128)(4,1)S(1)}, s32[]{:S(2)}) async-start(s8[6291456]{0:T(1024)(128)(4,1)} %bitcast.7), calls=%async_computation.2 | async-start | bytes 4194304
  85.5 5.1 %copy-start.2 = (f32[256,128]{1,0:T(8,128)S(1)}, f32[256,128]{1,0:T(8,128)}, u32[]{:S(2)}) copy-start(f32[256,128]{1,0:T(8,128)} %copy-done.1) | copy-start | bytes 393220
  85.5 5.1 %copy-start.4 = (f32[256,128]{1,0:T(8,128)S(1)}, f32[256,128]{1,0:T(8,128)}, u32[]{:S(2)}) copy-start(f32[256,128]{1,0:T(8,128)} %copy-done.3) | copy-start | bytes 393220

commit v5 on v3

--- a/solution.py
+++ b/solution.py
@@ -113,7 +113,7 @@
         functools.partial(start_kernel, slots, shares),
         out_shape=[shaped(PANELS, CYC, (runs * runs + runs // 2) * HALF), edge, edge],
         in_specs=[IN_SMEM, IN_HBM, IN_HBM],
-        out_specs=[IN_VMEM] * 3,
+        out_specs=[IN_VMEM, IN_HBM, IN_HBM],
         scratch_shapes=[pltpu.SemaphoreType.DMA((PANELS * (runs + runs // 2) + 2,))],
         compiler_params=params(4),
         cost_estimate=cost(0, 4 * MIB),

time: 95.7 us -> 95.7 us (level)
  no operation moved by 1% of the time
where the time goes in v5:
time: 95.7 us; the launch traced here: 95.3 us
  Pallas kernels  41 us (43%)
  starting transfers between devices  35.4 us (37%)
  waiting for transfers between devices  15.1 us (16%)
  local copies, waits for them, and re-layouts  3.31 us (3%)
    ppermute x14, starting transfers between devices, swap_with(): return lax.ppermute(value, axis, [(i, i ^ distance) for i in range(size)])  14.2 us
    all_to_all x1, starting transfers between devices, local(): lax.all_to_all(product, 'row', 0, 0, tiled=True).reshape(vectors.shape)  11.7 us
    pallas_call x2, Pallas kernels, invert_panel(): pl.pallas_call(functools.partial(invert_kernel, panel, owners, shares), o...  8.72 us
    pallas_call x1, Pallas kernels, band_product_split(): pl.pallas_call(band_kernel, out_shape=shaped(owners, rows // owners, colu...  8.32 us
    ppermute x2, starting transfers between devices, local(): halo = (lax.ppermute(first, 'row', down), lax.ppermute(last, 'row', up))  6.86 us
    ppermute x14, waiting for transfers between devices, swap_with(): return lax.ppermute(value, axis, [(i, i ^ distance) for i in range(size)])  5.87 us
    pallas_call x1, Pallas kernels, last_solve(): pl.pallas_call(functools.partial(last_kernel, owners, tile_rows), out_sha...  4.52 us
    pallas_call x1, Pallas kernels, halve_last(): pl.pallas_call(functools.partial(halve_kernel, tile_rows), out_shape=[sha...  4.03 us
  transfers between devices with their start and end apart: 19, of which 9 were waited for; matrix products, arithmetic and copies ran while one was open for 0% of the time, Pallas kernels for 36%

profile of v5, /device:TPU:0, one launch (start us, length us, event | category | flops | bytes accessed | tf_op | source)
XLA Modules:
  0.0 95.3 jit_solution(11388225551290232687)
XLA Ops:
  0.0 0.1 pad_add_fusion.place_ref.after_ref
  0.1 2.5 %first_sends.1 = (f32[2,16,2304]{2,1,0:T(8,128)}, f32[512,128]{1,0:T(8,128)S(1)}, f32[512,128]{1,0:T(8,128)S(1)}) custom-call(s32[2]{0:T(128)S(1)} %pad_add_fusion.place_ref.after_ref, f32[2048,2048]{1,0:T(8,128)} %factor_ref.5, f32[2048,128]{1,0:T(8,128)} %vec_ref.3), custom_call_target="tpu_custom_call" | custom-call | bytes 4194304 | tf_op jit(solution)/shard_map/first_sends/pallas_call | solution.py:112
  2.6 1.3 %collective-permute-start = (f32[512,128]{1,0:T(8,128)S(1)}, f32[512,128]{1,0:T(8,128)S(1)}, u32[]{:S(2)}, u32[]{:S(2)}) collective-permute-start(f32[512,128]{1,0:T(8,128)S(1)} %get-tuple-element.27), channel_id=1, source_target_pairs={{4,0},{8,4},{12,8},{5,1},{9,5},{13,9},{6,2},{10,6},{14,10},{7,3},{... | collective-permute-start | bytes 786440 | tf_op jit(solution)/shard_map/ppermute | solution.py:609
  3.9 5.6 %collective-permute-start.1 = (f32[512,128]{1,0:T(8,128)S(1)}, f32[512,128]{1,0:T(8,128)S(1)}, u32[]{:S(2)}, u32[]{:S(2)}) collective-permute-start(f32[512,128]{1,0:T(8,128)S(1)} %get-tuple-element.28), channel_id=1, source_target_pairs={{0,4},{4,8},{8,12},{1,5},{5,9},{9,13},{2,6},{6,10},{10,14},{3,7},{... | collective-permute-start | bytes 786440 | tf_op jit(solution)/shard_map/ppermute | solution.py:609
  9.5 3.1 %collective-permute-start.6 = (f32[2,16,2304]{2,1,0:T(8,128)}, f32[2,16,2304]{2,1,0:T(8,128)S(1)}, u32[]{:S(2)}, u32[]{:S(2)}) collective-permute-start(f32[2,16,2304]{2,1,0:T(8,128)} %get-tuple-element.32), channel_id=1, source_target_pairs={{0,8},{4,12},{8,0},{12,4},{1,9},{5,13},{9,1},{13,5},{2,10},{6,14},... | collective-permute-start | bytes 884744 | tf_op jit(solution)/shard_map/ppermute | solution.py:586
  12.5 0.0 collective-permute-start.5
  12.6 1.4 %collective-permute-start.7 = (f32[2,16,2304]{2,1,0:T(8,128)}, f32[2,16,2304]{2,1,0:T(8,128)}, u32[]{:S(2)}, u32[]{:S(2)}) collective-permute-start(f32[2,16,2304]{2,1,0:T(8,128)} %get-tuple-element.32), channel_id=1, source_target_pairs={{4,8},{8,4},{5,9},{9,5},{6,10},{10,6},{7,11},{11,7},{20,24},{24,20... | collective-permute-start | bytes 884744 | tf_op jit(solution)/shard_map/ppermute | solution.py:190
  13.9 0.0 collective-permute-done.after_ref
  13.9 2.2 %collective-permute-done.1.before_ref = f32[512,128]{1,0:T(8,128)S(1)} collective-permute-done((f32[512,128]{1,0:T(8,128)S(1)}, f32[512,128]{1,0:T(8,128)S(1)}, u32[]{:S(2)}, u32[]{:S(2)}) %collective-permute-start.1) | collective-permute-done | bytes 262176 | tf_op jit(solution)/shard_map/ppermute | solution.py:609
  16.1 8.3 %band_product_split.1.after_ref = f32[4,512,128]{2,1,0:T(8,128)} custom-call(f32[2048,1536]{1,0:T(8,128)} %inter_ref.1, f32[2048,128]{1,0:T(8,128)} %vec_ref.3, f32[512,128]{1,0:T(8,128)S(1)} %collective-permute-done.after_ref, f32[512,128]{1,0:T(8,128)S(1)} %collective-permute-done.1.before_ref), custom_call_target="tpu_custom_call" | custom-call | flops 3221225472 | bytes 12582912 | tf_op jit(solution)/shard_map/band_product_split/pallas_call | solution.py:151
  24.5 11.7 %all-to-all-start = ((f32[4,512,128]{2,1,0:T(8,128)}), f32[4,512,128]{2,1,0:T(8,128)S(1)}, u32[]{:S(2)}, u32[]{:S(2)}) async-start(f32[4,512,128]{2,1,0:T(8,128)} %band_product_split.1.after_ref), calls=%async_computation | async-start | bytes 2097152 | tf_op jit(solution)/shard_map/all_to_all | solution.py:611
  36.2 1.0 %own_weights.1 = (f32[256,128]{1,0:T(8,128)S(1)}, f32[256,128]{1,0:T(8,128)S(1)}) custom-call(s32[2]{0:T(128)S(1)} %pad_add_fusion.place_ref.after_ref, f32[4,512,128]{2,1,0:T(8,128)} %band_product_split.1.after_ref, s32[8,128]{1,0:T(8,128)S(1)} %bitcast.9, f32[8,256]{1,0:T(8,128)S(1)} %reshape.13.diag_ref, f32[8,128]{1,0:T(8,128)S(1)} %bitcast.10), custom_call_target="tpu_custom_call" | custom-call | flops 137438953472 | tf_op jit(solution)/shard_map/own_weights/pallas_call | solution.py:420
  37.1 0.0 collective-permute-done.6.value_ref
  37.2 0.6 copy-done.3
  37.8 1.3 %collective-permute-start.8 = (f32[2,16,2304]{2,1,0:T(8,128)S(1)}, f32[2,16,2304]{2,1,0:T(8,128)S(1)}, u32[]{:S(2)}, u32[]{:S(2)}) collective-permute-start(f32[2,16,2304]{2,1,0:T(8,128)S(1)} %pass_on.3.across_ref), channel_id=1, source_target_pairs={{4,0},{8,12},{5,1},{9,13},{6,2},{10,14},{7,3},{11,15},{20,16},{24,... | collective-permute-start | bytes 884744 | tf_op jit(solution)/shard_map/ppermute | solution.py:191
  39.1 4.0 %halve_last.1 = (bf16[3,2,512,1024]{3,2,1,0:T(8,128)(2,1)S(1)}, f32[2,256,1024]{2,1,0:T(8,128)S(1)}, bf16[2,256,1024]{2,1,0:T(8,128)(2,1)S(1)}) custom-call(f32[2048,2048]{1,0:T(8,128)} %factor_ref.5, f32[256,128]{1,0:T(8,128)S(1)} %get-tuple-element.29.after_ref.refs_9_), custom_call_target="tpu_custom_call" | custom-call | flops 1073741824 | bytes 12582912 | tf_op jit(solution)/shard_map/halve_last/pallas_call | solution.py:462
  43.1 2.6 %copy-done = bf16[3,2,512,1024]{3,2,1,0:T(8,128)(2,1)} copy-done((bf16[3,2,512,1024]{3,2,1,0:T(8,128)(2,1)}, bf16[3,2,512,1024]{3,2,1,0:T(8,128)(2,1)S(1)}, u32[]{:S(2)}) %copy-start) | copy-done | bytes 6291480
  45.8 0.0 collective-permute-done.5.near_ref
  45.8 0.0 collective-permute-done.7.inner_ref
  45.8 3.4 %collective-permute-done.8.outer_ref = f32[2,16,2304]{2,1,0:T(8,128)S(1)} collective-permute-done((f32[2,16,2304]{2,1,0:T(8,128)S(1)}, f32[2,16,2304]{2,1,0:T(8,128)S(1)}, u32[]{:S(2)}, u32[]{:S(2)}) %collective-permute-start.8) | collective-permute-done | bytes 294944 | tf_op jit(solution)/shard_map/ppermute | solution.py:191
  49.2 2.1 %stack.13 = (f32[3,16,2304]{2,1,0:T(8,128)}, f32[3,16,2304]{2,1,0:T(8,128)}) custom-call(s32[2]{0:T(128)S(1)} %pad_add_fusion.place_ref.after_ref, f32[2,16,2304]{2,1,0:T(8,128)} %collective-permute-done.5.near_ref, f32[2,16,2304]{2,1,0:T(8,128)S(1)} %pass_on.3.across_ref, f32[2,16,2304]{2,1,0:T(8,128)} %collective-permute-done.7.inner_ref, ...), custom_call_target="tpu_custom_call" | custom-call | tf_op jit(solution)/shard_map/stack/pallas_call | solution.py:214
  51.3 1.5 %collective-permute-start.10 = (f32[3,16,2304]{2,1,0:T(8,128)}, f32[3,16,2304]{2,1,0:T(8,128)}, u32[]{:S(2)}, u32[]{:S(2)}) collective-permute-start(f32[3,16,2304]{2,1,0:T(8,128)} %get-tuple-element.33.refs_0_), channel_id=1, source_target_pairs={{0,2},{1,3},{2,0},{3,1},{4,6},{5,7},{6,4},{7,5},{8,10},{9,11},{10,... | collective-permute-start | bytes 1327112 | tf_op jit(solution)/shard_map/ppermute | solution.py:586
  52.8 3.6 %all-to-all-done = f32[4,512,128]{2,1,0:T(8,128)S(1)} async-done(((f32[4,512,128]{2,1,0:T(8,128)}), f32[4,512,128]{2,1,0:T(8,128)S(1)}, u32[]{:S(2)}, u32[]{:S(2)}) %all-to-all-start) | async-done | bytes 1048608 | tf_op jit(solution)/shard_map/all_to_all | solution.py:611
  56.4 0.9 order_rows.2.after_ref.refs_0_
  57.3 2.6 %collective-permute-done.10.value_ref = f32[3,16,2304]{2,1,0:T(8,128)} collective-permute-done((f32[3,16,2304]{2,1,0:T(8,128)}, f32[3,16,2304]{2,1,0:T(8,128)}, u32[]{:S(2)}, u32[]{:S(2)}) %collective-permute-start.10) | collective-permute-done | bytes 442400 | tf_op jit(solution)/shard_map/ppermute | solution.py:586
  60.0 0.0 collective-permute-start.11
  60.0 1.5 %collective-permute-start.16 = (f32[3,16,2304]{2,1,0:T(8,128)}, f32[3,16,2304]{2,1,0:T(8,128)S(1)}, u32[]{:S(2)}, u32[]{:S(2)}) collective-permute-start(f32[3,16,2304]{2,1,0:T(8,128)} %get-tuple-element.42.refs_0_), channel_id=1, source_target_pairs={{0,2},{1,3},{2,0},{3,1},{4,6},{5,7},{6,4},{7,5},{8,10},{9,11},{10,... | collective-permute-start | bytes 1327112 | tf_op jit(solution)/shard_map/ppermute | solution.py:586
  61.4 0.2 collective-permute-start.15
  61.7 2.0 %collective-permute-start.2 = (f32[256,128]{1,0:T(8,128)S(1)}, f32[256,128]{1,0:T(8,128)S(1)}, u32[]{:S(2)}, u32[]{:S(2)}) collective-permute-start(f32[256,128]{1,0:T(8,128)S(1)} %order_rows.2.after_ref.refs_0_), channel_id=1, source_target_pairs={{0,8},{4,12},{8,0},{12,4},{1,9},{5,13},{9,1},{13,5},{2,10},{6,14},... | collective-permute-start | bytes 393224 | tf_op jit(solution)/shard_map/ppermute | solution.py:586
  63.7 0.1 collective-permute-start.3
  63.8 0.0 collective-permute-done.11.refs_3_
  63.8 1.4 %collective-permute-start.4 = (f32[256,128]{1,0:T(8,128)S(1)}, f32[256,128]{1,0:T(8,128)S(1)}, u32[]{:S(2)}, u32[]{:S(2)}) collective-permute-start(f32[256,128]{1,0:T(8,128)S(1)} %order_rows.2.after_ref.refs_0_), channel_id=1, source_target_pairs={{0,4},{4,0},{8,12},{12,8},{1,5},{5,1},{9,13},{13,9},{2,6},{6,2},{1... | collective-permute-start | bytes 393224 | tf_op jit(solution)/shard_map/ppermute | solution.py:586
  65.2 4.4 %invert_panel.2 = (bf16[1024,1024]{1,0:T(8,128)(2,1)S(1)}, bf16[1024,1024]{1,0:T(8,128)(2,1)S(1)}, bf16[4,256,256]{2,1,0:T(8,128)(2,1)S(1)}, bf16[4,256,256]{2,1,0:T(8,128)(2,1)S(1)}) custom-call(s32[2]{0:T(128)S(1)} %pad_add_fusion.place_ref.after_ref, f32[256,128]{1,0:T(8,128)S(1)} %order_rows.2.after_ref.refs_0_, ...), custom_call_target="tpu_custom_call" | custom-call | flops 137438953472 | bytes 12582912 | tf_op jit(solution)/shard_map/invert_panel/pallas_call | solution.py:295
  69.6 2.6 %order_rows.3 = (f32[256,128]{1,0:T(8,128)S(1)}, f32[1536,128]{1,0:T(8,128)S(1)}) custom-call(s32[2048]{0:T(1024)S(1)} %copy-done.5, f32[2048,128]{1,0:T(8,128)S(1)} %bitcast.6, bf16[4,256,256]{2,1,0:T(8,128)(2,1)S(1)} %get-tuple-element.36.after_ref.refs_6_), custom_call_target="tpu_custom_call" | custom-call | bytes 2097152 | tf_op jit(solution)/shard_map/order_rows/pallas_call | solution.py:328
  72.2 0.6 collective-permute-done.16.value_ref
  72.8 0.7 collective-permute-done.2.refs_1_
  73.5 1.3 %collective-permute-done.4.refs_3_ = f32[256,128]{1,0:T(8,128)S(1)} collective-permute-done((f32[256,128]{1,0:T(8,128)S(1)}, f32[256,128]{1,0:T(8,128)S(1)}, u32[]{:S(2)}, u32[]{:S(2)}) %collective-permute-start.4) | collective-permute-done | bytes 131104 | tf_op jit(solution)/shard_map/ppermute | solution.py:586
  74.8 2.3 %first_solve.1 = (f32[64,16,128]{2,1,0:T(8,128)S(1)}, f32[256,128]{1,0:T(8,128)S(1)}) custom-call(s32[2]{0:T(128)S(1)} %pad_add_fusion.place_ref.after_ref, f32[256,128]{1,0:T(8,128)S(1)} %order_rows.2.after_ref.refs_0_, f32[256,128]{1,0:T(8,128)S(1)} %collective-permute-done.2.refs_1_, f32[256,128]{1,0:T(8,128)S(1)} %collective-permute-done.3.refs_2_, ...), custom_call_target="tpu_custom_call" | custom-call | flops 137438953472 | bytes 6291456 | tf_op jit(solution)/shard_map/first_solve/pallas_call | solution.py:380
  77.1 3.3 %collective-permute-start.12 = (f32[256,128]{1,0:T(8,128)S(1)}, f32[256,128]{1,0:T(8,128)S(1)}, u32[]{:S(2)}, u32[]{:S(2)}) collective-permute-start(f32[256,128]{1,0:T(8,128)S(1)} %get-tuple-element.40.refs_0_), channel_id=1, source_target_pairs={{0,8},{4,12},{8,0},{12,4},{1,9},{5,13},{9,1},{13,5},{2,10},{6,14},... | collective-permute-start | bytes 393224 | tf_op jit(solution)/shard_map/ppermute | solution.py:586
  80.4 1.2 %collective-permute-start.13 = (f32[256,128]{1,0:T(8,128)S(1)}, f32[256,128]{1,0:T(8,128)S(1)}, u32[]{:S(2)}, u32[]{:S(2)}) collective-permute-start(f32[256,128]{1,0:T(8,128)S(1)} %get-tuple-element.40.refs_0_), channel_id=1, source_target_pairs={{0,12},{4,8},{8,4},{12,0},{1,13},{5,9},{9,5},{13,1},{2,14},{6,10},... | collective-permute-start | bytes 393224 | tf_op jit(solution)/shard_map/ppermute | solution.py:586
  81.6 0.0 collective-permute-start.14
  81.6 3.9 %middle_update.1.refs_11_ = f32[1536,128]{1,0:T(8,128)S(1)} custom-call(f32[2048,2048]{1,0:T(8,128)} %factor_ref.5, f32[1536,128]{1,0:T(8,128)S(1)} %get-tuple-element.48.rest_ref, f32[64,16,128]{2,1,0:T(8,128)S(1)} %get-tuple-element.41.after_ref.y_ref.refs_8_), custom_call_target="tpu_custom_call" | custom-call | flops 1610612736 | bytes 8388608 | tf_op jit(solution)/shard_map/middle_update/pallas_call | solution.py:502
  85.6 0.0 collective-permute-done.15.refs_1_
  85.6 4.3 %invert_panel.3 = (bf16[1024,1024]{1,0:T(8,128)(2,1)S(1)}, bf16[1024,1024]{1,0:T(8,128)(2,1)S(1)}, bf16[4,256,256]{2,1,0:T(8,128)(2,1)S(1)}, bf16[4,256,256]{2,1,0:T(8,128)(2,1)S(1)}) custom-call(s32[2]{0:T(128)S(1)} %pad_add_fusion.place_ref.after_ref, f32[64,16,128]{2,1,0:T(8,128)S(1)} %get-tuple-element.41.after_ref.y_ref.refs_8_, ...), custom_call_target="tpu_custom_call" | custom-call | flops 1073741824 | bytes 12582912 | tf_op jit(solution)/shard_map/invert_panel/pallas_call | solution.py:295
  89.9 0.5 collective-permute-done.12.refs_1_
  90.4 0.0 collective-permute-done.13.refs_2_
  90.4 0.1 collective-permute-done.14.refs_3_
  90.6 4.5 %last_solve.1 = f32[2048,128]{1,0:T(8,128)} custom-call(s32[2]{0:T(128)S(1)} %pad_add_fusion.place_ref.after_ref, bf16[3,2,512,1024]{3,2,1,0:T(8,128)(2,1)S(1)} %bitcast.8, f32[256,128]{1,0:T(8,128)S(1)} %get-tuple-element.40.refs_0_, f32[256,128]{1,0:T(8,128)S(1)} %collective-permute-done.12.refs_1_, f32[256,128]{1,0:T(8,128)S(1)} %collective-permute-done.13.refs_2_, ...), custom_call_target="tpu_custom_call" | custom-call | flops 2147483648 | bytes 12582912 | tf_op jit(solution)/shard_map/last_solve/pallas_call | solution.py:567
  (34 shorter events, 0.1 us)
Async XLA Ops:
  0.1 13.9 %copy-start.10 = (f32[2048]{0:T(1024)S(1)}, f32[2048]{0:T(1024)}, u32[]{:S(2)}) copy-start(f32[2048]{0:T(1024)} %param.12) | copy-start | bytes 24580
  2.6 11.4 %collective-permute-start = (f32[512,128]{1,0:T(8,128)S(1)}, f32[512,128]{1,0:T(8,128)S(1)}, u32[]{:S(2)}, u32[]{:S(2)}) collective-permute-start(f32[512,128]{1,0:T(8,128)S(1)} %get-tuple-element.27), channel_id=1, source_target_pairs={{4,0},{8,4},{12,8},{5,1},{9,5},{13,9},{6,2},{10,6},{14,10},{7,3},{... | collective-permute-start | bytes 786440 | tf_op jit(solution)/shard_map/ppermute | solution.py:609
  3.9 12.3 %collective-permute-start.1 = (f32[512,128]{1,0:T(8,128)S(1)}, f32[512,128]{1,0:T(8,128)S(1)}, u32[]{:S(2)}, u32[]{:S(2)}) collective-permute-start(f32[512,128]{1,0:T(8,128)S(1)} %get-tuple-element.28), channel_id=1, source_target_pairs={{0,4},{4,8},{8,12},{1,5},{5,9},{9,13},{2,6},{6,10},{10,14},{3,7},{... | collective-permute-start | bytes 786440 | tf_op jit(solution)/shard_map/ppermute | solution.py:609
  9.5 27.7 %collective-permute-start.6 = (f32[2,16,2304]{2,1,0:T(8,128)}, f32[2,16,2304]{2,1,0:T(8,128)S(1)}, u32[]{:S(2)}, u32[]{:S(2)}) collective-permute-start(f32[2,16,2304]{2,1,0:T(8,128)} %get-tuple-element.32), channel_id=1, source_target_pairs={{0,8},{4,12},{8,0},{12,4},{1,9},{5,13},{9,1},{13,5},{2,10},{6,14},... | collective-permute-start | bytes 884744 | tf_op jit(solution)/shard_map/ppermute | solution.py:586
  12.5 33.2 %collective-permute-start.5 = (f32[2,16,2304]{2,1,0:T(8,128)}, f32[2,16,2304]{2,1,0:T(8,128)}, u32[]{:S(2)}, u32[]{:S(2)}) collective-permute-start(f32[2,16,2304]{2,1,0:T(8,128)} %get-tuple-element.32), channel_id=1, source_target_pairs={{0,4},{4,0},{8,12},{12,8},{1,5},{5,1},{9,13},{13,9},{2,6},{6,2},{1... | collective-permute-start | bytes 884744 | tf_op jit(solution)/shard_map/ppermute | solution.py:586
  12.6 33.2 %collective-permute-start.7 = (f32[2,16,2304]{2,1,0:T(8,128)}, f32[2,16,2304]{2,1,0:T(8,128)}, u32[]{:S(2)}, u32[]{:S(2)}) collective-permute-start(f32[2,16,2304]{2,1,0:T(8,128)} %get-tuple-element.32), channel_id=1, source_target_pairs={{4,8},{8,4},{5,9},{9,5},{6,10},{10,6},{7,11},{11,7},{20,24},{24,20... | collective-permute-start | bytes 884744 | tf_op jit(solution)/shard_map/ppermute | solution.py:190
  24.5 11.7 %copy-start.8 = (s32[1024]{0:T(1024)S(1)}, s32[1024]{0:T(1024)}, u32[]{:S(2)}) copy-start(s32[1024]{0:T(1024)} %param.11) | copy-start | bytes 12292
  24.5 11.7 %copy-start.9 = (f32[1024]{0:T(1024)S(1)}, f32[1024]{0:T(1024)}, u32[]{:S(2)}) copy-start(f32[1024]{0:T(1024)} %param.13) | copy-start | bytes 12292
  24.5 31.9 %all-to-all-start = ((f32[4,512,128]{2,1,0:T(8,128)}), f32[4,512,128]{2,1,0:T(8,128)S(1)}, u32[]{:S(2)}, u32[]{:S(2)}) async-start(f32[4,512,128]{2,1,0:T(8,128)} %band_product_split.1.after_ref), calls=%async_computation | async-start | bytes 2097152 | tf_op jit(solution)/shard_map/all_to_all | solution.py:611
  37.1 0.7 copy-start.3
  37.1 6.0 %copy-start.1 = (f32[256,128]{1,0:T(8,128)}, f32[256,128]{1,0:T(8,128)S(1)}, u32[]{:S(2)}) copy-start(f32[256,128]{1,0:T(8,128)S(1)} %get-tuple-element.29.after_ref.refs_9_) | copy-start | bytes 393220
  37.8 11.4 %collective-permute-start.8 = (f32[2,16,2304]{2,1,0:T(8,128)S(1)}, f32[2,16,2304]{2,1,0:T(8,128)S(1)}, u32[]{:S(2)}, u32[]{:S(2)}) collective-permute-start(f32[2,16,2304]{2,1,0:T(8,128)S(1)} %pass_on.3.across_ref), channel_id=1, source_target_pairs={{4,0},{8,12},{5,1},{9,13},{6,2},{10,14},{7,3},{11,15},{20,16},{24,... | collective-permute-start | bytes 884744 | tf_op jit(solution)/shard_map/ppermute | solution.py:191
  43.1 2.7 %copy-start = (bf16[3,2,512,1024]{3,2,1,0:T(8,128)(2,1)}, bf16[3,2,512,1024]{3,2,1,0:T(8,128)(2,1)S(1)}, u32[]{:S(2)}) copy-start(bf16[3,2,512,1024]{3,2,1,0:T(8,128)(2,1)S(1)} %get-tuple-element.30.left_ref) | copy-start | bytes 18874372
  45.8 7.0 %copy-start.6 = (bf16[2,256,1024]{2,1,0:T(8,128)(2,1)}, bf16[2,256,1024]{2,1,0:T(8,128)(2,1)S(1)}, u32[]{:S(2)}) copy-start(bf16[2,256,1024]{2,1,0:T(8,128)(2,1)S(1)} %get-tuple-element.38.refs_8_) | copy-start | bytes 3145732
  45.8 10.6 %copy-start.5 = (s32[2048]{0:T(1024)S(1)}, s32[2048]{0:T(1024)}, u32[]{:S(2)}) copy-start(s32[2048]{0:T(1024)} %pivot_ref.3) | copy-start | bytes 24580
  51.3 8.6 %collective-permute-start.10 = (f32[3,16,2304]{2,1,0:T(8,128)}, f32[3,16,2304]{2,1,0:T(8,128)}, u32[]{:S(2)}, u32[]{:S(2)}) collective-permute-start(f32[3,16,2304]{2,1,0:T(8,128)} %get-tuple-element.33.refs_0_), channel_id=1, source_target_pairs={{0,2},{1,3},{2,0},{3,1},{4,6},{5,7},{6,4},{7,5},{8,10},{9,11},{10,... | collective-permute-start | bytes 1327112 | tf_op jit(solution)/shard_map/ppermute | solution.py:586
  52.8 10.9 %collective-permute-start.9 = (f32[3,16,2304]{2,1,0:T(8,128)}, f32[3,16,2304]{2,1,0:T(8,128)}, u32[]{:S(2)}, u32[]{:S(2)}) collective-permute-start(f32[3,16,2304]{2,1,0:T(8,128)} %get-tuple-element.33.refs_0_), channel_id=1, source_target_pairs={{0,1},{1,0},{2,3},{3,2},{4,5},{5,4},{6,7},{7,6},{8,9},{9,8},{10,11... | collective-permute-start | bytes 1327112 | tf_op jit(solution)/shard_map/ppermute | solution.py:586
  60.0 3.8 %collective-permute-start.11 = (f32[3,16,2304]{2,1,0:T(8,128)}, f32[3,16,2304]{2,1,0:T(8,128)S(1)}, u32[]{:S(2)}, u32[]{:S(2)}) collective-permute-start(f32[3,16,2304]{2,1,0:T(8,128)} %pass_on.4.refs_2_), channel_id=1, source_target_pairs={{0,1},{1,0},{2,3},{3,2},{4,5},{5,4},{6,7},{7,6},{8,9},{9,8},{10,11... | collective-permute-start | bytes 1327112 | tf_op jit(solution)/shard_map/ppermute | solution.py:586
  60.0 12.8 %collective-permute-start.16 = (f32[3,16,2304]{2,1,0:T(8,128)}, f32[3,16,2304]{2,1,0:T(8,128)S(1)}, u32[]{:S(2)}, u32[]{:S(2)}) collective-permute-start(f32[3,16,2304]{2,1,0:T(8,128)} %get-tuple-element.42.refs_0_), channel_id=1, source_target_pairs={{0,2},{1,3},{2,0},{3,1},{4,6},{5,7},{6,4},{7,5},{8,10},{9,11},{10,... | collective-permute-start | bytes 1327112 | tf_op jit(solution)/shard_map/ppermute | solution.py:586
  61.4 24.1 %collective-permute-start.15 = (f32[3,16,2304]{2,1,0:T(8,128)}, f32[3,16,2304]{2,1,0:T(8,128)}, u32[]{:S(2)}, u32[]{:S(2)}) collective-permute-start(f32[3,16,2304]{2,1,0:T(8,128)} %get-tuple-element.42.refs_0_), channel_id=1, source_target_pairs={{0,1},{1,0},{2,3},{3,2},{4,5},{5,4},{6,7},{7,6},{8,9},{9,8},{10,11... | collective-permute-start | bytes 1327112 | tf_op jit(solution)/shard_map/ppermute | solution.py:586
  61.7 11.8 %collective-permute-start.2 = (f32[256,128]{1,0:T(8,128)S(1)}, f32[256,128]{1,0:T(8,128)S(1)}, u32[]{:S(2)}, u32[]{:S(2)}) collective-permute-start(f32[256,128]{1,0:T(8,128)S(1)} %order_rows.2.after_ref.refs_0_), channel_id=1, source_target_pairs={{0,8},{4,12},{8,0},{12,4},{1,9},{5,13},{9,1},{13,5},{2,10},{6,14},... | collective-permute-start | bytes 393224 | tf_op jit(solution)/shard_map/ppermute | solution.py:586
  63.7 9.8 %collective-permute-start.3 = (f32[256,128]{1,0:T(8,128)S(1)}, f32[256,128]{1,0:T(8,128)S(1)}, u32[]{:S(2)}, u32[]{:S(2)}) collective-permute-start(f32[256,128]{1,0:T(8,128)S(1)} %order_rows.2.after_ref.refs_0_), channel_id=1, source_target_pairs={{0,12},{4,8},{8,4},{12,0},{1,13},{5,9},{9,5},{13,1},{2,14},{6,10},... | collective-permute-start | bytes 393224 | tf_op jit(solution)/shard_map/ppermute | solution.py:586
  63.8 11.0 %collective-permute-start.4 = (f32[256,128]{1,0:T(8,128)S(1)}, f32[256,128]{1,0:T(8,128)S(1)}, u32[]{:S(2)}, u32[]{:S(2)}) collective-permute-start(f32[256,128]{1,0:T(8,128)S(1)} %order_rows.2.after_ref.refs_0_), channel_id=1, source_target_pairs={{0,4},{4,0},{8,12},{12,8},{1,5},{5,1},{9,13},{13,9},{2,6},{6,2},{1... | collective-permute-start | bytes 393224 | tf_op jit(solution)/shard_map/ppermute | solution.py:586
  69.6 5.2 %copy-start.7 = (bf16[2,256,1024]{2,1,0:T(8,128)(2,1)S(1)}, bf16[2,256,1024]{2,1,0:T(8,128)(2,1)}, u32[]{:S(2)}) copy-start(bf16[2,256,1024]{2,1,0:T(8,128)(2,1)} %copy-done.6) | copy-start | bytes 3145732
  72.8 12.8 %collective-permute-start.17 = (f32[3,16,2304]{2,1,0:T(8,128)S(1)}, f32[3,16,2304]{2,1,0:T(8,128)S(1)}, u32[]{:S(2)}, u32[]{:S(2)}) collective-permute-start(f32[3,16,2304]{2,1,0:T(8,128)S(1)} %pass_on.5.refs_2_), channel_id=1, source_target_pairs={{0,1},{1,0},{2,3},{3,2},{4,5},{5,4},{6,7},{7,6},{8,9},{9,8},{10,11... | collective-permute-start | bytes 1327112 | tf_op jit(solution)/shard_map/ppermute | solution.py:586
  77.1 13.3 %collective-permute-start.12 = (f32[256,128]{1,0:T(8,128)S(1)}, f32[256,128]{1,0:T(8,128)S(1)}, u32[]{:S(2)}, u32[]{:S(2)}) collective-permute-start(f32[256,128]{1,0:T(8,128)S(1)} %get-tuple-element.40.refs_0_), channel_id=1, source_target_pairs={{0,8},{4,12},{8,0},{12,4},{1,9},{5,13},{9,1},{13,5},{2,10},{6,14},... | collective-permute-start | bytes 393224 | tf_op jit(solution)/shard_map/ppermute | solution.py:586
  80.4 10.0 %collective-permute-start.13 = (f32[256,128]{1,0:T(8,128)S(1)}, f32[256,128]{1,0:T(8,128)S(1)}, u32[]{:S(2)}, u32[]{:S(2)}) collective-permute-start(f32[256,128]{1,0:T(8,128)S(1)} %get-tuple-element.40.refs_0_), channel_id=1, source_target_pairs={{0,12},{4,8},{8,4},{12,0},{1,13},{5,9},{9,5},{13,1},{2,14},{6,10},... | collective-permute-start | bytes 393224 | tf_op jit(solution)/shard_map/ppermute | solution.py:586
  81.6 9.0 %collective-permute-start.14 = (f32[256,128]{1,0:T(8,128)S(1)}, f32[256,128]{1,0:T(8,128)S(1)}, u32[]{:S(2)}, u32[]{:S(2)}) collective-permute-start(f32[256,128]{1,0:T(8,128)S(1)} %get-tuple-element.40.refs_0_), channel_id=1, source_target_pairs={{0,4},{4,0},{8,12},{12,8},{1,5},{5,1},{9,13},{13,9},{2,6},{6,2},{1... | collective-permute-start | bytes 393224 | tf_op jit(solution)/shard_map/ppermute | solution.py:586
  81.6 9.0 %slice-start = ((s8[6291456]{0:T(1024)(128)(4,1)}), s8[4194304]{0:T(1024)(128)(4,1)S(1)}, s32[]{:S(2)}) async-start(s8[6291456]{0:T(1024)(128)(4,1)} %bitcast.7), calls=%async_computation.1 | async-start | bytes 8388608
  81.6 9.0 %slice-start.1 = ((s8[6291456]{0:T(1024)(128)(4,1)}), s8[2097152]{0:T(1024)(128)(4,1)S(1)}, s32[]{:S(2)}) async-start(s8[6291456]{0:T(1024)(128)(4,1)} %bitcast.7), calls=%async_computation.2 | async-start | bytes 4194304
  85.6 5.0 %copy-start.2 = (f32[256,128]{1,0:T(8,128)S(1)}, f32[256,128]{1,0:T(8,128)}, u32[]{:S(2)}) copy-start(f32[256,128]{1,0:T(8,128)} %copy-done.1) | copy-start | bytes 393220
  85.6 5.0 %copy-start.4 = (f32[256,128]{1,0:T(8,128)S(1)}, f32[256,128]{1,0:T(8,128)}, u32[]{:S(2)}) copy-start(f32[256,128]{1,0:T(8,128)} %copy-done.3) | copy-start | bytes 393220

commit v6 on v4

--- a/solution.py
+++ b/solution.py
@@ -113,7 +113,7 @@
         functools.partial(start_kernel, slots, shares),
         out_shape=[shaped(PANELS, CYC, (runs * runs + runs // 2) * HALF), edge, edge],
         in_specs=[IN_SMEM, IN_HBM, IN_HBM],
-        out_specs=[IN_VMEM] * 3,
+        out_specs=[IN_VMEM, IN_HBM, IN_HBM],
         scratch_shapes=[pltpu.SemaphoreType.DMA((PANELS * (runs + runs // 2) + 2,))],
         compiler_params=params(4),
         cost_estimate=cost(0, 4 * MIB),

time: 95.7 us -> 95.7 us (level)
  no operation moved by 1% of the time
where the time goes in v6:
time: 95.7 us; the launch traced here: 95.3 us
  Pallas kernels  40.7 us (43%)
  starting transfers between devices  35.4 us (37%)
  waiting for transfers between devices  16.1 us (17%)
  local copies, waits for them, and re-layouts  2.68 us (3%)
    ppermute x14, starting transfers between devices, swap_with(): return lax.ppermute(value, axis, [(i, i ^ distance) for i in range(size)])  14.3 us
    all_to_all x1, starting transfers between devices, local(): lax.all_to_all(product, 'row', 0, 0, tiled=True).reshape(vectors.shape)  11.6 us
    pallas_call x2, Pallas kernels, invert_panel(): pl.pallas_call(functools.partial(invert_kernel, panel, owners, shares), o...  8.72 us
    pallas_call x1, Pallas kernels, band_product_split(): pl.pallas_call(band_kernel, out_shape=shaped(owners, rows // owners, colu...  8.32 us
    ppermute x2, starting transfers between devices, local(): halo = (lax.ppermute(first, 'row', down), lax.ppermute(last, 'row', up))  6.86 us
    ppermute x14, waiting for transfers between devices, swap_with(): return lax.ppermute(value, axis, [(i, i ^ distance) for i in range(size)])  5.89 us
    pallas_call x1, Pallas kernels, halve_last(): pl.pallas_call(functools.partial(halve_kernel, tile_rows), out_shape=[sha...  4.58 us
    pallas_call x1, Pallas kernels, last_solve(): pl.pallas_call(functools.partial(last_kernel, owners, tile_rows), out_sha...  4.54 us
  transfers between devices with their start and end apart: 19, of which 9 were waited for; matrix products, arithmetic and copies ran while one was open for 0% of the time, Pallas kernels for 35%

profile of v6, /device:TPU:0, one launch (start us, length us, event | category | flops | bytes accessed | tf_op | source)
XLA Modules:
  0.0 95.3 jit_solution(15760745167282827497)
XLA Ops:
  0.0 0.1 pad_add_fusion.place_ref.after_ref
  0.1 2.5 %first_sends.1 = (f32[2,16,2304]{2,1,0:T(8,128)}, f32[512,128]{1,0:T(8,128)S(1)}, f32[512,128]{1,0:T(8,128)S(1)}) custom-call(s32[2]{0:T(128)S(1)} %pad_add_fusion.place_ref.after_ref, f32[2048,2048]{1,0:T(8,128)} %factor_ref.5, f32[2048,128]{1,0:T(8,128)} %vec_ref.3), custom_call_target="tpu_custom_call" | custom-call | bytes 4194304 | tf_op jit(solution)/shard_map/first_sends/pallas_call | solution.py:112
  2.6 1.3 %collective-permute-start = (f32[512,128]{1,0:T(8,128)S(1)}, f32[512,128]{1,0:T(8,128)S(1)}, u32[]{:S(2)}, u32[]{:S(2)}) collective-permute-start(f32[512,128]{1,0:T(8,128)S(1)} %get-tuple-element.27), channel_id=1, source_target_pairs={{4,0},{8,4},{12,8},{5,1},{9,5},{13,9},{6,2},{10,6},{14,10},{7,3},{... | collective-permute-start | bytes 786440 | tf_op jit(solution)/shard_map/ppermute | solution.py:612
  3.9 5.6 %collective-permute-start.1 = (f32[512,128]{1,0:T(8,128)S(1)}, f32[512,128]{1,0:T(8,128)S(1)}, u32[]{:S(2)}, u32[]{:S(2)}) collective-permute-start(f32[512,128]{1,0:T(8,128)S(1)} %get-tuple-element.28), channel_id=1, source_target_pairs={{0,4},{4,8},{8,12},{1,5},{5,9},{9,13},{2,6},{6,10},{10,14},{3,7},{... | collective-permute-start | bytes 786440 | tf_op jit(solution)/shard_map/ppermute | solution.py:612
  9.4 3.1 %collective-permute-start.6 = (f32[2,16,2304]{2,1,0:T(8,128)}, f32[2,16,2304]{2,1,0:T(8,128)S(1)}, u32[]{:S(2)}, u32[]{:S(2)}) collective-permute-start(f32[2,16,2304]{2,1,0:T(8,128)} %get-tuple-element.31), channel_id=1, source_target_pairs={{0,8},{4,12},{8,0},{12,4},{1,9},{5,13},{9,1},{13,5},{2,10},{6,14},... | collective-permute-start | bytes 884744 | tf_op jit(solution)/shard_map/ppermute | solution.py:589
  12.5 0.0 collective-permute-start.5
  12.5 1.4 %collective-permute-start.7 = (f32[2,16,2304]{2,1,0:T(8,128)}, f32[2,16,2304]{2,1,0:T(8,128)}, u32[]{:S(2)}, u32[]{:S(2)}) collective-permute-start(f32[2,16,2304]{2,1,0:T(8,128)} %get-tuple-element.31), channel_id=1, source_target_pairs={{4,8},{8,4},{5,9},{9,5},{6,10},{10,6},{7,11},{11,7},{20,24},{24,20... | collective-permute-start | bytes 884744 | tf_op jit(solution)/shard_map/ppermute | solution.py:190
  13.9 0.0 collective-permute-done.after_ref
  13.9 2.2 %collective-permute-done.1.before_ref = f32[512,128]{1,0:T(8,128)S(1)} collective-permute-done((f32[512,128]{1,0:T(8,128)S(1)}, f32[512,128]{1,0:T(8,128)S(1)}, u32[]{:S(2)}, u32[]{:S(2)}) %collective-permute-start.1) | collective-permute-done | bytes 262176 | tf_op jit(solution)/shard_map/ppermute | solution.py:612
  16.1 8.3 %band_product_split.1.after_ref = f32[4,512,128]{2,1,0:T(8,128)} custom-call(f32[2048,1536]{1,0:T(8,128)} %inter_ref.1, f32[2048,128]{1,0:T(8,128)} %vec_ref.3, f32[512,128]{1,0:T(8,128)S(1)} %collective-permute-done.after_ref, f32[512,128]{1,0:T(8,128)S(1)} %collective-permute-done.1.before_ref), custom_call_target="tpu_custom_call" | custom-call | flops 3221225472 | bytes 12582912 | tf_op jit(solution)/shard_map/band_product_split/pallas_call | solution.py:151
  24.4 11.6 %all-to-all-start = ((f32[4,512,128]{2,1,0:T(8,128)}), f32[4,512,128]{2,1,0:T(8,128)S(1)}, u32[]{:S(2)}, u32[]{:S(2)}) async-start(f32[4,512,128]{2,1,0:T(8,128)} %band_product_split.1.after_ref), calls=%async_computation | async-start | bytes 2097152 | tf_op jit(solution)/shard_map/all_to_all | solution.py:614
  36.0 0.0 collective-permute-done.6.value_ref
  36.0 1.3 %collective-permute-start.8 = (f32[2,16,2304]{2,1,0:T(8,128)S(1)}, f32[2,16,2304]{2,1,0:T(8,128)}, u32[]{:S(2)}, u32[]{:S(2)}) collective-permute-start(f32[2,16,2304]{2,1,0:T(8,128)S(1)} %pass_on.3.across_ref), channel_id=1, source_target_pairs={{4,0},{8,12},{5,1},{9,13},{6,2},{10,14},{7,3},{11,15},{20,16},{24,... | collective-permute-start | bytes 884744 | tf_op jit(solution)/shard_map/ppermute | solution.py:191
  37.4 4.6 %halve_last.1 = (bf16[3,2,512,1024]{3,2,1,0:T(8,128)(2,1)S(1)}, f32[2,256,1024]{2,1,0:T(8,128)S(1)}, bf16[2,256,1024]{2,1,0:T(8,128)(2,1)S(1)}, f32[256,128]{1,0:T(8,128)S(1)}, f32[256,128]{1,0:T(8,128)S(1)}) custom-call(s32[2]{0:T(128)S(1)} %pad_add_fusion.place_ref.after_ref, f32[2048,2048]{1,0:T(8,128)} %factor_ref.5, s32[8,128]{1,0:T(8,128)S(1)} %bitcast.9, ...), custom_call_target="tpu_custom_call" | custom-call | flops 1073741824 | bytes 12582912 | tf_op jit(solution)/shard_map/halve_last/pallas_call | solution.py:463
  42.0 2.6 %copy-done = bf16[3,2,512,1024]{3,2,1,0:T(8,128)(2,1)} copy-done((bf16[3,2,512,1024]{3,2,1,0:T(8,128)(2,1)}, bf16[3,2,512,1024]{3,2,1,0:T(8,128)(2,1)S(1)}, u32[]{:S(2)}) %copy-start) | copy-done | bytes 6291480
  44.6 0.0 collective-permute-done.5.near_ref
  44.6 0.0 collective-permute-done.7.inner_ref
  44.6 4.4 %collective-permute-done.8.outer_ref = f32[2,16,2304]{2,1,0:T(8,128)} collective-permute-done((f32[2,16,2304]{2,1,0:T(8,128)S(1)}, f32[2,16,2304]{2,1,0:T(8,128)}, u32[]{:S(2)}, u32[]{:S(2)}) %collective-permute-start.8) | collective-permute-done | bytes 294944 | tf_op jit(solution)/shard_map/ppermute | solution.py:191
  49.0 2.2 %stack.13 = (f32[3,16,2304]{2,1,0:T(8,128)}, f32[3,16,2304]{2,1,0:T(8,128)}) custom-call(s32[2]{0:T(128)S(1)} %pad_add_fusion.place_ref.after_ref, f32[2,16,2304]{2,1,0:T(8,128)} %collective-permute-done.5.near_ref, f32[2,16,2304]{2,1,0:T(8,128)S(1)} %pass_on.3.across_ref, f32[2,16,2304]{2,1,0:T(8,128)} %collective-permute-done.7.inner_ref, ...), custom_call_target="tpu_custom_call" | custom-call | tf_op jit(solution)/shard_map/stack/pallas_call | solution.py:214
  51.2 1.5 %collective-permute-start.10 = (f32[3,16,2304]{2,1,0:T(8,128)}, f32[3,16,2304]{2,1,0:T(8,128)}, u32[]{:S(2)}, u32[]{:S(2)}) collective-permute-start(f32[3,16,2304]{2,1,0:T(8,128)} %get-tuple-element.32.refs_0_), channel_id=1, source_target_pairs={{0,2},{1,3},{2,0},{3,1},{4,6},{5,7},{6,4},{7,5},{8,10},{9,11},{10,... | collective-permute-start | bytes 1327112 | tf_op jit(solution)/shard_map/ppermute | solution.py:589
  52.7 0.1 collective-permute-start.9
  52.8 3.6 %all-to-all-done = f32[4,512,128]{2,1,0:T(8,128)S(1)} async-done(((f32[4,512,128]{2,1,0:T(8,128)}), f32[4,512,128]{2,1,0:T(8,128)S(1)}, u32[]{:S(2)}, u32[]{:S(2)}) %all-to-all-start) | async-done | bytes 1048608 | tf_op jit(solution)/shard_map/all_to_all | solution.py:614
  56.4 0.9 order_rows.2.after_ref.refs_0_
  57.3 2.5 %collective-permute-done.10.value_ref = f32[3,16,2304]{2,1,0:T(8,128)} collective-permute-done((f32[3,16,2304]{2,1,0:T(8,128)}, f32[3,16,2304]{2,1,0:T(8,128)}, u32[]{:S(2)}, u32[]{:S(2)}) %collective-permute-start.10) | collective-permute-done | bytes 442400 | tf_op jit(solution)/shard_map/ppermute | solution.py:589
  59.9 0.0 collective-permute-start.11
  59.9 1.5 %collective-permute-start.16 = (f32[3,16,2304]{2,1,0:T(8,128)}, f32[3,16,2304]{2,1,0:T(8,128)S(1)}, u32[]{:S(2)}, u32[]{:S(2)}) collective-permute-start(f32[3,16,2304]{2,1,0:T(8,128)} %get-tuple-element.41.refs_0_), channel_id=1, source_target_pairs={{0,2},{1,3},{2,0},{3,1},{4,6},{5,7},{6,4},{7,5},{8,10},{9,11},{10,... | collective-permute-start | bytes 1327112 | tf_op jit(solution)/shard_map/ppermute | solution.py:589
  61.3 0.2 collective-permute-start.15
  61.5 1.9 %collective-permute-start.2 = (f32[256,128]{1,0:T(8,128)S(1)}, f32[256,128]{1,0:T(8,128)S(1)}, u32[]{:S(2)}, u32[]{:S(2)}) collective-permute-start(f32[256,128]{1,0:T(8,128)S(1)} %order_rows.2.after_ref.refs_0_), channel_id=1, source_target_pairs={{0,8},{4,12},{8,0},{12,4},{1,9},{5,13},{9,1},{13,5},{2,10},{6,14},... | collective-permute-start | bytes 393224 | tf_op jit(solution)/shard_map/ppermute | solution.py:589
  63.5 0.0 collective-permute-done.9.refs_1_
  63.5 0.3 collective-permute-start.3
  63.8 0.0 collective-permute-done.11.refs_3_
  63.8 1.3 %collective-permute-start.4 = (f32[256,128]{1,0:T(8,128)S(1)}, f32[256,128]{1,0:T(8,128)S(1)}, u32[]{:S(2)}, u32[]{:S(2)}) collective-permute-start(f32[256,128]{1,0:T(8,128)S(1)} %order_rows.2.after_ref.refs_0_), channel_id=1, source_target_pairs={{0,4},{4,0},{8,12},{12,8},{1,5},{5,1},{9,13},{13,9},{2,6},{6,2},{1... | collective-permute-start | bytes 393224 | tf_op jit(solution)/shard_map/ppermute | solution.py:589
  65.0 4.4 %invert_panel.2 = (bf16[1024,1024]{1,0:T(8,128)(2,1)S(1)}, bf16[1024,1024]{1,0:T(8,128)(2,1)S(1)}, bf16[4,256,256]{2,1,0:T(8,128)(2,1)S(1)}, bf16[4,256,256]{2,1,0:T(8,128)(2,1)S(1)}) custom-call(s32[2]{0:T(128)S(1)} %pad_add_fusion.place_ref.after_ref, f32[256,128]{1,0:T(8,128)S(1)} %order_rows.2.after_ref.refs_0_, ...), custom_call_target="tpu_custom_call" | custom-call | flops 137438953472 | bytes 12582912 | tf_op jit(solution)/shard_map/invert_panel/pallas_call | solution.py:295
  69.5 2.6 %order_rows.3 = (f32[256,128]{1,0:T(8,128)S(1)}, f32[1536,128]{1,0:T(8,128)S(1)}) custom-call(s32[2048]{0:T(1024)S(1)} %copy-done.5, f32[2048,128]{1,0:T(8,128)S(1)} %bitcast.6, bf16[4,256,256]{2,1,0:T(8,128)(2,1)S(1)} %get-tuple-element.35.after_ref.refs_6_), custom_call_target="tpu_custom_call" | custom-call | bytes 2097152 | tf_op jit(solution)/shard_map/order_rows/pallas_call | solution.py:328
  72.1 0.6 collective-permute-done.16.value_ref
  72.6 0.0 collective-permute-start.17
  72.6 0.8 collective-permute-done.2.refs_1_
  73.5 1.3 %collective-permute-done.4.refs_3_ = f32[256,128]{1,0:T(8,128)S(1)} collective-permute-done((f32[256,128]{1,0:T(8,128)S(1)}, f32[256,128]{1,0:T(8,128)S(1)}, u32[]{:S(2)}, u32[]{:S(2)}) %collective-permute-start.4) | collective-permute-done | bytes 131104 | tf_op jit(solution)/shard_map/ppermute | solution.py:589
  74.7 2.3 %first_solve.1 = (f32[64,16,128]{2,1,0:T(8,128)S(1)}, f32[256,128]{1,0:T(8,128)S(1)}) custom-call(s32[2]{0:T(128)S(1)} %pad_add_fusion.place_ref.after_ref, f32[256,128]{1,0:T(8,128)S(1)} %order_rows.2.after_ref.refs_0_, f32[256,128]{1,0:T(8,128)S(1)} %collective-permute-done.2.refs_1_, f32[256,128]{1,0:T(8,128)S(1)} %collective-permute-done.3.refs_2_, ...), custom_call_target="tpu_custom_call" | custom-call | flops 137438953472 | bytes 6291456 | tf_op jit(solution)/shard_map/first_solve/pallas_call | solution.py:380
  77.1 3.3 %collective-permute-start.12 = (f32[256,128]{1,0:T(8,128)S(1)}, f32[256,128]{1,0:T(8,128)S(1)}, u32[]{:S(2)}, u32[]{:S(2)}) collective-permute-start(f32[256,128]{1,0:T(8,128)S(1)} %get-tuple-element.39.refs_0_), channel_id=1, source_target_pairs={{0,8},{4,12},{8,0},{12,4},{1,9},{5,13},{9,1},{13,5},{2,10},{6,14},... | collective-permute-start | bytes 393224 | tf_op jit(solution)/shard_map/ppermute | solution.py:589
  80.4 1.2 %collective-permute-start.13 = (f32[256,128]{1,0:T(8,128)S(1)}, f32[256,128]{1,0:T(8,128)S(1)}, u32[]{:S(2)}, u32[]{:S(2)}) collective-permute-start(f32[256,128]{1,0:T(8,128)S(1)} %get-tuple-element.39.refs_0_), channel_id=1, source_target_pairs={{0,12},{4,8},{8,4},{12,0},{1,13},{5,9},{9,5},{13,1},{2,14},{6,10},... | collective-permute-start | bytes 393224 | tf_op jit(solution)/shard_map/ppermute | solution.py:589
  81.6 3.9 %middle_update.1.refs_11_ = f32[1536,128]{1,0:T(8,128)S(1)} custom-call(f32[2048,2048]{1,0:T(8,128)} %factor_ref.5, f32[1536,128]{1,0:T(8,128)S(1)} %get-tuple-element.48.rest_ref, f32[64,16,128]{2,1,0:T(8,128)S(1)} %get-tuple-element.40.after_ref.y_ref.refs_8_), custom_call_target="tpu_custom_call" | custom-call | flops 1610612736 | bytes 8388608 | tf_op jit(solution)/shard_map/middle_update/pallas_call | solution.py:505
  85.5 0.0 collective-permute-done.15.refs_1_
  85.6 0.0 collective-permute-done.17.refs_3_
  85.6 4.3 %invert_panel.3 = (bf16[1024,1024]{1,0:T(8,128)(2,1)S(1)}, bf16[1024,1024]{1,0:T(8,128)(2,1)S(1)}, bf16[4,256,256]{2,1,0:T(8,128)(2,1)S(1)}, bf16[4,256,256]{2,1,0:T(8,128)(2,1)S(1)}) custom-call(s32[2]{0:T(128)S(1)} %pad_add_fusion.place_ref.after_ref, f32[64,16,128]{2,1,0:T(8,128)S(1)} %get-tuple-element.40.after_ref.y_ref.refs_8_, ...), custom_call_target="tpu_custom_call" | custom-call | flops 1073741824 | bytes 12582912 | tf_op jit(solution)/shard_map/invert_panel/pallas_call | solution.py:295
  89.9 0.5 collective-permute-done.12.refs_1_
  90.4 0.2 collective-permute-done.14.refs_3_
  90.6 4.5 %last_solve.1 = f32[2048,128]{1,0:T(8,128)} custom-call(s32[2]{0:T(128)S(1)} %pad_add_fusion.place_ref.after_ref, bf16[3,2,512,1024]{3,2,1,0:T(8,128)(2,1)S(1)} %bitcast.8, f32[256,128]{1,0:T(8,128)S(1)} %get-tuple-element.39.refs_0_, f32[256,128]{1,0:T(8,128)S(1)} %collective-permute-done.12.refs_1_, f32[256,128]{1,0:T(8,128)S(1)} %collective-permute-done.13.refs_2_, ...), custom_call_target="tpu_custom_call" | custom-call | flops 2147483648 | bytes 12582912 | tf_op jit(solution)/shard_map/last_solve/pallas_call | solution.py:570
  (34 shorter events, 0.1 us)
Async XLA Ops:
  2.6 11.4 %collective-permute-start = (f32[512,128]{1,0:T(8,128)S(1)}, f32[512,128]{1,0:T(8,128)S(1)}, u32[]{:S(2)}, u32[]{:S(2)}) collective-permute-start(f32[512,128]{1,0:T(8,128)S(1)} %get-tuple-element.27), channel_id=1, source_target_pairs={{4,0},{8,4},{12,8},{5,1},{9,5},{13,9},{6,2},{10,6},{14,10},{7,3},{... | collective-permute-start | bytes 786440 | tf_op jit(solution)/shard_map/ppermute | solution.py:612
  3.9 12.3 %collective-permute-start.1 = (f32[512,128]{1,0:T(8,128)S(1)}, f32[512,128]{1,0:T(8,128)S(1)}, u32[]{:S(2)}, u32[]{:S(2)}) collective-permute-start(f32[512,128]{1,0:T(8,128)S(1)} %get-tuple-element.28), channel_id=1, source_target_pairs={{0,4},{4,8},{8,12},{1,5},{5,9},{9,13},{2,6},{6,10},{10,14},{3,7},{... | collective-permute-start | bytes 786440 | tf_op jit(solution)/shard_map/ppermute | solution.py:612
  9.4 26.6 %collective-permute-start.6 = (f32[2,16,2304]{2,1,0:T(8,128)}, f32[2,16,2304]{2,1,0:T(8,128)S(1)}, u32[]{:S(2)}, u32[]{:S(2)}) collective-permute-start(f32[2,16,2304]{2,1,0:T(8,128)} %get-tuple-element.31), channel_id=1, source_target_pairs={{0,8},{4,12},{8,0},{12,4},{1,9},{5,13},{9,1},{13,5},{2,10},{6,14},... | collective-permute-start | bytes 884744 | tf_op jit(solution)/shard_map/ppermute | solution.py:589
  12.5 32.1 %collective-permute-start.5 = (f32[2,16,2304]{2,1,0:T(8,128)}, f32[2,16,2304]{2,1,0:T(8,128)}, u32[]{:S(2)}, u32[]{:S(2)}) collective-permute-start(f32[2,16,2304]{2,1,0:T(8,128)} %get-tuple-element.31), channel_id=1, source_target_pairs={{0,4},{4,0},{8,12},{12,8},{1,5},{5,1},{9,13},{13,9},{2,6},{6,2},{1... | collective-permute-start | bytes 884744 | tf_op jit(solution)/shard_map/ppermute | solution.py:589
  12.5 32.1 %collective-permute-start.7 = (f32[2,16,2304]{2,1,0:T(8,128)}, f32[2,16,2304]{2,1,0:T(8,128)}, u32[]{:S(2)}, u32[]{:S(2)}) collective-permute-start(f32[2,16,2304]{2,1,0:T(8,128)} %get-tuple-element.31), channel_id=1, source_target_pairs={{4,8},{8,4},{5,9},{9,5},{6,10},{10,6},{7,11},{11,7},{20,24},{24,20... | collective-permute-start | bytes 884744 | tf_op jit(solution)/shard_map/ppermute | solution.py:190
  24.4 31.9 %all-to-all-start = ((f32[4,512,128]{2,1,0:T(8,128)}), f32[4,512,128]{2,1,0:T(8,128)S(1)}, u32[]{:S(2)}, u32[]{:S(2)}) async-start(f32[4,512,128]{2,1,0:T(8,128)} %band_product_split.1.after_ref), calls=%async_computation | async-start | bytes 2097152 | tf_op jit(solution)/shard_map/all_to_all | solution.py:614
  36.0 1.3 %copy-start.10 = (f32[2048]{0:T(1024)S(1)}, f32[2048]{0:T(1024)}, u32[]{:S(2)}) copy-start(f32[2048]{0:T(1024)} %param.12) | copy-start | bytes 24580
  36.0 1.4 %copy-start.6 = (s32[1024]{0:T(1024)S(1)}, s32[1024]{0:T(1024)}, u32[]{:S(2)}) copy-start(s32[1024]{0:T(1024)} %param.11) | copy-start | bytes 12292
  36.0 1.4 %copy-start.7 = (f32[1024]{0:T(1024)S(1)}, f32[1024]{0:T(1024)}, u32[]{:S(2)}) copy-start(f32[1024]{0:T(1024)} %param.13) | copy-start | bytes 12292
  36.0 13.0 %collective-permute-start.8 = (f32[2,16,2304]{2,1,0:T(8,128)S(1)}, f32[2,16,2304]{2,1,0:T(8,128)}, u32[]{:S(2)}, u32[]{:S(2)}) collective-permute-start(f32[2,16,2304]{2,1,0:T(8,128)S(1)} %pass_on.3.across_ref), channel_id=1, source_target_pairs={{4,0},{8,12},{5,1},{9,13},{6,2},{10,14},{7,3},{11,15},{20,16},{24,... | collective-permute-start | bytes 884744 | tf_op jit(solution)/shard_map/ppermute | solution.py:191
  42.0 2.6 %copy-start = (bf16[3,2,512,1024]{3,2,1,0:T(8,128)(2,1)}, bf16[3,2,512,1024]{3,2,1,0:T(8,128)(2,1)S(1)}, u32[]{:S(2)}) copy-start(bf16[3,2,512,1024]{3,2,1,0:T(8,128)(2,1)S(1)} %get-tuple-element.29.left_ref) | copy-start | bytes 18874372
  44.6 8.1 %copy-start.1 = (f32[256,128]{1,0:T(8,128)}, f32[256,128]{1,0:T(8,128)S(1)}, u32[]{:S(2)}) copy-start(f32[256,128]{1,0:T(8,128)S(1)} %get-tuple-element.46.refs_9_) | copy-start | bytes 393220
  44.6 8.1 %copy-start.3 = (f32[256,128]{1,0:T(8,128)}, f32[256,128]{1,0:T(8,128)S(1)}, u32[]{:S(2)}) copy-start(f32[256,128]{1,0:T(8,128)S(1)} %get-tuple-element.47.refs_10_) | copy-start | bytes 393220
  44.6 8.1 %copy-start.8 = (bf16[2,256,1024]{2,1,0:T(8,128)(2,1)}, bf16[2,256,1024]{2,1,0:T(8,128)(2,1)S(1)}, u32[]{:S(2)}) copy-start(bf16[2,256,1024]{2,1,0:T(8,128)(2,1)S(1)} %get-tuple-element.37.refs_8_) | copy-start | bytes 3145732
  44.6 11.8 %copy-start.5 = (s32[2048]{0:T(1024)S(1)}, s32[2048]{0:T(1024)}, u32[]{:S(2)}) copy-start(s32[2048]{0:T(1024)} %pivot_ref.3) | copy-start | bytes 24580
  51.2 8.6 %collective-permute-start.10 = (f32[3,16,2304]{2,1,0:T(8,128)}, f32[3,16,2304]{2,1,0:T(8,128)}, u32[]{:S(2)}, u32[]{:S(2)}) collective-permute-start(f32[3,16,2304]{2,1,0:T(8,128)} %get-tuple-element.32.refs_0_), channel_id=1, source_target_pairs={{0,2},{1,3},{2,0},{3,1},{4,6},{5,7},{6,4},{7,5},{8,10},{9,11},{10,... | collective-permute-start | bytes 1327112 | tf_op jit(solution)/shard_map/ppermute | solution.py:589
  52.7 10.8 %collective-permute-start.9 = (f32[3,16,2304]{2,1,0:T(8,128)}, f32[3,16,2304]{2,1,0:T(8,128)}, u32[]{:S(2)}, u32[]{:S(2)}) collective-permute-start(f32[3,16,2304]{2,1,0:T(8,128)} %get-tuple-element.32.refs_0_), channel_id=1, source_target_pairs={{0,1},{1,0},{2,3},{3,2},{4,5},{5,4},{6,7},{7,6},{8,9},{9,8},{10,11... | collective-permute-start | bytes 1327112 | tf_op jit(solution)/shard_map/ppermute | solution.py:589
  59.9 3.9 %collective-permute-start.11 = (f32[3,16,2304]{2,1,0:T(8,128)}, f32[3,16,2304]{2,1,0:T(8,128)S(1)}, u32[]{:S(2)}, u32[]{:S(2)}) collective-permute-start(f32[3,16,2304]{2,1,0:T(8,128)} %pass_on.4.refs_2_), channel_id=1, source_target_pairs={{0,1},{1,0},{2,3},{3,2},{4,5},{5,4},{6,7},{7,6},{8,9},{9,8},{10,11... | collective-permute-start | bytes 1327112 | tf_op jit(solution)/shard_map/ppermute | solution.py:589
  59.9 12.8 %collective-permute-start.16 = (f32[3,16,2304]{2,1,0:T(8,128)}, f32[3,16,2304]{2,1,0:T(8,128)S(1)}, u32[]{:S(2)}, u32[]{:S(2)}) collective-permute-start(f32[3,16,2304]{2,1,0:T(8,128)} %get-tuple-element.41.refs_0_), channel_id=1, source_target_pairs={{0,2},{1,3},{2,0},{3,1},{4,6},{5,7},{6,4},{7,5},{8,10},{9,11},{10,... | collective-permute-start | bytes 1327112 | tf_op jit(solution)/shard_map/ppermute | solution.py:589
  61.3 24.2 %collective-permute-start.15 = (f32[3,16,2304]{2,1,0:T(8,128)}, f32[3,16,2304]{2,1,0:T(8,128)}, u32[]{:S(2)}, u32[]{:S(2)}) collective-permute-start(f32[3,16,2304]{2,1,0:T(8,128)} %get-tuple-element.41.refs_0_), channel_id=1, source_target_pairs={{0,1},{1,0},{2,3},{3,2},{4,5},{5,4},{6,7},{7,6},{8,9},{9,8},{10,11... | collective-permute-start | bytes 1327112 | tf_op jit(solution)/shard_map/ppermute | solution.py:589
  61.5 11.9 %collective-permute-start.2 = (f32[256,128]{1,0:T(8,128)S(1)}, f32[256,128]{1,0:T(8,128)S(1)}, u32[]{:S(2)}, u32[]{:S(2)}) collective-permute-start(f32[256,128]{1,0:T(8,128)S(1)} %order_rows.2.after_ref.refs_0_), channel_id=1, source_target_pairs={{0,8},{4,12},{8,0},{12,4},{1,9},{5,13},{9,1},{13,5},{2,10},{6,14},... | collective-permute-start | bytes 393224 | tf_op jit(solution)/shard_map/ppermute | solution.py:589
  63.5 10.0 %collective-permute-start.3 = (f32[256,128]{1,0:T(8,128)S(1)}, f32[256,128]{1,0:T(8,128)S(1)}, u32[]{:S(2)}, u32[]{:S(2)}) collective-permute-start(f32[256,128]{1,0:T(8,128)S(1)} %order_rows.2.after_ref.refs_0_), channel_id=1, source_target_pairs={{0,12},{4,8},{8,4},{12,0},{1,13},{5,9},{9,5},{13,1},{2,14},{6,10},... | collective-permute-start | bytes 393224 | tf_op jit(solution)/shard_map/ppermute | solution.py:589
  63.8 11.0 %collective-permute-start.4 = (f32[256,128]{1,0:T(8,128)S(1)}, f32[256,128]{1,0:T(8,128)S(1)}, u32[]{:S(2)}, u32[]{:S(2)}) collective-permute-start(f32[256,128]{1,0:T(8,128)S(1)} %order_rows.2.after_ref.refs_0_), channel_id=1, source_target_pairs={{0,4},{4,0},{8,12},{12,8},{1,5},{5,1},{9,13},{13,9},{2,6},{6,2},{1... | collective-permute-start | bytes 393224 | tf_op jit(solution)/shard_map/ppermute | solution.py:589
  69.5 5.3 %copy-start.9 = (bf16[2,256,1024]{2,1,0:T(8,128)(2,1)S(1)}, bf16[2,256,1024]{2,1,0:T(8,128)(2,1)}, u32[]{:S(2)}) copy-start(bf16[2,256,1024]{2,1,0:T(8,128)(2,1)} %copy-done.8) | copy-start | bytes 3145732
  72.6 12.9 %collective-permute-start.17 = (f32[3,16,2304]{2,1,0:T(8,128)S(1)}, f32[3,16,2304]{2,1,0:T(8,128)S(1)}, u32[]{:S(2)}, u32[]{:S(2)}) collective-permute-start(f32[3,16,2304]{2,1,0:T(8,128)S(1)} %pass_on.5.refs_2_), channel_id=1, source_target_pairs={{0,1},{1,0},{2,3},{3,2},{4,5},{5,4},{6,7},{7,6},{8,9},{9,8},{10,11... | collective-permute-start | bytes 1327112 | tf_op jit(solution)/shard_map/ppermute | solution.py:589
  77.1 13.3 %collective-permute-start.12 = (f32[256,128]{1,0:T(8,128)S(1)}, f32[256,128]{1,0:T(8,128)S(1)}, u32[]{:S(2)}, u32[]{:S(2)}) collective-permute-start(f32[256,128]{1,0:T(8,128)S(1)} %get-tuple-element.39.refs_0_), channel_id=1, source_target_pairs={{0,8},{4,12},{8,0},{12,4},{1,9},{5,13},{9,1},{13,5},{2,10},{6,14},... | collective-permute-start | bytes 393224 | tf_op jit(solution)/shard_map/ppermute | solution.py:589
  80.4 10.0 %collective-permute-start.13 = (f32[256,128]{1,0:T(8,128)S(1)}, f32[256,128]{1,0:T(8,128)S(1)}, u32[]{:S(2)}, u32[]{:S(2)}) collective-permute-start(f32[256,128]{1,0:T(8,128)S(1)} %get-tuple-element.39.refs_0_), channel_id=1, source_target_pairs={{0,12},{4,8},{8,4},{12,0},{1,13},{5,9},{9,5},{13,1},{2,14},{6,10},... | collective-permute-start | bytes 393224 | tf_op jit(solution)/shard_map/ppermute | solution.py:589
  81.6 9.0 %collective-permute-start.14 = (f32[256,128]{1,0:T(8,128)S(1)}, f32[256,128]{1,0:T(8,128)S(1)}, u32[]{:S(2)}, u32[]{:S(2)}) collective-permute-start(f32[256,128]{1,0:T(8,128)S(1)} %get-tuple-element.39.refs_0_), channel_id=1, source_target_pairs={{0,4},{4,0},{8,12},{12,8},{1,5},{5,1},{9,13},{13,9},{2,6},{6,2},{1... | collective-permute-start | bytes 393224 | tf_op jit(solution)/shard_map/ppermute | solution.py:589
  81.6 9.0 %slice-start = ((s8[6291456]{0:T(1024)(128)(4,1)}), s8[4194304]{0:T(1024)(128)(4,1)S(1)}, s32[]{:S(2)}) async-start(s8[6291456]{0:T(1024)(128)(4,1)} %bitcast.7), calls=%async_computation.1 | async-start | bytes 8388608
  81.6 9.0 %slice-start.1 = ((s8[6291456]{0:T(1024)(128)(4,1)}), s8[2097152]{0:T(1024)(128)(4,1)S(1)}, s32[]{:S(2)}) async-start(s8[6291456]{0:T(1024)(128)(4,1)} %bitcast.7), calls=%async_computation.2 | async-start | bytes 4194304
  85.5 5.1 %copy-start.2 = (f32[256,128]{1,0:T(8,128)S(1)}, f32[256,128]{1,0:T(8,128)}, u32[]{:S(2)}) copy-start(f32[256,128]{1,0:T(8,128)} %copy-done.1) | copy-start | bytes 393220
  85.5 5.1 %copy-start.4 = (f32[256,128]{1,0:T(8,128)S(1)}, f32[256,128]{1,0:T(8,128)}, u32[]{:S(2)}) copy-start(f32[256,128]{1,0:T(8,128)} %copy-done.3) | copy-start | bytes 393220
